TPU v7x, 128 devices: a whole 4x4x4 slice. The times are simulated.
128 devices in a mesh: dp: 16 (over x_lo, z, core), tensor: 8 (over y, x_hi).
Axes of the slice: x: 4 (x_hi: 2, x_lo: 2; x = x_hi * 2 + x_lo), y: 4, z: 4, core: 2. Of those that a mesh axis runs over, the one named last changes fastest.
Arguments:
- tokens: bfloat16 [16384, 2048], P(('dp', 'tensor')), may hold values from -6 to 6
- cotangent: bfloat16 [16384, 2048], P(('dp', 'tensor')), may hold values from -6 to 6
- row_lengths: int32 [3], replicated, may hold values from 1 to 15872, as said below
- gains: float32 [2, 2048], P(None, 'dp'), may hold values from 0.5 to 1.5
- gain_first: float32 [2, 2048], P(None, 'dp'), may hold values from -768 to 768
- gain_second: float32 [2, 2048], P(None, 'dp'), may hold values from 8192 to 131072
- feature_weight: float32 [2048, 2, 256], P('dp', None, 'tensor'), may hold values from -0.125 to 0.125
- feature_first: float32 [2048, 2, 256], P('dp', None, 'tensor'), may hold values from -80 to 80
- feature_second: float32 [2048, 2, 256], P('dp', None, 'tensor'), may hold values from 81.92 to 1310.72
- value_weight: float32 [2048, 2048], P('dp', 'tensor'), may hold values from -0.125 to 0.125
- value_first: float32 [2048, 2048], P('dp', 'tensor'), may hold values from -80 to 80
- value_second: float32 [2048, 2048], P('dp', 'tensor'), may hold values from 81.92 to 1310.72
- output_weight: float32 [2048, 2048], P('tensor', 'dp'), may hold values from -1 to 1
- output_first: float32 [2048, 2048], P('tensor', 'dp'), may hold values from -24 to 24
- output_second: float32 [2048, 2048], P('tensor', 'dp'), may hold values from 8.192 to 131.072
- gateup_weight: float32 [2048, 2, 5504], P('dp', None, 'tensor'), may hold values from -0.125 to 0.125
- gateup_first: float32 [2048, 2, 5504], P('dp', None, 'tensor'), may hold values from -384 to 384
- gateup_second: float32 [2048, 2, 5504], P('dp', None, 'tensor'), may hold values from 2048 to 32768
- down_weight: float32 [5504, 2048], P('tensor', 'dp'), may hold values from -0.078125 to 0.078125
- down_first: float32 [5504, 2048], P('tensor', 'dp'), may hold values from -384 to 384
- down_second: float32 [5504, 2048], P('tensor', 'dp'), may hold values from 2048 to 32768
Outputs:
- mixed: bfloat16 [16384, 2048], P(('dp', 'tensor'))
- grad_tokens: float32 [16384, 2048], P(('dp', 'tensor'))
- den_mean: float32 [], replicated
- gain_moment: float32 [2, 2048], P(None, 'dp')
- gain_square: float32 [2, 2048], P(None, 'dp')
- gain_master: float32 [2, 2048], P(None, 'dp')
- feature_moment: float32 [2048, 2, 256], P('dp', None, 'tensor')
- feature_square: float32 [2048, 2, 256], P('dp', None, 'tensor')
- feature_master: float32 [2048, 2, 256], P('dp', None, 'tensor')
- value_moment: float32 [2048, 2048], P('dp', 'tensor')
- value_square: float32 [2048, 2048], P('dp', 'tensor')
- value_master: float32 [2048, 2048], P('dp', 'tensor')
- output_moment: float32 [2048, 2048], P('tensor', 'dp')
- output_square: float32 [2048, 2048], P('tensor', 'dp')
- output_master: float32 [2048, 2048], P('tensor', 'dp')
- gateup_moment: float32 [2048, 2, 5504], P('dp', None, 'tensor')
- gateup_square: float32 [2048, 2, 5504], P('dp', None, 'tensor')
- gateup_master: float32 [2048, 2, 5504], P('dp', None, 'tensor')
- down_moment: float32 [5504, 2048], P('tensor', 'dp')
- down_square: float32 [5504, 2048], P('tensor', 'dp')
- down_master: float32 [5504, 2048], P('tensor', 'dp')
Inputs may be any that keep to these rules, and one draw needn't show every extreme that they name: `row_lengths`: three rows are packed in order: a short row, a row of 15872 tokens, and a short row; the two short rows hold 512 tokens together.
All inputs are finite; a program needn't handle non-finite values.
Results may differ from a plain program's by a relative error of at most 0.035.
Values may be sent and summed in bfloat16 or wider, within the bound.
No kernel may reach another device: no remote copies, remote signals or barrier semaphores. Data moves between devices by JAX's collectives and lax.ppermute only.
A program may use at most 192 MiB of HBM per device.

v0:
```python
import jax
import jax.numpy as jnp
from jax import lax
from jax.sharding import PartitionSpec as P

D = 2048
HEADS = 16
FEAT = 16
DV = 128
FF = 5504
BLOCK = 512
STEP = 10


norm_eps = 1e-05
beta_one = 0.5
beta_two = 0.5
adam_eps = 1e-08
weight_decay = 0.01
gain_rate = 0.5
highest = lax.Precision.HIGHEST


def carried_in(part, axis, combine, identity):
    place = lax.axis_index(axis)
    gathered = jax.tree.map(lambda a: lax.all_gather(a, axis), part)
    state = jax.tree.map(lambda a, e: jnp.zeros_like(a) + jnp.asarray(e, a.dtype), part, identity)

    def one(hop, state):
        return combine(
            state, jax.tree.map(lambda a: lax.dynamic_index_in_dim(a, hop, 0, False), gathered)
        )

    return lax.fori_loop(0, place, one, state)


def carried_in_2(shard, axis, join, neutral):
    count = lax.axis_size(axis)
    place = lax.axis_index(axis)
    ahead = count - 1 - place
    gathered = jax.tree.map(
        lambda a, kind: lax.all_gather(a.astype(kind), axis),
        shard,
        jax.tree.map(lambda a: jnp.bfloat16 if a.dtype == jnp.float32 else a.dtype, shard),
    )
    state = jax.tree.map(lambda a, e: jnp.zeros_like(a) + jnp.asarray(e, a.dtype), shard, neutral)

    def one(hop, state):
        source = count - 1 - hop
        return join(
            state,
            jax.tree.map(
                lambda a, own: lax.dynamic_index_in_dim(a, source, 0, False).astype(own.dtype),
                gathered,
                shard,
            ),
        )

    return lax.fori_loop(0, ahead, one, state)


def doc_index(positions, row_lengths):
    ends = jnp.cumsum(row_lengths)
    return jnp.sum((positions[:, None] >= ends[None, :]).astype(jnp.int32), axis=1)


def features(values, feat_dim):
    leading = values.shape[:-1]
    outer_pairs = (values[..., :, None] * values[..., None, :]).reshape(
        leading + (feat_dim * feat_dim,)
    )
    constant = jnp.ones(leading + (1,), jnp.float32)
    return jnp.concatenate(
        [constant, values * feat_dim ** (-0.25), outer_pairs * (2.0 * feat_dim) ** (-0.5)], axis=-1
    )


def features_back(values, grad_feats, feat_dim):
    linear_grad = grad_feats[..., 1 : 1 + feat_dim] * feat_dim ** (-0.25)
    second = grad_feats[..., 1 + feat_dim :].reshape(values.shape + (feat_dim,))
    symmetric = second + jnp.swapaxes(second, -1, -2)
    return linear_grad + jnp.einsum("...ab,...b->...a", symmetric, values, precision=highest) * (
        2.0 * feat_dim
    ) ** (-0.5)


def rms_norm(inputs, gain_row):
    inv_rms = lax.rsqrt(jnp.mean(inputs * inputs, axis=-1, keepdims=True) + norm_eps)
    unit_rows = inputs * inv_rms
    return (unit_rows * gain_row, unit_rows, inv_rms)


def norm_backward(upstream, unit_rows, inv_rms, gain_row):
    shaped = upstream * gain_row
    grad_in = inv_rms * (shaped - unit_rows * jnp.mean(shaped * unit_rows, axis=-1, keepdims=True))
    return (grad_in, jnp.sum(upstream * unit_rows, axis=0))


def chain(earlier, later):
    passes = 1.0 - later[2]
    return (
        later[0] + passes * earlier[0],
        later[1] + passes * earlier[1],
        jnp.maximum(earlier[2], later[2]),
    )


def block_masks(doc_blk, previous):
    block_len = doc_blk.shape[0]
    row_pos = lax.broadcasted_iota(jnp.int32, (block_len, block_len), 0)
    col_pos = lax.broadcasted_iota(jnp.int32, (block_len, block_len), 1)
    allowed = (col_pos <= row_pos) & (doc_blk[None, :] == doc_blk[:, None])
    continues = (doc_blk == previous).astype(jnp.float32)[:, None]
    last_doc = doc_blk[block_len - 1]
    carry_on = (last_doc == previous).astype(jnp.float32)
    in_last = (doc_blk == last_doc).astype(jnp.float32)[:, None, None]
    return (allowed, continues, carry_on, in_last)


def block_forward(query_blk, key_blk, value_blk, doc_blk, previous, kv_state, norm_state):
    allowed, continues, carry_on, in_last = block_masks(doc_blk, previous)
    scores = jnp.einsum(
        "thf,jhf->htj", query_blk, key_blk, preferred_element_type=jnp.float32
    ) * FEAT ** (-0.5)
    kernel = jnp.where(allowed[None], 1.0 + scores + 0.5 * scores * scores, 0.0)
    inner_sum = jnp.einsum(
        "htj,jhv->thv", kernel.astype(jnp.bfloat16), value_blk, preferred_element_type=jnp.float32
    )
    query_feats = features(query_blk.astype(jnp.float32), FEAT)
    carried = jnp.einsum("thp,hpv->thv", query_feats, kv_state, precision=highest)
    numerator = inner_sum + continues[:, :, None] * carried
    denominator = jnp.sum(kernel, axis=-1).T + continues * jnp.einsum(
        "thp,hp->th", query_feats, norm_state, precision=highest
    )
    result = numerator / denominator[:, :, None]
    key_feats = features(key_blk.astype(jnp.float32), FEAT) * in_last
    new_state = carry_on * kv_state + jnp.einsum(
        "thp,thv->hpv", key_feats, value_blk.astype(jnp.float32), precision=highest
    )
    new_norm = carry_on * norm_state + jnp.sum(key_feats, axis=0)
    return (result, denominator, new_state, new_norm)


def block_backward(
    query_blk,
    key_blk,
    value_blk,
    doc_blk,
    previous,
    kv_state,
    norm_state,
    result,
    denominator,
    grad_result,
    grad_state,
    grad_norm,
):
    allowed, continues, carry_on, in_last = block_masks(doc_blk, previous)
    factor = FEAT ** (-0.5)
    scores = (
        jnp.einsum("thf,jhf->htj", query_blk, key_blk, preferred_element_type=jnp.float32) * factor
    )
    kernel = jnp.where(allowed[None], 1.0 + scores + 0.5 * scores * scores, 0.0)
    low_kernel = kernel.astype(jnp.bfloat16)
    grad_numer = grad_result / denominator[:, :, None]
    grad_denom = -jnp.sum(grad_result * result, axis=-1) / denominator
    low_numer = grad_numer.astype(jnp.bfloat16)
    grad_kernel = (
        jnp.einsum("thv,jhv->htj", low_numer, value_blk, preferred_element_type=jnp.float32)
        + grad_denom.T[:, :, None]
    )
    grad_scores = jnp.where(allowed[None], grad_kernel * (1.0 + scores), 0.0).astype(jnp.bfloat16)
    grad_query = (
        jnp.einsum("htj,jhf->thf", grad_scores, key_blk, preferred_element_type=jnp.float32)
        * factor
    )
    grad_key = (
        jnp.einsum("htj,thf->jhf", grad_scores, query_blk, preferred_element_type=jnp.float32)
        * factor
    )
    grad_value = jnp.einsum(
        "htj,thv->jhv", low_kernel, low_numer, preferred_element_type=jnp.float32
    )
    query_real = query_blk.astype(jnp.float32)
    key_real = key_blk.astype(jnp.float32)
    query_feats = features(query_real, FEAT)
    weighted = query_feats * continues[:, :, None]
    grad_qfeat = continues[:, :, None] * (
        jnp.einsum("thv,hpv->thp", grad_numer, kv_state, precision=highest)
        + grad_denom[:, :, None] * norm_state[None]
    )
    state_back = carry_on * grad_state + jnp.einsum(
        "thp,thv->hpv", weighted, grad_numer, precision=highest
    )
    norm_back = carry_on * grad_norm + jnp.sum(weighted * grad_denom[:, :, None], axis=0)
    key_feats = features(key_real, FEAT) * in_last
    grad_kfeat = in_last * (
        jnp.einsum("thv,hpv->thp", value_blk.astype(jnp.float32), grad_state, precision=highest)
        + grad_norm[None]
    )
    grad_value = grad_value + jnp.einsum("thp,hpv->thv", key_feats, grad_state, precision=highest)
    grad_query = grad_query + features_back(query_real, grad_qfeat, FEAT)
    grad_key = grad_key + features_back(key_real, grad_kfeat, FEAT)
    return (grad_query, grad_key, grad_value, state_back, norm_back)


def adam_step(weight, moment_one, moment_two, reduced, step_rate):
    new_one = beta_one * moment_one + (1.0 - beta_one) * reduced
    new_two = beta_two * moment_two + (1.0 - beta_two) * reduced * reduced
    corrected_one = new_one / (1.0 - beta_one**STEP)
    corrected_two = new_two / (1.0 - beta_two**STEP)
    master = weight - step_rate * (
        corrected_one / (jnp.sqrt(corrected_two) + adam_eps) + weight_decay * weight
    )
    return (new_one, new_two, master)


def shards(
    tokens,
    cotangent,
    row_lengths,
    gains,
    gain_first,
    gain_second,
    feature_weight,
    feature_first,
    feature_second,
    value_weight,
    value_first,
    value_second,
    output_weight,
    output_first,
    output_second,
    gateup_weight,
    gateup_first,
    gateup_second,
    down_weight,
    down_first,
    down_second,
):
    tensor_count = lax.axis_size("tensor")
    data_count = lax.axis_size("dp")
    local_rows = tokens.shape[0]
    group_rows = local_rows * tensor_count
    blocks = group_rows // BLOCK
    low_params = (
        gains.astype(jnp.bfloat16),
        feature_weight.astype(jnp.bfloat16),
        value_weight.astype(jnp.bfloat16),
        output_weight.astype(jnp.bfloat16),
        gateup_weight.astype(jnp.bfloat16),
        down_weight.astype(jnp.bfloat16),
    )
    gain_full, feature_full, value_full, output_full, gateup_full, down_full = (
        lax.all_gather(low_params[0], "dp", axis=1, tiled=True),
        lax.all_gather(low_params[1], "dp", axis=0, tiled=True),
        lax.all_gather(low_params[2], "dp", axis=0, tiled=True),
        lax.all_gather(low_params[3], "dp", axis=1, tiled=True),
        lax.all_gather(low_params[4], "dp", axis=0, tiled=True),
        lax.all_gather(low_params[5], "dp", axis=1, tiled=True),
    )
    gain_rows = gain_full.astype(jnp.float32)
    local_heads = value_full.shape[1] // DV

    def gather_normed(normed_rows):
        return lax.all_gather(normed_rows, "tensor", axis=0, tiled=True)

    def gather_grad(grad_rows):
        return lax.all_gather(grad_rows, "tensor", axis=0, tiled=True)

    def branch_sum(operand, weight_mat):
        return lax.psum_scatter(
            jnp.dot(operand, weight_mat, preferred_element_type=jnp.float32),
            "tensor",
            scatter_dimension=0,
            tiled=True,
        )

    def input_sum(pieces):
        summed = jnp.zeros((lax.axis_size("tensor") * local_rows, D), jnp.float32)
        for operand, weight_mat, pattern in pieces:
            summed = summed + jnp.einsum(
                pattern, operand, weight_mat, preferred_element_type=jnp.float32
            )
        return lax.psum_scatter(summed, "tensor", scatter_dimension=0, tiled=True)

    inputs = tokens.astype(jnp.float32)
    normed_one, unit_one, inv_one = rms_norm(inputs, gain_rows[0])
    acts_one = gather_normed(normed_one.astype(jnp.bfloat16))
    projected = jnp.einsum(
        "td,dcf->tcf", acts_one, feature_full, preferred_element_type=jnp.float32
    ).astype(jnp.bfloat16)
    queries = projected[:, 0].reshape(group_rows, local_heads, FEAT)
    keys_all = projected[:, 1].reshape(group_rows, local_heads, FEAT)
    values_all = (
        jnp.dot(acts_one, value_full, preferred_element_type=jnp.float32)
        .astype(jnp.bfloat16)
        .reshape(group_rows, local_heads, DV)
    )
    my_index = lax.axis_index("dp")
    first_pos = my_index * group_rows
    positions = first_pos + jnp.arange(group_rows, dtype=jnp.int32)
    doc_ids = doc_index(positions, row_lengths)
    before = jnp.where(
        first_pos > 0, doc_index(jnp.reshape(first_pos - 1, (1,)), row_lengths)[0], -1
    )
    last_doc = doc_ids[group_rows - 1]
    boundary = jnp.reshape((last_doc != before).astype(jnp.float32), (1,))
    in_last = (doc_ids == last_doc).astype(jnp.float32)[:, None, None]
    key_feats = features(keys_all.astype(jnp.float32), FEAT) * in_last
    own_state = jnp.einsum(
        "thp,thv->hpv", key_feats, values_all.astype(jnp.float32), precision=highest
    )
    own_norm = jnp.sum(key_feats, axis=0)
    identity = (jnp.zeros_like(own_state), jnp.zeros_like(own_norm), jnp.zeros((1,), jnp.float32))
    carry_all = carried_in((own_state, own_norm, boundary), "dp", chain, identity)
    carry_state = carry_all[0]
    carry_norm = carry_all[1]
    previous = jnp.concatenate(
        [jnp.reshape(before, (1,)), doc_ids[BLOCK - 1 :: BLOCK][: blocks - 1]]
    )
    query_blocks = queries.reshape(blocks, BLOCK, local_heads, FEAT)
    key_blocks = keys_all.reshape(blocks, BLOCK, local_heads, FEAT)
    value_blocks = values_all.reshape(blocks, BLOCK, local_heads, DV)
    doc_blocks = doc_ids.reshape(blocks, BLOCK)

    def forward_step(carried, block_item):
        query_blk, key_blk, value_blk, doc_blk, prev_doc = block_item
        result, denominator, new_state, new_norm = block_forward(
            query_blk, key_blk, value_blk, doc_blk, prev_doc, carried[0], carried[1]
        )
        return ((new_state, new_norm), (result, denominator, carried[0], carried[1]))

    unused_end, (results, denoms, state_ins, norm_ins) = lax.scan(
        forward_step,
        (carry_state, carry_norm),
        (query_blocks, key_blocks, value_blocks, doc_blocks, previous),
    )
    den_total = lax.psum(jnp.sum(denoms), ("dp", "tensor"))
    den_mean = den_total / (group_rows * data_count * local_heads * tensor_count)
    attn_rows = results.reshape(group_rows, local_heads * DV).astype(jnp.bfloat16)
    middle = inputs + branch_sum(attn_rows, output_full)
    normed_two, unit_two, inv_two = rms_norm(middle, gain_rows[1])
    acts_two = gather_normed(normed_two.astype(jnp.bfloat16))
    gate_up = jnp.einsum("td,dcf->tcf", acts_two, gateup_full, preferred_element_type=jnp.float32)
    gate_vals = gate_up[:, 0]
    up_vals = gate_up[:, 1]
    sigmoid = jax.nn.sigmoid(gate_vals)
    silu_vals = gate_vals * sigmoid
    hidden = (silu_vals * up_vals).astype(jnp.bfloat16)
    mixed = middle + branch_sum(hidden, down_full)
    grad_out = cotangent.astype(jnp.float32)
    grad_mlp = gather_grad(grad_out.astype(jnp.bfloat16))
    grad_hidden = jnp.einsum("td,fd->tf", grad_mlp, down_full, preferred_element_type=jnp.float32)
    down_grad = jnp.einsum("tf,td->fd", hidden, grad_mlp, preferred_element_type=jnp.float32)
    dsilu = sigmoid * (1.0 + gate_vals * (1.0 - sigmoid))
    grad_gate_up = jnp.stack(
        [grad_hidden * up_vals * dsilu, grad_hidden * silu_vals], axis=1
    ).astype(jnp.bfloat16)
    gateup_grad = jnp.einsum(
        "td,tcf->dcf", acts_two, grad_gate_up, preferred_element_type=jnp.float32
    )
    grad_norm_two = input_sum([(grad_gate_up, gateup_full, "tcf,dcf->td")])
    grad_mid_norm, gain_grad_two = norm_backward(grad_norm_two, unit_two, inv_two, gain_rows[1])
    grad_mid = grad_out + grad_mid_norm
    grad_attn = gather_grad(grad_mid.astype(jnp.bfloat16))
    output_grad = jnp.einsum("tf,td->fd", attn_rows, grad_attn, preferred_element_type=jnp.float32)
    grad_low = jnp.einsum(
        "td,fd->tf", grad_attn, output_full, preferred_element_type=jnp.float32
    ).astype(jnp.bfloat16)
    grad_result = (
        lax.optimization_barrier(grad_low)
        .astype(jnp.float32)
        .reshape(blocks, BLOCK, local_heads, DV)
    )
    grad_numer_all = grad_result / denoms[..., None]
    grad_denom_all = -jnp.sum(grad_result * results, axis=-1) / denoms
    starts_in = (doc_ids == before).astype(jnp.float32).reshape(blocks, BLOCK, 1, 1)
    query_feats = features(query_blocks.astype(jnp.float32), FEAT) * starts_in
    own_grad_state = jnp.einsum("bthp,bthv->hpv", query_feats, grad_numer_all, precision=highest)
    own_grad_norm = jnp.einsum("bthp,bth->hp", query_feats, grad_denom_all, precision=highest)
    end_all = carried_in_2((own_grad_state, own_grad_norm, boundary), "dp", chain, identity)

    def backward_step(carried, block_item):
        (
            query_blk,
            key_blk,
            value_blk,
            doc_blk,
            prev_doc,
            state_in,
            norm_in,
            result,
            denominator,
            grad_blk,
        ) = block_item
        grad_query, grad_key, grad_value, state_back, norm_back = block_backward(
            query_blk,
            key_blk,
            value_blk,
            doc_blk,
            prev_doc,
            state_in,
            norm_in,
            result,
            denominator,
            grad_blk,
            carried[0],
            carried[1],
        )
        return ((state_back, norm_back), (grad_query, grad_key, grad_value))

    unused_start, (grad_q_blocks, grad_k_blocks, grad_v_blocks) = lax.scan(
        backward_step,
        (end_all[0], end_all[1]),
        (
            query_blocks,
            key_blocks,
            value_blocks,
            doc_blocks,
            previous,
            state_ins,
            norm_ins,
            results,
            denoms,
            grad_result,
        ),
        reverse=True,
    )
    grad_proj = jnp.stack(
        [
            grad_q_blocks.reshape(group_rows, local_heads * FEAT),
            grad_k_blocks.reshape(group_rows, local_heads * FEAT),
        ],
        axis=1,
    ).astype(jnp.bfloat16)
    grad_values = grad_v_blocks.reshape(group_rows, local_heads * DV).astype(jnp.bfloat16)
    feature_grad = jnp.einsum(
        "td,tcf->dcf", acts_one, grad_proj, preferred_element_type=jnp.float32
    )
    value_grad = jnp.einsum("td,tf->df", acts_one, grad_values, preferred_element_type=jnp.float32)
    grad_norm_one = input_sum(
        [(grad_proj, feature_full, "tcf,dcf->td"), (grad_values, value_full, "tf,df->td")]
    )
    grad_in_norm, gain_grad_one = norm_backward(grad_norm_one, unit_one, inv_one, gain_rows[0])
    grad_tokens = grad_mid + grad_in_norm
    gain_grads = jnp.stack([gain_grad_one, gain_grad_two])
    gain_sum, feature_sum, value_sum, output_sum, gateup_sum, down_sum = (
        lax.psum_scatter(
            gain_grads.astype(jnp.bfloat16), "dp", scatter_dimension=1, tiled=True
        ).astype(jnp.float32),
        lax.psum_scatter(
            feature_grad.astype(jnp.bfloat16), "dp", scatter_dimension=0, tiled=True
        ).astype(jnp.float32),
        lax.psum_scatter(
            value_grad.astype(jnp.bfloat16), "dp", scatter_dimension=0, tiled=True
        ).astype(jnp.float32),
        lax.psum_scatter(
            output_grad.astype(jnp.bfloat16), "dp", scatter_dimension=1, tiled=True
        ).astype(jnp.float32),
        lax.psum_scatter(
            gateup_grad.astype(jnp.bfloat16), "dp", scatter_dimension=0, tiled=True
        ).astype(jnp.float32),
        lax.psum_scatter(
            down_grad.astype(jnp.bfloat16), "dp", scatter_dimension=1, tiled=True
        ).astype(jnp.float32),
    )
    gain_total = lax.psum(gain_sum, "tensor")
    gain_new = adam_step(gains, gain_first, gain_second, gain_total, gain_rate)
    feature_new = adam_step(feature_weight, feature_first, feature_second, feature_sum, D ** (-0.5))
    value_new = adam_step(value_weight, value_first, value_second, value_sum, D ** (-0.5))
    output_new = adam_step(
        output_weight, output_first, output_second, output_sum, (HEADS * DV // 64) ** (-0.5)
    )
    gateup_new = adam_step(gateup_weight, gateup_first, gateup_second, gateup_sum, D ** (-0.5))
    down_new = adam_step(down_weight, down_first, down_second, down_sum, FF ** (-0.5))
    return (
        mixed.astype(jnp.bfloat16),
        grad_tokens,
        den_mean,
        gain_new[0],
        gain_new[1],
        gain_new[2],
        feature_new[0],
        feature_new[1],
        feature_new[2],
        value_new[0],
        value_new[1],
        value_new[2],
        output_new[0],
        output_new[1],
        output_new[2],
        gateup_new[0],
        gateup_new[1],
        gateup_new[2],
        down_new[0],
        down_new[1],
        down_new[2],
    )


def solution(mesh):
    placed = (
        P(("dp", "tensor"), None),
        P(("dp", "tensor"), None),
        P(),
        P(None, "dp"),
        P(None, "dp"),
        P(None, "dp"),
        P("dp", None, "tensor"),
        P("dp", None, "tensor"),
        P("dp", None, "tensor"),
        P("dp", "tensor"),
        P("dp", "tensor"),
        P("dp", "tensor"),
        P("tensor", "dp"),
        P("tensor", "dp"),
        P("tensor", "dp"),
        P("dp", None, "tensor"),
        P("dp", None, "tensor"),
        P("dp", None, "tensor"),
        P("tensor", "dp"),
        P("tensor", "dp"),
        P("tensor", "dp"),
    )
    return jax.shard_map(
        shards,
        mesh=mesh,
        in_specs=placed,
        out_specs=(
            P(("dp", "tensor"), None),
            P(("dp", "tensor"), None),
            P(),
            P(None, "dp"),
            P(None, "dp"),
            P(None, "dp"),
            P("dp", None, "tensor"),
            P("dp", None, "tensor"),
            P("dp", None, "tensor"),
            P("dp", "tensor"),
            P("dp", "tensor"),
            P("dp", "tensor"),
            P("tensor", "dp"),
            P("tensor", "dp"),
            P("tensor", "dp"),
            P("dp", None, "tensor"),
            P("dp", None, "tensor"),
            P("dp", None, "tensor"),
            P("tensor", "dp"),
            P("tensor", "dp"),
            P("tensor", "dp"),
        ),
        check_vma=False,
    )
```

profile of v0, /device:TPU:1, one launch (start us, length us, event | category | flops | bytes accessed | tf_op | source)
XLA Modules:
  0.0 1513.5 jit_solution(15589791032479778216)
XLA Ops:
  8.0 22.1 %all_gather.63 = bf16[2,2048]{1,0:T(2,128)(2,1)S(1)} all-gather(bf16[2,128]{1,0:T(2,128)(2,1)S(1)} %convert_element_type.387), channel_id=1, replica_groups=mesh['dp'=16,'tensor'=8] {'dp'}, dimensions={1}, use_global_device_ids=true | all-gather | bytes 8704 | tf_op jit(solution)/shard_map/all_gather | solution.py:255
  35.0 17.6 %all_gather.65 = bf16[2048,2,32]{0,2,1:T(8,128)(2,1)S(1)} all-gather(bf16[128,2,32]{0,2,1:T(8,128)(2,1)S(1)} %convert_element_type.390), channel_id=1, replica_groups=mesh['dp'=16,'tensor'=8] {'dp'}, dimensions={0}, use_global_device_ids=true | all-gather | bytes 278528 | tf_op jit(solution)/shard_map/all_gather | solution.py:256
  53.3 49.6 %all-gather.17.cloned.1.call-done = bf16[1024,2048]{1,0:T(8,128)(2,1)} async-done(((bf16[128,2048]{1,0:T(8,128)(2,1)}), bf16[1024,2048]{1,0:T(8,128)(2,1)}) %all-gather.17.cloned.1.call-update) | async-done | bytes 4194320 | tf_op jit(solution)/shard_map/all_gather | solution.py:266
  106.8 29.6 %all-gather.19.cloned.1.call-done = bf16[2048,256]{1,0:T(8,128)(2,1)} async-done(((bf16[128,256]{1,0:T(8,128)(2,1)}), bf16[2048,256]{1,0:T(8,128)(2,1)}) %all-gather.19.cloned.1.call-update) | async-done | bytes 1048592 | tf_op jit(solution)/shard_map/all_gather | solution.py:257
  146.7 26.8 %all-reduce = f32[16]{0:T(128)S(1)} all-reduce(f32[16]{0:T(128)S(1)} %dynamic-update-slice), channel_id=1, replica_groups=mesh['dp'=16,'tensor'=8] {'dp'}, use_global_device_ids=true, to_apply=%add | all-reduce | flops 16 | bytes 128
  174.6 18.4 %all-gather.4 = f32[16,2,273]{2,1,0:T(2,128)S(1)} all-gather(f32[1,2,273]{2,1,0:T(2,128)S(1)} %bitcast.604), channel_id=3, replica_groups=mesh['dp'=16,'tensor'=8] {'dp'}, dimensions={0}, use_global_device_ids=true | all-gather | bytes 37128 | tf_op jit(solution)/shard_map/all_gather | solution.py:26
  196.7 21.4 %while.79 = (s32[]{:T(128)}, f32[2,273,128]{2,1,0:T(8,128)S(1)}, f32[2,273]{1,0:T(2,128)S(1)}, f32[2,512,2,128]{1,3,2,0:T(8,128)}, f32[2,512,2]{1,2,0:T(2,128)S(...) while((s32[]{:T(128)}, f32[2,273,128]{2,1,0:T(8,128)S(1)}, ...), condition=%wide.region_10.11_spmd.clone, body=%wide.region_7.10_spmd.sunk.clone | while | flops 1022874624 | bytes 13359251 | solution.py:334
  228.0 152.4 %reduce-scatter.21.cloned.1.call-done = f32[128,2048]{1,0:T(8,128)} async-done(((f32[1024,2048]{1,0:T(8,128)}), f32[128,2048]{1,0:T(8,128)}) %reduce-scatter.21.cloned.1.call-update) | async-done | bytes 1048592 | tf_op jit(solution)/shard_map/reduce_scatter | solution.py:272
  384.9 47.4 %all-gather.25.cloned.1.call-done = bf16[2048,2,688]{0,2,1:T(8,128)(2,1)} async-done(((bf16[128,2,688]{0,2,1:T(8,128)(2,1)}), bf16[2048,2,688]{0,2,1:T(8,128)(2,1)}) %all-gather.25.cloned.1.call-update) | async-done | bytes 5636112 | tf_op jit(solution)/shard_map/all_gather | solution.py:259
  432.3 73.3 %all-gather.23.cloned.1.call-done = bf16[1024,2048]{1,0:T(8,128)(2,1)} async-done(((bf16[128,2048]{1,0:T(8,128)(2,1)}), bf16[1024,2048]{1,0:T(8,128)(2,1)}) %all-gather.23.cloned.1.call-update) | async-done | bytes 4194320 | tf_op jit(solution)/shard_map/all_gather | solution.py:266
  516.4 30.1 %all-gather.27.cloned.1.call-done = bf16[688,2048]{1,0:T(8,128)(2,1)} async-done(((bf16[688,128]{1,0:T(8,128)(2,1)}), bf16[688,2048]{1,0:T(8,128)(2,1)}) %all-gather.27.cloned.1.call-update) | async-done | bytes 2818064 | tf_op jit(solution)/shard_map/all_gather | solution.py:260
  546.6 73.4 %all-gather.29.cloned.1.call-done = bf16[1024,2048]{1,0:T(8,128)(2,1)} async-done(((bf16[128,2048]{1,0:T(8,128)(2,1)}), bf16[1024,2048]{1,0:T(8,128)(2,1)}) %all-gather.29.cloned.1.call-update) | async-done | bytes 4194320 | tf_op jit(solution)/shard_map/all_gather | solution.py:269
  640.7 112.8 %reduce-scatter.25.cloned.1.call-done = f32[128,2048]{1,0:T(8,128)} async-done(((f32[1024,2048]{1,0:T(8,128)}), f32[128,2048]{1,0:T(8,128)}) %reduce-scatter.25.cloned.1.call-update) | async-done | bytes 1048592 | tf_op jit(solution)/shard_map/reduce_scatter | solution.py:285
  768.7 57.3 %all-gather.31.cloned.1.call-done = bf16[1024,2048]{1,0:T(8,128)(2,1)} async-done(((bf16[128,2048]{1,0:T(8,128)(2,1)}), bf16[1024,2048]{1,0:T(8,128)(2,1)}) %all-gather.31.cloned.1.call-update) | async-done | bytes 4194320 | tf_op jit(solution)/shard_map/all_gather | solution.py:269
  866.5 27.6 %all-reduce.1 = bf16[16]{0:T(256)(128)(2,1)S(1)} all-reduce(bf16[16]{0:T(256)(128)(2,1)S(1)} %dynamic-update-slice.1), channel_id=1, replica_groups=mesh['dp'=16,'tensor'=8] {'dp'}, use_global_device_ids=true, to_apply=%add.1 | all-reduce | flops 16 | bytes 64
  905.3 18.5 %all-gather.5 = bf16[16,2,273]{2,1,0:T(2,128)(2,1)S(1)} all-gather(bf16[1,2,273]{2,1,0:T(2,128)(2,1)S(1)} %bitcast.605), channel_id=5, replica_groups=mesh['dp'=16,'tensor'=8] {'dp'}, dimensions={0}, use_global_device_ids=true | all-gather | bytes 18564 | tf_op jit(solution)/shard_map/all_gather | solution.py:42
  923.9 41.3 %while.80 = (s32[]{:T(128)}, f32[2,273,128]{2,1,0:T(8,128)S(1)}, f32[2,273]{1,0:T(2,128)S(1)}, s32[]{:T(128)}, bf16[16,2,273,128]{3,2,1,0:T(8,128)(2,1)}, /*inde...) while((s32[]{:T(128)}, f32[2,273,128]{2,1,0:T(8,128)S(1)}, f32[2,273]{1,0:T(2,128)S(1)}, ...), condition=%wide.region_18.19_spmd.clone, body=%wide.region_17.18_spmd.sunk.clone | while | flops 211309 | bytes 704489 | solution.py:59
  966.5 47.1 %while.81 = (s32[]{:T(128)}, f32[2,273,128]{2,1,0:T(8,128)S(1)}, f32[2,273]{1,0:T(2,128)S(1)}, bf16[2,512,2,16]{1,3,2,0:T(8,128)(2,1)}, bf16[2,512,2,16]{1,3,2,0...) while((s32[]{:T(128)}, f32[2,273,128]{2,1,0:T(8,128)S(1)}, ...), condition=%wide.region_22.23_spmd.clone, body=%wide.region_19.22_spmd.sunk.clone | while | flops 2052583424 | bytes 40645540 | solution.py:413
  1046.3 65.1 %psum.14 = f32[]{:T(128)} all-reduce(f32[]{:T(128)} %get-tuple-element.914), channel_id=1, replica_groups=mesh['dp'=16,'tensor'=8] {'dp','tensor'}, use_global_device_ids=true, to_apply=%region_26.27 | all-reduce | flops 1 | bytes 8 | tf_op jit(solution)/shard_map/psum | solution.py:339
  1127.6 61.2 %reduce-scatter.29.cloned.1.call-done = bf16[128,256]{1,0:T(8,128)(2,1)} async-done(((bf16[2048,256]{1,0:T(8,128)(2,1)}), bf16[128,256]{1,0:T(8,128)(2,1)}) %reduce-scatter.29.cloned.1.call-update) | async-done | bytes 65552 | tf_op jit(solution)/shard_map/reduce_scatter | solution.py:455
  1190.7 118.1 %reduce-scatter.27.cloned.1.call-done = f32[128,2048]{1,0:T(8,128)} async-done(((f32[1024,2048]{1,0:T(8,128)}), f32[128,2048]{1,0:T(8,128)}) %reduce-scatter.27.cloned.1.call-update) | async-done | bytes 1048592 | tf_op jit(solution)/shard_map/reduce_scatter | solution.py:285
  1311.6 113.5 %reduce-scatter.23.cloned.1.call-done = f32[128,2048]{1,0:T(8,128)} async-done(((f32[1024,2048]{1,0:T(8,128)}), f32[128,2048]{1,0:T(8,128)}) %reduce-scatter.23.cloned.1.call-update) | async-done | bytes 1048592 | tf_op jit(solution)/shard_map/reduce_scatter | solution.py:272
  1428.3 54.7 %reduce-scatter.31.cloned.1.call-done = bf16[128,2]{1,0:T(8,128)(2,1)} async-done(((bf16[2048,2]{1,0:T(8,128)(2,1)}), bf16[128,2]{1,0:T(8,128)(2,1)}) %reduce-scatter.31.cloned.1.call-update) | async-done | bytes 528
  1483.8 20.7 %psum.15 = f32[2,128]{1,0:T(2,128)S(1)} all-reduce(bf16[2,128]{1,0:T(2,128)(2,1)S(1)} %copy.166), channel_id=1, replica_groups=mesh['dp'=16,'tensor'=8] {'tensor'}, use_global_device_ids=true, to_apply=%region_30.31 | all-reduce | flops 256 | bytes 1536 | tf_op jit(solution)/shard_map/psum | solution.py:468
  (463 shorter events, 300.8 us)
Async XLA Ops:
  7.2 95.6 %all-gather.17.cloned.1.call-start = ((), (), s32[]{:S(2)}) async-start(), calls=%async_computation.10 | async-start | bytes 4718592 | tf_op jit(solution)/shard_map/all_gather | solution.py:266
  33.3 103.1 %all-gather.19.cloned.1.call-start = ((), (), s32[]{:S(2)}) async-start(), calls=%async_computation.11 | async-start | bytes 1114112 | tf_op jit(solution)/shard_map/all_gather | solution.py:257
  34.1 159.4 %all-gather.33.cloned.1.call-start = ((), (), s32[]{:S(2)}) async-start(), calls=%async_computation.23 | async-start | bytes 4874240 | tf_op jit(solution)/shard_map/all_gather | solution.py:26
  142.5 77.7 %all-gather.21.cloned.1.call-start = ((), (), s32[]{:S(2)}) async-start(), calls=%async_computation.12 | async-start | bytes 1114112 | tf_op jit(solution)/shard_map/all_gather | solution.py:258
  143.2 237.2 %reduce-scatter.21.cloned.1.call-start = ((), (), s32[]{:S(2)}) async-start(), calls=%async_computation.13 | async-start | bytes 9437184 | tf_op jit(solution)/shard_map/reduce_scatter | solution.py:272
  226.1 206.2 %all-gather.25.cloned.1.call-start = ((), (), s32[]{:S(2)}) async-start(), calls=%async_computation.15 | async-start | bytes 5988352 | tf_op jit(solution)/shard_map/all_gather | solution.py:259
  228.0 277.6 %all-gather.23.cloned.1.call-start = ((), (), s32[]{:S(2)}) async-start(), calls=%async_computation.14 | async-start | bytes 4718592 | tf_op jit(solution)/shard_map/all_gather | solution.py:266
  381.8 373.4 %copy-start = (f32[128,2048]{1,0:T(8,128)}, f32[128,2048]{1,0:T(8,128)S(1)}, u32[]{:S(2)}) copy-start(f32[128,2048]{1,0:T(8,128)S(1)} %get-tuple-element.892) | copy-start | bytes 3145732
  381.8 373.4 %copy-start.47 = (f32[128]{0:T(128)}, f32[128]{0:T(128)S(1)}, u32[]{:S(2)}) copy-start(f32[128]{0:T(128)S(1)} %add_rsqrt_fusion) | copy-start | bytes 1540
  383.0 163.5 %all-gather.27.cloned.1.call-start = ((), (), s32[]{:S(2)}) async-start(), calls=%async_computation.16 | async-start | bytes 2994176 | tf_op jit(solution)/shard_map/all_gather | solution.py:260
  383.8 236.1 %all-gather.29.cloned.1.call-start = ((), (), s32[]{:S(2)}) async-start(), calls=%async_computation.18 | async-start | bytes 4718592 | tf_op jit(solution)/shard_map/all_gather | solution.py:269
  384.5 369.0 %reduce-scatter.25.cloned.1.call-start = ((), (), s32[]{:S(2)}) async-start(), calls=%async_computation.19 | async-start | bytes 9437184 | tf_op jit(solution)/shard_map/reduce_scatter | solution.py:285
  640.6 185.3 %all-gather.31.cloned.1.call-start = ((), (), s32[]{:S(2)}) async-start(), calls=%async_computation.20 | async-start | bytes 4718592 | tf_op jit(solution)/shard_map/all_gather | solution.py:269
  756.4 167.5 %all-gather.35.cloned.1.call-start = ((), (), s32[]{:S(2)}) async-start(), calls=%async_computation.24 | async-start | bytes 2437120 | tf_op jit(solution)/shard_map/all_gather | solution.py:42
  834.8 206.1 %reduce-scatter.39.cloned.1.call-start = ((), (), s32[]{:S(2)}) async-start(), calls=%async_computation.29 | async-start | bytes 3342336
  846.8 196.5 %reduce-scatter.37.cloned.1.call-start = ((), (), s32[]{:S(2)}) async-start(), calls=%async_computation.28 | async-start | bytes 6127616
  865.6 246.4 %reduce-scatter.35.cloned.1.call-start = ((), (), s32[]{:S(2)}) async-start(), calls=%async_computation.27 | async-start | bytes 1114112
  923.8 202.3 %reduce-scatter.33.cloned.1.call-start = ((), (), s32[]{:S(2)}) async-start(), calls=%async_computation.26 | async-start | bytes 557056
  1019.7 169.1 %reduce-scatter.29.cloned.1.call-start = ((), (), s32[]{:S(2)}) async-start(), calls=%async_computation.22 | async-start | bytes 1114112 | tf_op jit(solution)/shard_map/reduce_scatter | solution.py:455
  1025.7 283.1 %reduce-scatter.27.cloned.1.call-start = ((), (), s32[]{:S(2)}) async-start(), calls=%async_computation.21 | async-start | bytes 9437184 | tf_op jit(solution)/shard_map/reduce_scatter | solution.py:285
  1032.0 393.1 %reduce-scatter.23.cloned.1.call-start = ((), (), s32[]{:S(2)}) async-start(), calls=%async_computation.17 | async-start | bytes 9437184 | tf_op jit(solution)/shard_map/reduce_scatter | solution.py:272
  1040.8 442.2 %reduce-scatter.31.cloned.1.call-start = ((), (), s32[]{:S(2)}) async-start(), calls=%async_computation.25 | async-start | bytes 557056
  1113.8 311.3 %copy-start.48 = (f32[128]{0:T(128)S(1)}, f32[128]{0:T(128)}, u32[]{:S(2)}) copy-start(f32[128]{0:T(128)} %copy-done.47) | copy-start | bytes 1540
  1113.8 311.3 %copy-start.52 = (f32[128]{0:T(128)S(1)}, f32[128]{0:T(128)}, u32[]{:S(2)}) copy-start(f32[128]{0:T(128)} %copy-done.51) | copy-start | bytes 1540
  (75 other events, 3686.4 us)
Sparse Core Ops, SparseCore 0:
  33.5 69.3 all-gather.16
  105.1 31.2 all-gather.18
  142.6 38.3 all-gather.32
  183.0 33.9 all-gather.20
  226.2 154.1 reduce-scatter.20
  382.5 49.6 all-gather.24
  435.5 70.0 all-gather.22
  507.9 38.6 all-gather.26
  549.2 70.6 all-gather.28
  640.7 112.7 reduce-scatter.24
  756.5 69.3 all-gather.30
  834.9 33.3 all-gather.34
  870.7 60.7 reduce-scatter.38
  933.8 68.1 reduce-scatter.36
  1004.1 60.4 reduce-scatter.34
  1066.9 59.1 reduce-scatter.32
  1128.9 59.9 reduce-scatter.28
  1193.0 115.7 reduce-scatter.26
  1312.6 112.4 reduce-scatter.22
  1427.4 55.4 reduce-scatter.30
where the time goes:
time: 1530 us; the launch traced here: 1510 us
  waiting for transfers between devices  987 us (65%)
  blocking collectives  217 us (14%)
  matrix products  135 us (9%)
  other arithmetic  92.4 us (6%)
  local copies, waits for them, and re-layouts  44.7 us (3%)
  between operations  18.8 us (1%)
    reduce_scatter x2, waiting for transfers between devices, branch_sum(): lax.psum_scatter(jnp.dot(operand, weight_mat, preferred_element_type=jnp....  266 us
    reduce_scatter x2, waiting for transfers between devices, input_sum(): return lax.psum_scatter(summed, 'tensor', scatter_dimension=0, tiled=True)  231 us
    all_gather x2, waiting for transfers between devices, gather_grad(): return lax.all_gather(grad_rows, 'tensor', axis=0, tiled=True)  131 us
    all_gather x2, waiting for transfers between devices, gather_normed(): return lax.all_gather(normed_rows, 'tensor', axis=0, tiled=True)  123 us
    unnamed x25, waiting for transfers between devices  68 us
    psum x1, blocking collectives, shards(): den_total = lax.psum(jnp.sum(denoms), ('dp', 'tensor'))  65.1 us
    reduce_scatter x1, waiting for transfers between devices, shards(): lax.psum_scatter(value_grad.astype(jnp.bfloat16), 'dp', scatter_dimension...  61.2 us
    unnamed x2, blocking collectives  54.4 us
  transfers between devices with their start and end apart: 20, of which 14 were waited for; matrix products, arithmetic and copies ran while one was open for 14% of the time, Pallas kernels for 0%

commit v1 on v0

v1 whole, which is shorter than its diff:
```python
import functools

import jax
import jax.numpy as jnp
import numpy as np
from jax import lax
from jax.experimental import pallas as pl
from jax.experimental.pallas import tpu as pltpu
from jax.sharding import PartitionSpec as P

D = 2048
HEADS = 16
FEAT = 16
DV = 128
FF = 5504
STEP = 10
FINE = ("x_lo", "z", "core", "y", "x_hi")
GROUPS = ("x_lo", "z", "x_hi")
N_GROUPS = 16
ROWS = 1024
CHUNK = 128
LOCAL_HEADS = 2
QK = 2 * LOCAL_HEADS * FEAT
VW = LOCAL_HEADS * DV
PW = VW + QK
FFL = 688
FFP = 768
PHI = 256
PHI_ROWS = 160
HEAD_ROWS = 192
STATE_ROWS = LOCAL_HEADS * HEAD_ROWS
TILE = 256

norm_eps = 1e-05
beta_one = 0.5
beta_two = 0.5
adam_eps = 1e-08
weight_decay = 0.01
gain_rate = 0.5

f32 = jnp.float32
bf16 = jnp.bfloat16


def ring(step):
    return [(i, (i + step) % 4) for i in range(4)]


FLIP = [(0, 1), (1, 0)]
CROSS = [(0, 0), (1, 2), (2, 1), (3, 3)]


def cross(a):
    return lax.ppermute(a, ("core", "x_hi"), CROSS)


def from_y(a, step):
    return lax.ppermute(a, "y", ring(-step))


def to_y(a, step):
    return lax.ppermute(a, "y", ring(step))


def swap_core(a):
    return lax.ppermute(a, "core", FLIP)


def gather_rows(mine):
    pieces = [mine, from_y(mine, 1), from_y(mine, 2), from_y(mine, 3)]
    others = [swap_core(piece) for piece in pieces]
    return jnp.concatenate(pieces + others, axis=0)


def scatter_rows(partial_of):
    send = partial_of(1).astype(bf16)
    got = swap_core(send)
    kept = partial_of(0)
    total = kept + got.astype(f32)
    low = total.astype(bf16)
    parts = [to_y(low[d * CHUNK : (d + 1) * CHUNK], d) for d in (1, 2, 3)]
    out = total[:CHUNK]
    for part in parts:
        out = out + part.astype(f32)
    return out


def matmul(a, b, dims=((1,), (0,))):
    return lax.dot_general(a, b, (dims, ((), ())), preferred_element_type=f32)


def feature_tables():
    pairs = [(a, b) for a in range(FEAT) for b in range(a, FEAT)]
    left = np.zeros((4, QK, PHI), np.float32)
    right = np.zeros((4, QK, PHI), np.float32)
    rows = np.zeros((8, PHI), np.float32)
    rows[0, 0] = 1.0
    rows[1, : 1 + FEAT] = 1.0
    rows[2, 0] = 1.0
    rows[2, 1 : 1 + FEAT] = FEAT ** (-0.25)
    for i, (a, b) in enumerate(pairs):
        rows[2, 1 + FEAT + i] = (1.0 if a == b else 2.0**0.5) * (2.0 * FEAT) ** (-0.5)
    move = np.zeros((4, QK, QK), np.float32)
    for kind in range(2):
        for head in range(LOCAL_HEADS):
            base = kind * LOCAL_HEADS * FEAT + head * FEAT
            other = (1 - kind) * LOCAL_HEADS * FEAT + head * FEAT
            n = kind * LOCAL_HEADS + head
            for a in range(FEAT):
                left[n, base + a, 1 + a] = 1.0
                move[n, base + a, other + a] = FEAT ** (-0.5)
            for i, (a, b) in enumerate(pairs):
                left[n, base + a, 1 + FEAT + i] = 1.0
                right[n, base + b, 1 + FEAT + i] = 1.0
    return (
        jnp.asarray(left, bf16),
        jnp.asarray(right, bf16),
        jnp.asarray(rows, f32),
        jnp.asarray(move, bf16),
    )


def split(a):
    hi = a.astype(bf16)
    return hi, (a - hi.astype(f32)).astype(bf16)


def dot_low(a, b, dims):
    hi, lo = split(a)
    return matmul(hi, b, dims) + matmul(lo, b, dims)


def dot_full(a, b, dims):
    ah, al = split(a)
    bh, bl = split(b)
    return matmul(ah, bh, dims) + (matmul(al, bh, dims) + matmul(ah, bl, dims))


def side(u, left, right, rows):
    return matmul(u, left) + rows[0:1], matmul(u, right) + rows[1:2]


def to_order(idx_ref, src_ref, dst):
    for i in range(8):
        dst[pl.ds(i * CHUNK, CHUNK), :] = src_ref[
            pl.ds(pl.multiple_of(idx_ref[i] * CHUNK, CHUNK), CHUNK), :
        ]


def from_order(idx_ref, i, dst_ref, block):
    dst_ref[pl.ds(pl.multiple_of(idx_ref[i] * CHUNK, CHUNK), CHUNK), :] = block


def state_rows(ref, head):
    base = head * HEAD_ROWS
    mat = jnp.concatenate(
        [ref[base : base + PHI_ROWS, :], jnp.zeros((PHI - PHI_ROWS, DV), f32)], axis=0
    )
    vec = jnp.concatenate(
        [ref[base + PHI_ROWS : base + PHI_ROWS + 1, :], ref[base + PHI_ROWS + 1 : base + PHI_ROWS + 2, :]],
        axis=1,
    )
    return mat, vec


def store_state(ref, head, mat, vec):
    base = head * HEAD_ROWS
    ref[base : base + PHI_ROWS, :] = mat[:PHI_ROWS]
    tail = jnp.concatenate(
        [vec[:, :DV], vec[:, DV:], jnp.zeros((HEAD_ROWS - PHI_ROWS - 2, DV), f32)], axis=0
    )
    ref[base + PHI_ROWS : base + HEAD_ROWS, :] = tail


def key_state_kernel(idx_ref, p_ref, masks_ref, left_ref, right_ref, rows_ref, out_ref, scr):
    to_order(idx_ref, p_ref, scr)
    in_last = masks_ref[:, 0:1]
    rows = rows_ref[...]
    for head in range(LOCAL_HEADS):
        n = LOCAL_HEADS + head
        mat = jnp.zeros((PHI, DV), f32)
        vec = jnp.zeros((1, PHI), f32)
        for r in range(0, ROWS, TILE):
            u = scr[r : r + TILE, VW:PW]
            v = scr[r : r + TILE, head * DV : (head + 1) * DV]
            one, two = side(u, left_ref[n], right_ref[n], rows)
            phi = one * two * rows[2:3] * in_last[r : r + TILE]
            mat = mat + dot_low(phi, v, ((0,), (0,)))
            vec = vec + jnp.sum(phi, axis=0, keepdims=True)
        store_state(out_ref, head, mat, vec)


def attend_kernel(
    idx_ref, p_ref, masks_ref, doc_row_ref, state_ref, left_ref, right_ref, rows_ref, move_ref,
    att_ref, den_ref, low_ref, scr,
):
    to_order(idx_ref, p_ref, scr)
    rows = rows_ref[...]
    u_all = scr[:, VW:PW]
    for head in range(LOCAL_HEADS):
        mat, vec = state_rows(state_ref, head)
        v_all = scr[:, head * DV : (head + 1) * DV]
        for r in range(0, ROWS, TILE):
            end = r + TILE
            u = scr[r:end, VW:PW]
            cont = masks_ref[r:end, 1:2]
            doc_col = masks_ref[r:end, 2:3]
            one, two = side(u, left_ref[head], right_ref[head], rows)
            phi = one * two * rows[2:3]
            num = cont * dot_full(phi, mat, ((1,), (0,)))
            den = cont * jnp.sum(phi * vec, axis=1, keepdims=True)
            moved = matmul(u, move_ref[head]).astype(bf16)
            s = matmul(moved, u_all[:end], ((1,), (1,)))
            at = r + lax.broadcasted_iota(jnp.int32, (TILE, end), 0)
            of = lax.broadcasted_iota(jnp.int32, (TILE, end), 1)
            allowed = (of <= at) & (doc_col == doc_row_ref[:, :end])
            kern = jnp.where(allowed, 1.0 + s + 0.5 * s * s, 0.0)
            num = num + matmul(kern.astype(bf16), v_all[:end])
            den = den + jnp.sum(kern, axis=1, keepdims=True)
            att = num / den
            att_ref[r:end, head * DV : (head + 1) * DV] = att
            den_ref[r:end, head : head + 1] = den
    for i in range(8):
        from_order(idx_ref, i, low_ref, att_ref[i * CHUNK : (i + 1) * CHUNK, :].astype(bf16))


def query_state_kernel(
    idx_ref, p_ref, ga_ref, masks_ref, att_ref, den_ref, left_ref, right_ref, rows_ref,
    out_ref, gn_ref, gd_ref, scr, gscr,
):
    to_order(idx_ref, p_ref, scr)
    to_order(idx_ref, ga_ref, gscr)
    rows = rows_ref[...]
    for head in range(LOCAL_HEADS):
        mat = jnp.zeros((PHI, DV), f32)
        vec = jnp.zeros((1, PHI), f32)
        cols = slice(head * DV, (head + 1) * DV)
        for r in range(0, ROWS, TILE):
            end = r + TILE
            den = den_ref[r:end, head : head + 1]
            ga = gscr[r:end, cols].astype(f32)
            gn = ga / den
            gd = -jnp.sum(ga * att_ref[r:end, cols], axis=1, keepdims=True) / den
            gn_ref[r:end, cols] = gn
            gd_ref[r:end, head : head + 1] = gd
            one, two = side(scr[r:end, VW:PW], left_ref[head], right_ref[head], rows)
            phi = one * two * rows[2:3] * masks_ref[r:end, 1:2]
            mat = mat + dot_full(phi, gn, ((0,), (0,)))
            vec = vec + jnp.sum(phi * gd, axis=0, keepdims=True)
        store_state(out_ref, head, mat, vec)


def attend_back_kernel(
    idx_ref, p_ref, gn_ref, gd_ref, masks_ref, doc_row_ref, state_ref, grad_state_ref,
    left_ref, right_ref, rows_ref, move_ref, out_ref, scr, gqk, gv,
):
    to_order(idx_ref, p_ref, scr)
    rows = rows_ref[...]
    u_all = scr[:, VW:PW]
    for head in range(LOCAL_HEADS):
        key = LOCAL_HEADS + head
        cols = slice(head * DV, (head + 1) * DV)
        mat, vec = state_rows(state_ref, head)
        gmat, gvec = state_rows(grad_state_ref, head)
        v_all = scr[:, cols]
        back_all = matmul(u_all, move_ref[key]).astype(bf16)
        for r in range(0, ROWS, TILE):
            end = r + TILE
            u = scr[r:end, VW:PW]
            cont = masks_ref[r:end, 1:2]
            in_last = masks_ref[r:end, 0:1]
            gn = gn_ref[r:end, cols]
            gd = gd_ref[r:end, head : head + 1]
            one, two = side(u, left_ref[head], right_ref[head], rows)
            grad = (dot_full(gn, mat, ((1,), (1,))) + gd * vec) * cont * rows[2:3]
            acc = dot_low(grad * two, left_ref[head], ((1,), (1,)))
            acc = acc + dot_low(grad * one, right_ref[head], ((1,), (1,)))
            one, two = side(u, left_ref[key], right_ref[key], rows)
            grad = (dot_low_right(v_all[r:end], gmat) + gvec) * in_last * rows[2:3]
            acc = acc + dot_low(grad * two, left_ref[key], ((1,), (1,)))
            acc = acc + dot_low(grad * one, right_ref[key], ((1,), (1,)))
            phi = one * two * rows[2:3] * in_last
            if head == 0:
                gqk[r:end, :] = acc
            else:
                gqk[r:end, :] = gqk[r:end, :] + acc
            gv[r:end, cols] = dot_full(phi, gmat, ((1,), (0,)))
        for r in range(0, ROWS, TILE):
            end = r + TILE
            u = scr[r:end, VW:PW]
            doc_col = masks_ref[r:end, 2:3]
            low_gn = gn_ref[r:end, cols].astype(bf16)
            gd = gd_ref[r:end, head : head + 1]
            moved = matmul(u, move_ref[head]).astype(bf16)
            s = matmul(moved, u_all[:end], ((1,), (1,)))
            at = r + lax.broadcasted_iota(jnp.int32, (TILE, end), 0)
            of = lax.broadcasted_iota(jnp.int32, (TILE, end), 1)
            allowed = (of <= at) & (doc_col == doc_row_ref[:, :end])
            kern = jnp.where(allowed, 1.0 + s + 0.5 * s * s, 0.0).astype(bf16)
            gk = matmul(low_gn, v_all[:end], ((1,), (1,))) + gd
            gs = jnp.where(allowed, gk * (1.0 + s), 0.0).astype(bf16)
            gqk[r:end, :] = gqk[r:end, :] + matmul(gs, back_all[:end])
            gqk[:end, :] = gqk[:end, :] + matmul(gs, moved, ((0,), (0,)))
            gv[:end, cols] = gv[:end, cols] + matmul(kern, low_gn, ((0,), (0,)))
    for i in range(8):
        chunk = slice(i * CHUNK, (i + 1) * CHUNK)
        from_order(
            idx_ref, i, out_ref,
            jnp.concatenate([gv[chunk, :], gqk[chunk, :]], axis=1).astype(bf16),
        )


def dot_low_right(a, b):
    hi, lo = split(b)
    return matmul(a, hi, ((1,), (1,))) + matmul(a, lo, ((1,), (1,)))


def call(kernel, outs, scratch, n_in):
    return pl.pallas_call(
        kernel,
        out_shape=outs,
        in_specs=[pl.BlockSpec(memory_space=pltpu.SMEM)]
        + [pl.BlockSpec(memory_space=pltpu.VMEM)] * (n_in - 1),
        out_specs=[pl.BlockSpec(memory_space=pltpu.VMEM)] * len(outs),
        scratch_shapes=scratch,
        compiler_params=pltpu.CompilerParams(vmem_limit_bytes=48 * 1024 * 1024),
    )


def adam_step(weight, moment_one, moment_two, reduced, step_rate):
    new_one = beta_one * moment_one + (1.0 - beta_one) * reduced
    new_two = beta_two * moment_two + (1.0 - beta_two) * reduced * reduced
    corrected_one = new_one / (1.0 - beta_one**STEP)
    corrected_two = new_two / (1.0 - beta_two**STEP)
    master = weight - step_rate * (
        corrected_one / (jnp.sqrt(corrected_two) + adam_eps) + weight_decay * weight
    )
    return (new_one, new_two, master)


def unit_norm(rows):
    inv = lax.rsqrt(jnp.mean(rows * rows, axis=-1, keepdims=True) + norm_eps)
    return rows * inv, inv


def unit_norm_back(shaped, unit, inv):
    return inv * (shaped - unit * jnp.mean(shaped * unit, axis=-1, keepdims=True))


def exchange(a):
    return lax.all_to_all(a, GROUPS, 0, 0)


def pad_cols(a, width):
    return jnp.pad(a, ((0, 0), (0, width - a.shape[1])))


def shards(
    tokens, cotangent, row_lengths, gains, gain_first, gain_second,
    feature_weight, feature_first, feature_second,
    value_weight, value_first, value_second,
    output_weight, output_first, output_second,
    gateup_weight, gateup_first, gateup_second,
    down_weight, down_first, down_second,
):
    core = lax.axis_index("core")
    y = lax.axis_index("y")
    group = (lax.axis_index("x_lo") * 4 + lax.axis_index("z")) * 2 + lax.axis_index("x_hi")
    gain_low = gains.astype(bf16).astype(f32)

    value_low = value_weight.astype(bf16)
    feature_low = feature_weight.reshape(128, QK).astype(bf16)
    gate_low = gateup_weight[:, 0].astype(bf16)
    up_low = gateup_weight[:, 1].astype(bf16)
    scale_one = gain_low[0][:, None]
    scale_two = gain_low[1][:, None]
    first_part = (jnp.concatenate([value_low, feature_low], axis=1).astype(f32) * scale_one).astype(bf16)
    second_part = jnp.concatenate(
        [
            output_weight.astype(bf16).T,
            pad_cols((gate_low.astype(f32) * scale_two).astype(bf16), FFP),
            pad_cols((up_low.astype(f32) * scale_two).astype(bf16), FFP),
        ],
        axis=1,
    )
    third_part = pad_cols(down_weight.astype(bf16).T, FFP)

    tokens = cross(tokens)
    first_part = cross(first_part)
    second_part = cross(second_part)
    third_part = cross(third_part)
    cot = cross(cotangent)

    inputs = tokens.astype(f32)
    unit_one, inv_one = unit_norm(inputs)
    acts_one = gather_rows(unit_one.astype(bf16))
    proj_w = exchange(jnp.broadcast_to(first_part[None], (N_GROUPS, CHUNK, PW))).reshape(D, PW)
    wide_w = lax.all_gather(second_part, GROUPS, axis=0, tiled=True)
    down_w = lax.all_gather(third_part, GROUPS, axis=0, tiled=True)
    out_w = wide_w[:, :VW]
    gateup_w = wide_w[:, VW:]
    grad_mlp = gather_rows(cot)

    ends = jnp.cumsum(row_lengths)

    def doc_of(pos):
        return jnp.sum((pos[..., None] >= ends).astype(jnp.int32), axis=-1)

    positions = group * ROWS + jnp.arange(ROWS, dtype=jnp.int32)
    docs = doc_of(positions)
    group_ids = jnp.arange(N_GROUPS, dtype=jnp.int32)
    doc_end = doc_of(group_ids * ROWS + (ROWS - 1))
    doc_before = jnp.where(group_ids > 0, doc_of(group_ids * ROWS - 1), -1)
    last_doc = docs[ROWS - 1]
    before = jnp.where(group > 0, doc_of(group * ROWS - 1), -1)
    masks = jnp.stack(
        [
            (docs == last_doc).astype(f32),
            (docs == before).astype(f32),
            docs.astype(f32),
        ],
        axis=1,
    )
    doc_row = docs.astype(f32)[None]
    carry = ((group_ids[None, :] < group_ids[:, None]) & (doc_end[None, :] == doc_before[:, None])).astype(f32)
    back = ((group_ids[None, :] > group_ids[:, None]) & (doc_before[None, :] == doc_end[:, None])).astype(f32)
    chunk_ids = jnp.arange(8, dtype=jnp.int32)
    idx = ((chunk_ids % 2) ^ core) * 4 + (chunk_ids // 2 - y) % 4

    left, right, rows, move = feature_tables()
    proj = matmul(acts_one, proj_w).astype(bf16)
    own_state = call(
        key_state_kernel,
        [jax.ShapeDtypeStruct((STATE_ROWS, DV), f32)],
        [pltpu.VMEM((ROWS, PW), bf16)],
        6,
    )(idx, proj, masks, left, right, rows)[0]
    slices = exchange(own_state.reshape(N_GROUPS, STATE_ROWS // N_GROUPS, DV))
    slices = jnp.sum(carry[:, :, None, None] * slices[None], axis=1)
    state = exchange(slices).reshape(STATE_ROWS, DV)
    att, den, attn_rows = call(
        attend_kernel,
        [
            jax.ShapeDtypeStruct((ROWS, VW), f32),
            jax.ShapeDtypeStruct((ROWS, LOCAL_HEADS), f32),
            jax.ShapeDtypeStruct((ROWS, VW), bf16),
        ],
        [pltpu.VMEM((ROWS, PW), bf16)],
        9,
    )(idx, proj, masks, doc_row, state, left, right, rows, move)
    half = ROWS // 2

    def of_half(a, h):
        return a[h * half : (h + 1) * half]

    middle = inputs + scatter_rows(
        lambda h: matmul(of_half(attn_rows, h), out_w, ((1,), (1,)))
    )
    unit_two, inv_two = unit_norm(middle)
    acts_two = gather_rows(unit_two.astype(bf16))
    gate_up = matmul(acts_two, gateup_w)
    grad_hidden = matmul(grad_mlp, down_w)
    gate = gate_up[:, :FFP]
    up = gate_up[:, FFP:]
    sigmoid = jax.nn.sigmoid(gate)
    silu = gate * sigmoid
    hidden = (silu * up).astype(bf16)
    dsilu = sigmoid * (1.0 + gate * (1.0 - sigmoid))
    grad_gate_up = jnp.concatenate([grad_hidden * up * dsilu, grad_hidden * silu], axis=1).astype(bf16)

    shaped_two = scatter_rows(lambda h: matmul(of_half(grad_gate_up, h), gateup_w, ((1,), (1,))))
    grad_out = cot.astype(f32)
    grad_mid = grad_out + unit_norm_back(shaped_two, unit_two, inv_two)
    grad_attn = gather_rows(grad_mid.astype(bf16))

    gateup_grad = matmul(acts_two, grad_gate_up, ((0,), (0,))).astype(bf16)
    down_grad = matmul(grad_mlp, hidden, ((0,), (0,))).astype(bf16)
    mlp_grad = lax.psum_scatter(
        jnp.concatenate([gateup_grad, down_grad], axis=1), GROUPS, scatter_dimension=0, tiled=True
    )
    mixed = middle + scatter_rows(lambda h: matmul(of_half(hidden, h), down_w, ((1,), (1,))))
    mixed = cross(mixed.astype(bf16))

    grad_low = matmul(grad_attn, out_w).astype(bf16)
    own_grad, gn, gd = call(
        query_state_kernel,
        [
            jax.ShapeDtypeStruct((STATE_ROWS, DV), f32),
            jax.ShapeDtypeStruct((ROWS, VW), f32),
            jax.ShapeDtypeStruct((ROWS, LOCAL_HEADS), f32),
        ],
        [pltpu.VMEM((ROWS, PW), bf16), pltpu.VMEM((ROWS, VW), bf16)],
        9,
    )(idx, proj, grad_low, masks, att, den, left, right, rows)
    den_part = jnp.sum(jnp.abs(den))
    slices = exchange(
        jnp.concatenate(
            [
                own_grad.reshape(N_GROUPS, STATE_ROWS // N_GROUPS, DV),
                jnp.full((N_GROUPS, 8, DV), den_part, f32),
            ],
            axis=1,
        )
    )
    den_group = jnp.sum(slices[:, STATE_ROWS // N_GROUPS :], axis=0)
    slices = jnp.sum(back[:, :, None, None] * slices[None, :, : STATE_ROWS // N_GROUPS], axis=1)
    grad_state = exchange(slices).reshape(STATE_ROWS, DV)
    grad_proj = call(
        attend_back_kernel,
        [jax.ShapeDtypeStruct((ROWS, PW), bf16)],
        [pltpu.VMEM((ROWS, PW), bf16), pltpu.VMEM((ROWS, QK), f32), pltpu.VMEM((ROWS, VW), f32)],
        12,
    )(idx, proj, gn, gd, masks, doc_row, state, grad_state, left, right, rows, move)[0]

    shaped_one = scatter_rows(lambda h: matmul(of_half(grad_proj, h), proj_w, ((1,), (1,))))
    grad_tokens = grad_mid + unit_norm_back(shaped_one, unit_one, inv_one)
    grad_tokens = cross(grad_tokens.astype(bf16)).astype(f32)

    output_grad = matmul(grad_attn, attn_rows, ((0,), (0,))).astype(bf16)
    proj_grad = matmul(acts_one, grad_proj, ((0,), (0,))).astype(bf16)
    attn_grad = exchange(
        jnp.concatenate([output_grad, proj_grad], axis=1).reshape(N_GROUPS, CHUNK, VW + PW)
    )
    attn_grad = cross(jnp.sum(attn_grad.astype(f32), axis=0).astype(bf16)).astype(f32)
    mlp_grad = cross(mlp_grad).astype(f32)
    den_group = cross(den_group)

    output_sum = attn_grad[:, :VW].T
    unit_value = attn_grad[:, VW : 2 * VW]
    unit_feature = attn_grad[:, 2 * VW :]
    unit_gate = mlp_grad[:, :FFL]
    unit_up = mlp_grad[:, FFP : FFP + FFL]
    down_sum = mlp_grad[:, 2 * FFP : 2 * FFP + FFL].T
    gain_one = jnp.sum(unit_value * value_low.astype(f32), axis=1) + jnp.sum(
        unit_feature * feature_low.astype(f32), axis=1
    )
    gain_two = jnp.sum(unit_gate * gate_low.astype(f32), axis=1) + jnp.sum(
        unit_up * up_low.astype(f32), axis=1
    )
    small = jnp.concatenate([gain_one[None], gain_two[None], den_group[:6]], axis=0)
    small = jnp.sum(
        lax.all_to_all(jnp.broadcast_to(small[None], (8, 8, CHUNK)), ("y", "x_hi"), 0, 0), axis=0
    )
    gain_total = small[:2]
    den_mean = small[2, 0] / (N_GROUPS * ROWS * HEADS)
    value_sum = unit_value * scale_one
    feature_sum = (unit_feature * scale_one).reshape(CHUNK, 2, QK // 2)
    gateup_sum = jnp.stack([unit_gate * scale_two, unit_up * scale_two], axis=1)
    news = [
        adam_step(gains, gain_first, gain_second, gain_total, gain_rate),
        adam_step(feature_weight, feature_first, feature_second, feature_sum, D ** (-0.5)),
        adam_step(value_weight, value_first, value_second, value_sum, D ** (-0.5)),
        adam_step(
            output_weight, output_first, output_second, output_sum, (HEADS * DV // 64) ** (-0.5)
        ),
        adam_step(gateup_weight, gateup_first, gateup_second, gateup_sum, D ** (-0.5)),
        adam_step(down_weight, down_first, down_second, down_sum, FF ** (-0.5)),
    ]
    return (mixed, grad_tokens, den_mean) + tuple(a for new in news for a in new)


def solution(mesh):
    fine = jax.sharding.Mesh(mesh.devices.reshape(2, 4, 2, 4, 2), FINE)
    dp = ("x_lo", "z", "core")
    tensor = ("y", "x_hi")
    rows = P(FINE, None)
    gain = P(None, dp)
    deep = P(dp, None, tensor)
    down = P(dp, tensor)
    across = P(tensor, dp)
    return jax.shard_map(
        shards,
        mesh=fine,
        in_specs=(rows, rows, P())
        + (gain,) * 3
        + (deep,) * 3
        + (down,) * 3
        + (across,) * 3
        + (deep,) * 3
        + (across,) * 3,
        out_specs=(rows, rows, P())
        + (gain,) * 3
        + (deep,) * 3
        + (down,) * 3
        + (across,) * 3
        + (deep,) * 3
        + (across,) * 3,
        check_vma=False,
    )
```

time: 1530 us -> 749 us (0.49)
  waiting for transfers between devices: 987 us -> 298 us
  blocking collectives: 217 us -> 57.5 us
  starting transfers between devices: 12 us -> 167 us
  matrix products: 135 us -> 73.7 us
  other arithmetic: 92.4 us -> 47.4 us
  Pallas kernels: 0 us -> 28.6 us
    reduce_scatter x5 -> x0, waiting for transfers between devices: 558 us -> none  [the longest x2 266 us: branch_sum(): lax.psum_scatter(jnp.dot(operand, weight_mat, preferred_element_type=jnp....]
    all_gather x10 -> x2, waiting for transfers between devices: 361 us -> 70 us  [the longest x1 53.9 us: shards(): wide_w = lax.all_gather(second_part, GROUPS, axis=0, tiled=True)]
    ppermute x0 -> x54, waiting for transfers between devices: none -> 195 us  [the longest x10 86.9 us: cross(): return lax.ppermute(a, ('core', 'x_hi'), CROSS)]
    ppermute x0 -> x54, starting transfers between devices: none -> 103 us  [the longest x10 40.6 us: cross(): return lax.ppermute(a, ('core', 'x_hi'), CROSS)]
    psum x2 -> x0, blocking collectives: 85.8 us -> none  [the longest x1 65.1 us: shards(): den_total = lax.psum(jnp.sum(denoms), ('dp', 'tensor'))]
    all_gather x4 -> x0, blocking collectives: 76.5 us -> none  [the longest x1 22.1 us: shards(): lax.all_gather(low_params[0], 'dp', axis=1, tiled=True)]
    unnamed x25 -> x4, waiting for transfers between devices: 68 us -> 0.07 us
    all_to_all x0 -> x5, starting transfers between devices: none -> 64.2 us  [the longest x4 60.6 us: exchange(): return lax.all_to_all(a, GROUPS, 0, 0)]
  transfers between devices with their start and end apart: 20 -> 62, of which waited for: 14 -> 26; matrix products, arithmetic and copies ran while one was open for 14% -> 14% of each run, Pallas kernels for 0% -> 4%
where the time goes in v1:
time: 749 us; the launch traced here: 738 us
  waiting for transfers between devices  298 us (40%)
  starting transfers between devices  167 us (22%)
  matrix products  73.7 us (10%)
  blocking collectives  57.5 us (8%)
  other arithmetic  47.4 us (6%)
  local copies, waits for them, and re-layouts  47.4 us (6%)
  Pallas kernels  28.6 us (4%)
  between operations  18 us (2%)
    ppermute x10, waiting for transfers between devices, cross(): return lax.ppermute(a, ('core', 'x_hi'), CROSS)  86.9 us
    dot_general x16, matrix products, matmul(): return lax.dot_general(a, b, (dims, ((), ())), preferred_element_type=f32)  73.7 us
    all_to_all x4, starting transfers between devices, exchange(): return lax.all_to_all(a, GROUPS, 0, 0)  60.6 us
    all_to_all x2, blocking collectives, exchange(): return lax.all_to_all(a, GROUPS, 0, 0)  57.5 us
    ppermute x12, waiting for transfers between devices, to_y(): return lax.ppermute(a, 'y', ring(step))  54.5 us
    all_gather x1, waiting for transfers between devices, shards(): wide_w = lax.all_gather(second_part, GROUPS, axis=0, tiled=True)  53.9 us
    ppermute x12, waiting for transfers between devices, from_y(): return lax.ppermute(a, 'y', ring(-step))  51.2 us
    ppermute x10, starting transfers between devices, cross(): return lax.ppermute(a, ('core', 'x_hi'), CROSS)  40.6 us
  transfers between devices with their start and end apart: 62, of which 26 were waited for; matrix products, arithmetic and copies ran while one was open for 14% of the time, Pallas kernels for 4%

profile of v1, /device:TPU:1, one launch (start us, length us, event | category | flops | bytes accessed | tf_op | source)
XLA Modules:
  0.0 737.8 jit_solution(13260886844181573580)
XLA Ops:
  62.9 17.8 %all-to-all-done = bf16[16,128,320]{1,2,0:T(8,128)(2,1)S(1)} async-done(((bf16[16,128,320]{1,2,0:T(8,128)(2,1)}), bf16[16,128,320]{1,2,0:T(8,128)(2,1)S(1)}, u32[]{:S(2)}, u32[]{:S(2)}) %all-to-all-start) | async-done | bytes 1310752 | tf_op jit(solution)/shard_map/all_to_all | solution.py:351
  89.9 43.8 %all-to-all-start.1 = ((f32[16,24,128]{2,1,0:T(8,128)}), f32[16,24,128]{2,1,0:T(8,128)S(1)}, u32[]{:S(2)}, u32[]{:S(2)}) async-start(f32[16,24,128]{2,1,0:T(8,128)} %bitcast.9), calls=%async_computation.1 | async-start | bytes 393216 | tf_op jit(solution)/shard_map/all_to_all | solution.py:351
  133.8 8.5 %all-to-all-done.1 = f32[16,24,128]{2,1,0:T(8,128)S(1)} async-done(((f32[16,24,128]{2,1,0:T(8,128)}), f32[16,24,128]{2,1,0:T(8,128)S(1)}, u32[]{:S(2)}, u32[]{:S(2)}) %all-to-all-start.1) | async-done | bytes 196640 | tf_op jit(solution)/shard_map/all_to_all | solution.py:351
  142.6 39.0 %all_to_all.35 = f32[16,24,128]{2,1,0:T(8,128)S(1)} all-to-all(f32[16,24,128]{2,1,0:T(8,128)S(1)} %multiply_reduce_fusion.1), channel_id=1, replica_groups=mesh['x_lo'=2,'z'=4,'core'=2,'y'=4,'x_hi'=2] {'x_lo','z','x_hi'}, dimensions={0} | all-to-all | bytes 393216 | tf_op jit(solution)/shard_map/all_to_all | solution.py:351
  188.7 53.9 %all-gather.3.cloned.1.call-done = bf16[2048,1792]{0,1:T(8,128)(2,1)} async-done(((bf16[128,1792]{0,1:T(8,128)(2,1)}), bf16[2048,1792]{0,1:T(8,128)(2,1)}) %all-gather.3.cloned.1.call-update) | async-done | bytes 7340048 | tf_op jit(solution)/shard_map/all_gather | solution.py:398
  249.1 10.4 %collective-permute-done.27 = bf16[128,2048]{1,0:T(8,128)(2,1)} collective-permute-done((bf16[128,2048]{1,0:T(8,128)(2,1)}, bf16[128,2048]{1,0:T(8,128)(2,1)}, u32[]{:S(2)}, u32[]{:S(2)}) %collective-permute-start.27) | collective-permute-done | bytes 524320 | tf_op jit(solution)/shard_map/ppermute | solution.py:54
  285.3 8.7 %collective-permute-done.30 = bf16[128,2048]{1,0:T(8,128)(2,1)S(1)} collective-permute-done((bf16[128,2048]{1,0:T(8,128)(2,1)}, bf16[128,2048]{1,0:T(8,128)(2,1)S(1)}, u32[]{:S(2)}, u32[]{:S(2)}) %collective-permute-start.30) | collective-permute-done | bytes 524320 | tf_op jit(solution)/shard_map/ppermute | solution.py:58
  294.8 10.4 %collective-permute-done.11 = bf16[128,2048]{1,0:T(8,128)(2,1)S(1)} collective-permute-done((bf16[128,2048]{1,0:T(8,128)(2,1)S(1)}, bf16[128,2048]{1,0:T(8,128)(2,1)S(1)}, u32[]{:S(2)}, u32[]{:S(2)}) %collective-permute-start.11) | collective-permute-done | bytes 524320 | tf_op jit(solution)/shard_map/ppermute | solution.py:62
  316.8 9.6 %collective-permute-done.14 = bf16[128,2048]{1,0:T(8,128)(2,1)S(1)} collective-permute-done((bf16[128,2048]{1,0:T(8,128)(2,1)S(1)}, bf16[128,2048]{1,0:T(8,128)(2,1)S(1)}, u32[]{:S(2)}, u32[]{:S(2)}) %collective-permute-start.14) | collective-permute-done | bytes 524320 | tf_op jit(solution)/shard_map/ppermute | solution.py:58
  328.7 10.6 %collective-permute-done.16 = bf16[128,2048]{1,0:T(8,128)(2,1)S(1)} collective-permute-done((bf16[128,2048]{1,0:T(8,128)(2,1)S(1)}, bf16[128,2048]{1,0:T(8,128)(2,1)S(1)}, u32[]{:S(2)}, u32[]{:S(2)}) %collective-permute-start.16) | collective-permute-done | bytes 524320 | tf_op jit(solution)/shard_map/ppermute | solution.py:58
  343.3 8.6 %fusion.4 = f32[1024,1536]{1,0:T(8,128)} fusion(bf16[1024,2048]{1,0:T(8,128)(2,1)S(1)} %constant_dynamic-update-slice_fusion.8, bf16[2048,1792]{0,1:T(8,128)(2,1)S(1)} %bitcast.112), kind=kOutput, calls=%fused_computation.6 | convolution fusion | flops 6442450944 | bytes 16777216 | tf_op jit(solution)/shard_map/dot_general | solution.py:89
  351.8 16.1 %all-gather.5.cloned.1.call-done = bf16[2048,768]{0,1:T(8,128)(2,1)} async-done(((bf16[128,768]{0,1:T(8,128)(2,1)}), bf16[2048,768]{0,1:T(8,128)(2,1)}) %all-gather.5.cloned.1.call-update) | async-done | bytes 3145744 | tf_op jit(solution)/shard_map/all_gather | solution.py:399
  368.0 9.5 %multiply_convert_fusion = (bf16[1024,768]{1,0:T(8,128)(2,1)S(1)}, bf16[1024,768]{1,0:T(8,128)(2,1)S(1)}, bf16[1024,768]{1,0:T(8,128)(2,1)S(1)}) fusion(f32[1024,1536]{1,0:T(8,128)} %fusion.4, bf16[1024,2048]{1,0:T(8,128)(2,1)} %copy-done.39, bf16[2048,768]{0,1:T(8,128)(2,1)} %all-gather.5.cloned.1.call-done), kind=kOutput, calls=%fused_computation.19 | convolution fusion | flops 3233021952 | bytes 18350080 | tf_op jit(solution)/shard_map/dot_general | solution.py:89
  381.4 7.8 %convolution_convert_fusion = bf16[2048,1536]{0,1:T(8,128)(2,1)S(1)} fusion(bf16[1024,2048]{1,0:T(8,128)(2,1)S(1)} %copy-done.37, bf16[1024,768]{1,0:T(8,128)(2,1)S(1)} %get-tuple-element.169, bf16[1024,768]{1,0:T(8,128)(2,1)S(1)} %get-tuple-element.170), kind=kOutput, calls=%fused_computation.1 | convolution fusion | flops 6451888128 | bytes 13631488 | tf_op jit(solution)/shard_map/dot_general | solution.py:89
  389.2 11.9 %pad_maximum_fusion = bf16[2048,2304]{0,1:T(8,128)(2,1)} fusion(bf16[2048,768]{0,1:T(8,128)(2,1)S(1)} %convolution_convert_fusion.1, bf16[2048,1536]{0,1:T(8,128)(2,1)S(1)} %convolution_convert_fusion), kind=kLoop, calls=%fused_computation | loop fusion | flops 18874368 | bytes 18874368 | tf_op jit(solution)/shard_map/concatenate | solution.py:479
  401.1 12.6 %copy.125 = bf16[2048,2304]{1,0:T(8,128)(2,1)} copy(bf16[2048,2304]{0,1:T(8,128)(2,1)} %pad_maximum_fusion) | data formatting | bytes 18874368
  451.0 10.8 %collective-permute-done.24 = bf16[128,2048]{1,0:T(8,128)(2,1)S(1)} collective-permute-done((bf16[128,2048]{1,0:T(8,128)(2,1)S(1)}, bf16[128,2048]{1,0:T(8,128)(2,1)S(1)}, u32[]{:S(2)}, u32[]{:S(2)}) %collective-permute-start.24) | collective-permute-done | bytes 524320 | tf_op jit(solution)/shard_map/ppermute | solution.py:62
  461.9 10.0 %collective-permute-done.36 = bf16[128,2048]{1,0:T(8,128)(2,1)S(1)} collective-permute-done((bf16[128,2048]{1,0:T(8,128)(2,1)S(1)}, bf16[128,2048]{1,0:T(8,128)(2,1)S(1)}, u32[]{:S(2)}, u32[]{:S(2)}) %collective-permute-start.36) | collective-permute-done | bytes 524320 | tf_op jit(solution)/shard_map/ppermute | solution.py:62
  471.9 12.5 %collective-permute-done.37 = bf16[128,2048]{1,0:T(8,128)(2,1)S(1)} collective-permute-done((bf16[128,2048]{1,0:T(8,128)(2,1)S(1)}, bf16[128,2048]{1,0:T(8,128)(2,1)S(1)}, u32[]{:S(2)}, u32[]{:S(2)}) %collective-permute-start.37) | collective-permute-done | bytes 524320 | tf_op jit(solution)/shard_map/ppermute | solution.py:62
  494.8 18.2 %collective-permute-done.39 = bf16[128,2048]{1,0:T(8,128)(2,1)S(1)} collective-permute-done((bf16[128,2048]{1,0:T(8,128)(2,1)S(1)}, bf16[128,2048]{1,0:T(8,128)(2,1)S(1)}, u32[]{:S(2)}, u32[]{:S(2)}) %collective-permute-start.39) | collective-permute-done | bytes 524320 | tf_op jit(solution)/shard_map/ppermute | solution.py:58
  527.7 18.5 %all_to_all.36 = f32[16,32,128]{2,1,0:T(8,128)S(1)} all-to-all(f32[16,32,128]{2,1,0:T(8,128)S(1)} %concatenate.41), channel_id=1, replica_groups=mesh['x_lo'=2,'z'=4,'core'=2,'y'=4,'x_hi'=2] {'x_lo','z','x_hi'}, dimensions={0} | all-to-all | bytes 524288 | tf_op jit(solution)/shard_map/all_to_all | solution.py:351
  564.7 14.8 %shard_map.403 = bf16[1024,320]{1,0:T(8,128)(2,1)S(1)} custom-call(s32[8]{0:T(128)S(1)} %fusion.72.idx_ref, bf16[1024,320]{1,0:T(8,128)(2,1)S(1)} %convolution_convert_fusion.7.p_ref, f32[1024,256]{1,0:T(8,128)S(1)} %copy-done.5, f32[1024,2]{1,0:T(8,128)S(1)} %copy-done.7, f32[1024,3]{1,0:T(8,128)S(1)} %copy.110.masks_ref, f32[1,1024]{1,0:T(1,128)S(1)} %bitcast.110, ...), custom_call_target="tpu_custom_call" | custom-call | tf_op jit(solution)/shard_map/pallas_call | solution.py:508
  597.7 61.3 %collective-permute-done.26 = bf16[128,2048]{1,0:T(8,128)(2,1)} collective-permute-done((bf16[128,2048]{1,0:T(8,128)(2,1)S(1)}, bf16[128,2048]{1,0:T(8,128)(2,1)}, u32[]{:S(2)}, u32[]{:S(2)}) %collective-permute-start.26) | collective-permute-done | bytes 524320 | tf_op jit(solution)/shard_map/ppermute | solution.py:54
  691.4 8.6 %collective-permute-start.50 = (bf16[128,2048]{1,0:T(8,128)(2,1)S(1)}, bf16[128,2048]{1,0:T(8,128)(2,1)}, u32[]{:S(2)}, u32[]{:S(2)}) collective-permute-start(bf16[128,2048]{1,0:T(8,128)(2,1)S(1)} %fusion.29), channel_id=1, source_target_pairs={{0,0},{1,8},{8,1},{9,9},{2,2},{3,10},{10,3},{11,11},{4,4},{5,12},{... | collective-permute-start | bytes 1572872 | tf_op jit(solution)/shard_map/ppermute | solution.py:54
  (359 shorter events, 285.8 us)
Async XLA Ops:
  7.2 235.4 %all-gather.3.cloned.1.call-start = ((), (), s32[]{:S(2)}) async-start(), calls=%async_computation.8 | async-start | bytes 7798784 | tf_op jit(solution)/shard_map/all_gather | solution.py:398
  42.3 38.4 %all-to-all-start = ((bf16[16,128,320]{1,2,0:T(8,128)(2,1)}), bf16[16,128,320]{1,2,0:T(8,128)(2,1)S(1)}, u32[]{:S(2)}, u32[]{:S(2)}) async-start(bf16[16,128,320]{1,2,0:T(8,128)(2,1)} %broadcast_in_dim.5), calls=%async_computation | async-start | bytes 2621440 | tf_op jit(solution)/shard_map/all_to_all | solution.py:351
  89.9 52.4 %all-to-all-start.1 = ((f32[16,24,128]{2,1,0:T(8,128)}), f32[16,24,128]{2,1,0:T(8,128)S(1)}, u32[]{:S(2)}, u32[]{:S(2)}) async-start(f32[16,24,128]{2,1,0:T(8,128)} %bitcast.9), calls=%async_computation.1 | async-start | bytes 393216 | tf_op jit(solution)/shard_map/all_to_all | solution.py:351
  133.6 234.3 %all-gather.5.cloned.1.call-start = ((), (), s32[]{:S(2)}) async-start(), calls=%async_computation.9 | async-start | bytes 3342336 | tf_op jit(solution)/shard_map/all_gather | solution.py:399
  245.8 32.7 %collective-permute-start.10 = (bf16[512,2048]{1,0:T(8,128)(2,1)}, bf16[512,2048]{1,0:T(8,128)(2,1)}, u32[]{:S(2)}, u32[]{:S(2)}) collective-permute-start(bf16[512,2048]{1,0:T(8,128)(2,1)} %convolution_convert_fusion.2), channel_id=1, source_target_pairs={{0,8},{8,0},{1,9},{9,1},{2,10},{10,2},{3,11},{11,3},{4,12},{12,4},... | collective-permute-start | bytes 6291464 | tf_op jit(solution)/shard_map/ppermute | solution.py:66
  269.3 430.8 %reduce-scatter.4.cloned.1.call-start = ((), (), s32[]{:S(2)}) async-start(), calls=%async_computation.10 | async-start | bytes 10027008
  281.4 23.8 %collective-permute-start.11 = (bf16[128,2048]{1,0:T(8,128)(2,1)S(1)}, bf16[128,2048]{1,0:T(8,128)(2,1)S(1)}, u32[]{:S(2)}, u32[]{:S(2)}) collective-permute-start(bf16[128,2048]{1,0:T(8,128)(2,1)S(1)} %get-tuple-element.181), channel_id=1, source_target_pairs={{0,2},{2,4},{4,6},{6,0},{1,3},{3,5},{5,7},{7,1},{8,10},{10,12},{12... | collective-permute-start | bytes 1572872 | tf_op jit(solution)/shard_map/ppermute | solution.py:62
  281.8 29.8 %collective-permute-start.12 = (bf16[128,2048]{1,0:T(8,128)(2,1)S(1)}, bf16[128,2048]{1,0:T(8,128)(2,1)S(1)}, u32[]{:S(2)}, u32[]{:S(2)}) collective-permute-start(bf16[128,2048]{1,0:T(8,128)(2,1)S(1)} %get-tuple-element.183), channel_id=1, source_target_pairs={{0,4},{2,6},{4,0},{6,2},{1,5},{3,7},{5,1},{7,3},{8,12},{10,14},{12... | collective-permute-start | bytes 1572872 | tf_op jit(solution)/shard_map/ppermute | solution.py:62
  285.3 26.3 %collective-permute-start.13 = (bf16[128,2048]{1,0:T(8,128)(2,1)S(1)}, bf16[128,2048]{1,0:T(8,128)(2,1)S(1)}, u32[]{:S(2)}, u32[]{:S(2)}) collective-permute-start(bf16[128,2048]{1,0:T(8,128)(2,1)S(1)} %get-tuple-element.182), channel_id=1, source_target_pairs={{0,6},{2,0},{4,2},{6,4},{1,7},{3,1},{5,3},{7,5},{8,14},{10,8},{12,... | collective-permute-start | bytes 1572872 | tf_op jit(solution)/shard_map/ppermute | solution.py:62
  315.6 23.8 %collective-permute-start.16 = (bf16[128,2048]{1,0:T(8,128)(2,1)S(1)}, bf16[128,2048]{1,0:T(8,128)(2,1)S(1)}, u32[]{:S(2)}, u32[]{:S(2)}) collective-permute-start(bf16[128,2048]{1,0:T(8,128)(2,1)S(1)} %get-tuple-element.164), channel_id=1, source_target_pairs={{0,2},{2,4},{4,6},{6,0},{1,3},{3,5},{5,7},{7,1},{8,10},{10,12},{12... | collective-permute-start | bytes 1572872 | tf_op jit(solution)/shard_map/ppermute | solution.py:58
  316.5 23.0 %collective-permute-start.17 = (bf16[128,2048]{1,0:T(8,128)(2,1)S(1)}, bf16[128,2048]{1,0:T(8,128)(2,1)S(1)}, u32[]{:S(2)}, u32[]{:S(2)}) collective-permute-start(bf16[128,2048]{1,0:T(8,128)(2,1)S(1)} %get-tuple-element.164), channel_id=1, source_target_pairs={{0,8},{8,0},{1,9},{9,1},{2,10},{10,2},{3,11},{11,3},{4,12},{12,4},... | collective-permute-start | bytes 1572872 | tf_op jit(solution)/shard_map/ppermute | solution.py:66
  436.3 25.6 %collective-permute-start.24 = (bf16[128,2048]{1,0:T(8,128)(2,1)S(1)}, bf16[128,2048]{1,0:T(8,128)(2,1)S(1)}, u32[]{:S(2)}, u32[]{:S(2)}) collective-permute-start(bf16[128,2048]{1,0:T(8,128)(2,1)S(1)} %get-tuple-element.180), channel_id=1, source_target_pairs={{0,4},{2,6},{4,0},{6,2},{1,5},{3,7},{5,1},{7,3},{8,12},{10,14},{12... | collective-permute-start | bytes 1572872 | tf_op jit(solution)/shard_map/ppermute | solution.py:62
  438.8 23.1 %collective-permute-start.25 = (bf16[128,2048]{1,0:T(8,128)(2,1)S(1)}, bf16[128,2048]{1,0:T(8,128)(2,1)S(1)}, u32[]{:S(2)}, u32[]{:S(2)}) collective-permute-start(bf16[128,2048]{1,0:T(8,128)(2,1)S(1)} %get-tuple-element.179), channel_id=1, source_target_pairs={{0,6},{2,0},{4,2},{6,4},{1,7},{3,1},{5,3},{7,5},{8,14},{10,8},{12,... | collective-permute-start | bytes 1572872 | tf_op jit(solution)/shard_map/ppermute | solution.py:62
  445.5 26.4 %collective-permute-start.36 = (bf16[128,2048]{1,0:T(8,128)(2,1)S(1)}, bf16[128,2048]{1,0:T(8,128)(2,1)S(1)}, u32[]{:S(2)}, u32[]{:S(2)}) collective-permute-start(bf16[128,2048]{1,0:T(8,128)(2,1)S(1)} %get-tuple-element.175), channel_id=1, source_target_pairs={{0,2},{2,4},{4,6},{6,0},{1,3},{3,5},{5,7},{7,1},{8,10},{10,12},{12... | collective-permute-start | bytes 1572872 | tf_op jit(solution)/shard_map/ppermute | solution.py:62
  445.5 38.8 %collective-permute-start.37 = (bf16[128,2048]{1,0:T(8,128)(2,1)S(1)}, bf16[128,2048]{1,0:T(8,128)(2,1)S(1)}, u32[]{:S(2)}, u32[]{:S(2)}) collective-permute-start(bf16[128,2048]{1,0:T(8,128)(2,1)S(1)} %get-tuple-element.177), channel_id=1, source_target_pairs={{0,4},{2,6},{4,0},{6,2},{1,5},{3,7},{5,1},{7,3},{8,12},{10,14},{12... | collective-permute-start | bytes 1572872 | tf_op jit(solution)/shard_map/ppermute | solution.py:62
  449.7 34.6 %collective-permute-start.38 = (bf16[128,2048]{1,0:T(8,128)(2,1)S(1)}, bf16[128,2048]{1,0:T(8,128)(2,1)S(1)}, u32[]{:S(2)}, u32[]{:S(2)}) collective-permute-start(bf16[128,2048]{1,0:T(8,128)(2,1)S(1)} %get-tuple-element.176), channel_id=1, source_target_pairs={{0,6},{2,0},{4,2},{6,4},{1,7},{3,1},{5,3},{7,5},{8,14},{10,8},{12,... | collective-permute-start | bytes 1572872 | tf_op jit(solution)/shard_map/ppermute | solution.py:62
  488.5 24.5 %collective-permute-start.39 = (bf16[128,2048]{1,0:T(8,128)(2,1)S(1)}, bf16[128,2048]{1,0:T(8,128)(2,1)S(1)}, u32[]{:S(2)}, u32[]{:S(2)}) collective-permute-start(bf16[128,2048]{1,0:T(8,128)(2,1)S(1)} %get-tuple-element.161), channel_id=1, source_target_pairs={{0,6},{2,0},{4,2},{6,4},{1,7},{3,1},{5,3},{7,5},{8,14},{10,8},{12,... | collective-permute-start | bytes 1572872 | tf_op jit(solution)/shard_map/ppermute | solution.py:58
  491.0 23.5 %collective-permute-start.40 = (bf16[128,2048]{1,0:T(8,128)(2,1)S(1)}, bf16[128,2048]{1,0:T(8,128)(2,1)S(1)}, u32[]{:S(2)}, u32[]{:S(2)}) collective-permute-start(bf16[128,2048]{1,0:T(8,128)(2,1)S(1)} %get-tuple-element.161), channel_id=1, source_target_pairs={{0,4},{2,6},{4,0},{6,2},{1,5},{3,7},{5,1},{7,3},{8,12},{10,14},{12... | collective-permute-start | bytes 1572872 | tf_op jit(solution)/shard_map/ppermute | solution.py:58
  491.1 26.2 %collective-permute-start.41 = (bf16[128,2048]{1,0:T(8,128)(2,1)S(1)}, bf16[128,2048]{1,0:T(8,128)(2,1)S(1)}, u32[]{:S(2)}, u32[]{:S(2)}) collective-permute-start(bf16[128,2048]{1,0:T(8,128)(2,1)S(1)} %get-tuple-element.161), channel_id=1, source_target_pairs={{0,2},{2,4},{4,6},{6,0},{1,3},{3,5},{5,7},{7,1},{8,10},{10,12},{12... | collective-permute-start | bytes 1572872 | tf_op jit(solution)/shard_map/ppermute | solution.py:58
  492.7 25.2 %collective-permute-start.42 = (bf16[128,2048]{1,0:T(8,128)(2,1)S(1)}, bf16[128,2048]{1,0:T(8,128)(2,1)S(1)}, u32[]{:S(2)}, u32[]{:S(2)}) collective-permute-start(bf16[128,2048]{1,0:T(8,128)(2,1)S(1)} %get-tuple-element.161), channel_id=1, source_target_pairs={{0,8},{8,0},{1,9},{9,1},{2,10},{10,2},{3,11},{11,3},{4,12},{12,4},... | collective-permute-start | bytes 1572872 | tf_op jit(solution)/shard_map/ppermute | solution.py:66
  582.2 76.9 %collective-permute-start.46 = (bf16[512,2048]{1,0:T(8,128)(2,1)}, bf16[512,2048]{1,0:T(8,128)(2,1)}, u32[]{:S(2)}, u32[]{:S(2)}) collective-permute-start(bf16[512,2048]{1,0:T(8,128)(2,1)} %convolution_convert_fusion.3), channel_id=1, source_target_pairs={{0,8},{8,0},{1,9},{9,1},{2,10},{10,2},{3,11},{11,3},{4,12},{12,4},... | collective-permute-start | bytes 6291464 | tf_op jit(solution)/shard_map/ppermute | solution.py:66
  588.2 76.4 %all-to-all-start.5 = ((bf16[16,128,576]{1,2,0:T(8,128)(2,1)}), bf16[16,128,576]{1,2,0:T(8,128)(2,1)}, u32[]{:S(2)}, u32[]{:S(2)}) async-start(bf16[16,128,576]{1,2,0:T(8,128)(2,1)} %copy_bitcast_fusion), calls=%async_computation.5 | async-start | bytes 4718592 | tf_op jit(solution)/shard_map/all_to_all | solution.py:351
  592.7 66.3 %collective-permute-start.26 = (bf16[128,2048]{1,0:T(8,128)(2,1)S(1)}, bf16[128,2048]{1,0:T(8,128)(2,1)}, u32[]{:S(2)}, u32[]{:S(2)}) collective-permute-start(bf16[128,2048]{1,0:T(8,128)(2,1)S(1)} %copy-done.26), channel_id=1, source_target_pairs={{0,0},{1,8},{8,1},{9,9},{2,2},{3,10},{10,3},{11,11},{4,4},{5,12},{... | collective-permute-start | bytes 1572872 | tf_op jit(solution)/shard_map/ppermute | solution.py:54
  680.7 33.8 %collective-permute-start.53 = (f32[8,128]{1,0:T(8,128)}, f32[8,128]{1,0:T(8,128)}, u32[]{:S(2)}, u32[]{:S(2)}) collective-permute-start(f32[8,128]{1,0:T(8,128)} %slice_reduce_fusion), channel_id=1, source_target_pairs={{0,0},{1,8},{8,1},{9,9},{2,2},{3,10},{10,3},{11,11},{4,4},{5,12},{... | collective-permute-start | bytes 12296 | tf_op jit(solution)/shard_map/ppermute | solution.py:54
  (101 other events, 1542.9 us)
Sparse Core Ops, SparseCore 0:
  23.4 219.1 all-gather.2
  269.4 98.4 all-gather.4
  413.9 254.2 reduce-scatter.3

commit v2 on v1

--- a/solution.py
+++ b/solution.py
@@ -15,16 +15,18 @@
 FF = 5504
 STEP = 10
 FINE = ("x_lo", "z", "core", "y", "x_hi")
-GROUPS = ("x_lo", "z", "x_hi")
+GROUPS = ("x_hi", "x_lo", "z")
 N_GROUPS = 16
 ROWS = 1024
 CHUNK = 128
+HALF = ROWS // 2
 LOCAL_HEADS = 2
 QK = 2 * LOCAL_HEADS * FEAT
 VW = LOCAL_HEADS * DV
 PW = VW + QK
 FFL = 688
 FFP = 768
+AW = 640
 PHI = 256
 PHI_ROWS = 160
 HEAD_ROWS = 192
@@ -42,10 +44,6 @@
 bf16 = jnp.bfloat16
 
 
-def ring(step):
-    return [(i, (i + step) % 4) for i in range(4)]
-
-
 FLIP = [(0, 1), (1, 0)]
 CROSS = [(0, 0), (1, 2), (2, 1), (3, 3)]
 
@@ -54,35 +52,74 @@
     return lax.ppermute(a, ("core", "x_hi"), CROSS)
 
 
-def from_y(a, step):
-    return lax.ppermute(a, "y", ring(-step))
-
-
-def to_y(a, step):
-    return lax.ppermute(a, "y", ring(step))
-
-
 def swap_core(a):
     return lax.ppermute(a, "core", FLIP)
 
 
+def over_y(a):
+    return lax.all_to_all(a, "y", 0, 0)
+
+
+def spread(mine):
+    return jnp.broadcast_to(mine[None], (4,) + mine.shape)
+
+
+def to_y(a, step):
+    return lax.ppermute(a, "y", [(i, (i + step) % 4) for i in range(4)])
+
+
 def gather_rows(mine):
-    pieces = [mine, from_y(mine, 1), from_y(mine, 2), from_y(mine, 3)]
-    others = [swap_core(piece) for piece in pieces]
-    return jnp.concatenate(pieces + others, axis=0)
-
-
-def scatter_rows(partial_of):
-    send = partial_of(1).astype(bf16)
+    own = over_y(spread(mine)).reshape(HALF, -1)
+    return own, swap_core(own)
+
+
+def gather_rows_apart(mine):
+    y = lax.axis_index("y")
+    own = jnp.zeros((HALF, D), mine.dtype)
+    for step in range(4):
+        piece = to_y(mine, step) if step else mine
+        own = lax.dynamic_update_slice(own, piece, ((y - step) % 4 * CHUNK, 0))
+    return own, swap_core(own)
+
+
+def sum_rows(low):
+    return jnp.sum(over_y(low.reshape(4, CHUNK, D)).astype(f32), axis=0)
+
+
+def sum_rows_apart(low):
+    y = lax.axis_index("y")
+
+    def part(step):
+        return lax.dynamic_slice(low, ((y + step) % 4 * CHUNK, 0), (CHUNK, D))
+
+    parts = [to_y(part(step), step) for step in (1, 2, 3)]
+    out = part(0).astype(f32)
+    for a in parts:
+        out = out + a.astype(f32)
+    return out
+
+
+def scatter_rows(partial, between=None, total=sum_rows):
+    send = partial(1, None)
     got = swap_core(send)
-    kept = partial_of(0)
-    total = kept + got.astype(f32)
-    low = total.astype(bf16)
-    parts = [to_y(low[d * CHUNK : (d + 1) * CHUNK], d) for d in (1, 2, 3)]
-    out = total[:CHUNK]
-    for part in parts:
-        out = out + part.astype(f32)
-    return out
+    low = partial(0, got)
+    if between is not None:
+        between(send, low)
+    return total(low)
+
+
+def rows_of(halves, weight, dims):
+    def partial(half, more):
+        total = matmul(halves[half], weight, dims)
+        if more is not None:
+            total = total + more.astype(f32)
+        return total.astype(bf16)
+
+    return partial
+
+
+def halves_of(a):
+    return a[:HALF], a[HALF:]
 
 
 def matmul(a, b, dims=((1,), (0,))):
@@ -338,6 +375,147 @@
     return (new_one, new_two, master)
 
 
+def nothing_kernel(other_ref, a_ref, out_ref):
+    pass
+
+
+def after(a, other):
+    return pl.pallas_call(
+        nothing_kernel,
+        out_shape=jax.ShapeDtypeStruct(a.shape, a.dtype),
+        in_specs=[pl.BlockSpec(memory_space=pl.ANY)] * 2,
+        out_specs=pl.BlockSpec(memory_space=pl.ANY),
+        input_output_aliases={1: 0},
+    )(other, a)
+
+
+def feature_blocks(forward):
+    order = [(k % 8) * 2 + k // 8 for k in range(N_GROUPS)]
+    return order if forward else [order.index(k) for k in range(N_GROUPS)]
+
+
+def reorder_kernel(blocks, *refs):
+    n = len(refs) // 2
+    for src, dst in zip(refs[:n], refs[n:]):
+        for to, of in enumerate(blocks):
+            dst[:, to * CHUNK : (to + 1) * CHUNK] = src[:, of * CHUNK : (of + 1) * CHUNK].astype(dst.dtype)
+
+
+def reorder(blocks, arrays, dtype):
+    return pl.pallas_call(
+        functools.partial(reorder_kernel, blocks),
+        out_shape=[jax.ShapeDtypeStruct(a.shape, dtype) for a in arrays],
+    )(*arrays)
+
+
+def to_group_order(*arrays):
+    return reorder(feature_blocks(True), arrays, bf16)
+
+
+def from_group_order(rows, dtype):
+    return reorder(feature_blocks(False), (rows,), dtype)[0]
+
+
+def pack_first_kernel(value_ref, feature_ref, output_ref, gain_row_ref, gain_col_ref, out_ref):
+    def low(a):
+        return a.astype(bf16).astype(f32)
+
+    out_ref[:, :VW] = low(output_ref[...]).T.astype(bf16)
+    out_ref[:, VW : 2 * VW] = (low(value_ref[...]) * gain_col_ref[:, 0:1]).astype(bf16)
+    out_ref[:, 2 * VW : VW + PW] = (low(feature_ref[...]) * gain_row_ref[0:1]).T.astype(bf16)
+    out_ref[:, VW + PW :] = jnp.zeros((CHUNK, AW - VW - PW), bf16)
+
+
+def pack_mlp_kernel(gateup_ref, down_ref, gain_row_ref, out_ref):
+    def low(a):
+        return a.astype(bf16).astype(f32)
+
+    def wide(a):
+        return jnp.concatenate([a, jnp.zeros((FFP - FFL, CHUNK), f32)], axis=0).T.astype(bf16)
+
+    out_ref[:, :FFP] = wide(low(gateup_ref[0]) * gain_row_ref[1:2])
+    out_ref[:, FFP : 2 * FFP] = wide(low(gateup_ref[1]) * gain_row_ref[1:2])
+    out_ref[:, 2 * FFP :] = wide(low(down_ref[...]))
+
+
+def adam_store(weight, first, second, grad, rate, outs, at=()):
+    place = at if at else (slice(None), slice(None))
+    for ref, new in zip(outs, adam_step(weight[place], first[place], second[place], grad, rate)):
+        ref[place] = new
+
+
+def adam_mlp_kernel(
+    grad_ref, gain_row_ref, gw, gf, gs, dw, df, ds, g1, g2, g3, d1, d2, d3
+):
+    for part in range(2):
+        grad = grad_ref[:, part * FFP : (part + 1) * FFP].astype(f32).T[:FFL]
+        adam_store(
+            gw, gf, gs, grad * gain_row_ref[1:2], D ** (-0.5), (g1, g2, g3),
+            (part, slice(None), slice(None)),
+        )
+    grad = grad_ref[:, 2 * FFP :].astype(f32).T[:FFL]
+    adam_store(dw, df, ds, grad, FF ** (-0.5), (d1, d2, d3))
+
+
+def adam_attn_kernel(
+    grad_ref, gain_row_ref, gain_col_ref,
+    fw, ff, fs, vw, vf, vs, ow, of, os, f1, f2, f3, v1, v2, v3, o1, o2, o3,
+):
+    grad = grad_ref[:, VW : 2 * VW].astype(f32) * gain_col_ref[:, 0:1]
+    adam_store(vw, vf, vs, grad, D ** (-0.5), (v1, v2, v3))
+    grad = grad_ref[:, 2 * VW : VW + PW].astype(f32).T * gain_row_ref[0:1]
+    adam_store(fw, ff, fs, grad, D ** (-0.5), (f1, f2, f3))
+    grad = grad_ref[:, :VW].astype(f32).T
+    adam_store(ow, of, os, grad, (HEADS * DV // 64) ** (-0.5), (o1, o2, o3))
+
+
+def grad_tile(left, right):
+    return sum(matmul(a[...], b, ((0,), (0,))) for a, b in zip(left, right)).astype(bf16)
+
+
+def mlp_grads_kernel(other_ref, a0, a1, g0, g1, gu0, gu1, h0, h1, out_ref):
+    out_ref[:, : 2 * FFP] = grad_tile((a0, a1), (gu0[...], gu1[...]))
+    out_ref[:, 2 * FFP :] = grad_tile((g0, g1), (h0[...], h1[...]))
+
+
+def attn_grads_kernel(other_ref, a0, a1, g0, g1, proj_ref, rows_ref, out_ref):
+    one = grad_tile((g0, g1), (rows_ref[:HALF], rows_ref[HALF:]))
+    two = grad_tile((a0, a1), (proj_ref[:HALF], proj_ref[HALF:]))
+    for k in range(2):
+        part = slice(k * CHUNK, (k + 1) * CHUNK)
+        out_ref[k, :, :VW] = one[part]
+        out_ref[k, :, VW : VW + PW] = two[part]
+        out_ref[k, :, VW + PW :] = jnp.zeros((CHUNK, AW - VW - PW), bf16)
+
+
+def grads(kernel, out_shape, out_block, other, tiled, whole):
+    def full(a):
+        return pl.BlockSpec(a.shape, lambda i: (0, 0))
+
+    return pl.pallas_call(
+        kernel,
+        grid=(D // TILE,),
+        out_shape=jax.ShapeDtypeStruct(out_shape, bf16),
+        in_specs=[pl.BlockSpec(memory_space=pl.ANY)]
+        + [pl.BlockSpec((HALF, TILE), lambda i: (0, i))] * len(tiled)
+        + [full(a) for a in whole],
+        out_specs=pl.BlockSpec(out_block, lambda i: (i,) + (0,) * (len(out_block) - 1)),
+        compiler_params=pltpu.CompilerParams(vmem_limit_bytes=48 * 1024 * 1024),
+    )(other, *tiled, *whole)
+
+
+def plain(kernel, outs, *args):
+    return pl.pallas_call(
+        kernel,
+        out_shape=outs,
+        compiler_params=pltpu.CompilerParams(vmem_limit_bytes=48 * 1024 * 1024),
+    )(*args)
+
+
+def same(*arrays):
+    return [jax.ShapeDtypeStruct(a.shape, f32) for a in arrays]
+
+
 def unit_norm(rows):
     inv = lax.rsqrt(jnp.mean(rows * rows, axis=-1, keepdims=True) + norm_eps)
     return rows * inv, inv
@@ -349,10 +527,6 @@
 
 def exchange(a):
     return lax.all_to_all(a, GROUPS, 0, 0)
-
-
-def pad_cols(a, width):
-    return jnp.pad(a, ((0, 0), (0, width - a.shape[1])))
 
 
 def shards(
@@ -364,42 +538,42 @@
     down_weight, down_first, down_second,
 ):
     core = lax.axis_index("core")
-    y = lax.axis_index("y")
     group = (lax.axis_index("x_lo") * 4 + lax.axis_index("z")) * 2 + lax.axis_index("x_hi")
     gain_low = gains.astype(bf16).astype(f32)
 
-    value_low = value_weight.astype(bf16)
-    feature_low = feature_weight.reshape(128, QK).astype(bf16)
-    gate_low = gateup_weight[:, 0].astype(bf16)
-    up_low = gateup_weight[:, 1].astype(bf16)
-    scale_one = gain_low[0][:, None]
-    scale_two = gain_low[1][:, None]
-    first_part = (jnp.concatenate([value_low, feature_low], axis=1).astype(f32) * scale_one).astype(bf16)
-    second_part = jnp.concatenate(
-        [
-            output_weight.astype(bf16).T,
-            pad_cols((gate_low.astype(f32) * scale_two).astype(bf16), FFP),
-            pad_cols((up_low.astype(f32) * scale_two).astype(bf16), FFP),
-        ],
-        axis=1,
-    )
-    third_part = pad_cols(down_weight.astype(bf16).T, FFP)
-
+    gain_col = gain_low.T
+    flat = [jnp.transpose(a, (1, 2, 0)) for a in (gateup_weight, gateup_first, gateup_second)]
+    thin = [
+        jnp.transpose(a, (1, 2, 0)).reshape(QK, CHUNK)
+        for a in (feature_weight, feature_first, feature_second)
+    ]
+    first_part = plain(
+        pack_first_kernel,
+        jax.ShapeDtypeStruct((CHUNK, AW), bf16),
+        value_weight, thin[0], output_weight, gain_low, gain_col,
+    )
+    gateup_part = plain(
+        pack_mlp_kernel,
+        jax.ShapeDtypeStruct((CHUNK, 3 * FFP), bf16),
+        flat[0], down_weight, gain_low,
+    )
+    tokens, cot = to_group_order(tokens, cotangent)
+
+    first_part = cross(first_part)
     tokens = cross(tokens)
-    first_part = cross(first_part)
-    second_part = cross(second_part)
-    third_part = cross(third_part)
-    cot = cross(cotangent)
-
     inputs = tokens.astype(f32)
     unit_one, inv_one = unit_norm(inputs)
     acts_one = gather_rows(unit_one.astype(bf16))
-    proj_w = exchange(jnp.broadcast_to(first_part[None], (N_GROUPS, CHUNK, PW))).reshape(D, PW)
-    wide_w = lax.all_gather(second_part, GROUPS, axis=0, tiled=True)
-    down_w = lax.all_gather(third_part, GROUPS, axis=0, tiled=True)
-    out_w = wide_w[:, :VW]
-    gateup_w = wide_w[:, VW:]
-    grad_mlp = gather_rows(cot)
+    attn_w = lax.all_gather(first_part, GROUPS, axis=0, tiled=True)
+    out_w = attn_w[:, :VW]
+    proj_w = attn_w[:, VW : VW + PW]
+    gateup_part = cross(after(gateup_part, acts_one[0]))
+    mlp_w = lax.all_gather(gateup_part, GROUPS, axis=0, tiled=True)
+    gateup_w = mlp_w[:, : 2 * FFP]
+    down_w = mlp_w[:, 2 * FFP :]
+    proj = jnp.concatenate([matmul(a, proj_w).astype(bf16) for a in acts_one])
+    cot = cross(after(cot, gateup_part))
+    grad_mlp = gather_rows_apart(after(cot, proj))
 
     ends = jnp.cumsum(row_lengths)
 
@@ -408,7 +582,8 @@
 
     positions = group * ROWS + jnp.arange(ROWS, dtype=jnp.int32)
     docs = doc_of(positions)
-    group_ids = jnp.arange(N_GROUPS, dtype=jnp.int32)
+    places = jnp.arange(N_GROUPS, dtype=jnp.int32)
+    group_ids = (places % 8) * 2 + places // 8
     doc_end = doc_of(group_ids * ROWS + (ROWS - 1))
     doc_before = jnp.where(group_ids > 0, doc_of(group_ids * ROWS - 1), -1)
     last_doc = docs[ROWS - 1]
@@ -425,10 +600,9 @@
     carry = ((group_ids[None, :] < group_ids[:, None]) & (doc_end[None, :] == doc_before[:, None])).astype(f32)
     back = ((group_ids[None, :] > group_ids[:, None]) & (doc_before[None, :] == doc_end[:, None])).astype(f32)
     chunk_ids = jnp.arange(8, dtype=jnp.int32)
-    idx = ((chunk_ids % 2) ^ core) * 4 + (chunk_ids // 2 - y) % 4
+    idx = ((chunk_ids % 2) ^ core) * 4 + chunk_ids // 2
 
     left, right, rows, move = feature_tables()
-    proj = matmul(acts_one, proj_w).astype(bf16)
     own_state = call(
         key_state_kernel,
         [jax.ShapeDtypeStruct((STATE_ROWS, DV), f32)],
@@ -448,40 +622,47 @@
         [pltpu.VMEM((ROWS, PW), bf16)],
         9,
     )(idx, proj, masks, doc_row, state, left, right, rows, move)
-    half = ROWS // 2
-
-    def of_half(a, h):
-        return a[h * half : (h + 1) * half]
 
     middle = inputs + scatter_rows(
-        lambda h: matmul(of_half(attn_rows, h), out_w, ((1,), (1,)))
+        rows_of(halves_of(after(attn_rows, grad_mlp[1])), out_w, ((1,), (1,)))
     )
     unit_two, inv_two = unit_norm(middle)
     acts_two = gather_rows(unit_two.astype(bf16))
-    gate_up = matmul(acts_two, gateup_w)
-    grad_hidden = matmul(grad_mlp, down_w)
-    gate = gate_up[:, :FFP]
-    up = gate_up[:, FFP:]
-    sigmoid = jax.nn.sigmoid(gate)
-    silu = gate * sigmoid
-    hidden = (silu * up).astype(bf16)
-    dsilu = sigmoid * (1.0 + gate * (1.0 - sigmoid))
-    grad_gate_up = jnp.concatenate([grad_hidden * up * dsilu, grad_hidden * silu], axis=1).astype(bf16)
-
-    shaped_two = scatter_rows(lambda h: matmul(of_half(grad_gate_up, h), gateup_w, ((1,), (1,))))
+    hidden = []
+    grad_gate_up = []
+    for acts, grad in zip(acts_two, grad_mlp):
+        gate_up = matmul(acts, gateup_w)
+        grad_hidden = matmul(grad, down_w)
+        gate = gate_up[:, :FFP]
+        up = gate_up[:, FFP:]
+        sigmoid = jax.nn.sigmoid(gate)
+        silu = gate * sigmoid
+        hidden.append((silu * up).astype(bf16))
+        dsilu = sigmoid * (1.0 + gate * (1.0 - sigmoid))
+        grad_gate_up.append(
+            jnp.concatenate([grad_hidden * up * dsilu, grad_hidden * silu], axis=1).astype(bf16)
+        )
+
+    late = []
+
+    def mlp_grads(send, low):
+        mlp_grad = grads(
+            mlp_grads_kernel, (D, 3 * FFP), (TILE, 3 * FFP), low,
+            acts_two + grad_mlp, (*grad_gate_up, *hidden),
+        )
+        late.append(mlp_grad)
+
+    shaped_two = scatter_rows(rows_of(grad_gate_up, gateup_w, ((1,), (1,))), mlp_grads)
+    mlp_grad = lax.psum_scatter(after(late[0], shaped_two), GROUPS, scatter_dimension=0, tiled=True)
     grad_out = cot.astype(f32)
     grad_mid = grad_out + unit_norm_back(shaped_two, unit_two, inv_two)
     grad_attn = gather_rows(grad_mid.astype(bf16))
 
-    gateup_grad = matmul(acts_two, grad_gate_up, ((0,), (0,))).astype(bf16)
-    down_grad = matmul(grad_mlp, hidden, ((0,), (0,))).astype(bf16)
-    mlp_grad = lax.psum_scatter(
-        jnp.concatenate([gateup_grad, down_grad], axis=1), GROUPS, scatter_dimension=0, tiled=True
-    )
-    mixed = middle + scatter_rows(lambda h: matmul(of_half(hidden, h), down_w, ((1,), (1,))))
-    mixed = cross(mixed.astype(bf16))
-
-    grad_low = matmul(grad_attn, out_w).astype(bf16)
+    last_hidden = [after(a, grad_attn[1]) for a in hidden]
+    mixed = middle + scatter_rows(rows_of(last_hidden, down_w, ((1,), (1,))), total=sum_rows_apart)
+    mixed = mixed.astype(bf16)
+
+    grad_low = jnp.concatenate([matmul(a, out_w).astype(bf16) for a in grad_attn])
     own_grad, gn, gd = call(
         query_state_kernel,
         [
@@ -510,53 +691,47 @@
         [jax.ShapeDtypeStruct((ROWS, PW), bf16)],
         [pltpu.VMEM((ROWS, PW), bf16), pltpu.VMEM((ROWS, QK), f32), pltpu.VMEM((ROWS, VW), f32)],
         12,
-    )(idx, proj, gn, gd, masks, doc_row, state, grad_state, left, right, rows, move)[0]
-
-    shaped_one = scatter_rows(lambda h: matmul(of_half(grad_proj, h), proj_w, ((1,), (1,))))
+    )(idx, proj, gn, after(gd, mixed), masks, doc_row, state, grad_state, left, right, rows, move)[0]
+
+    def proj_grads(send, low):
+        attn_grad = grads(
+            attn_grads_kernel, (N_GROUPS, CHUNK, AW), (2, CHUNK, AW), send,
+            acts_one + grad_attn, (grad_proj, attn_rows),
+        )
+        late.append(exchange(attn_grad))
+
+    mixed = from_group_order(cross(mixed), bf16)
+    shaped_one = scatter_rows(rows_of(halves_of(grad_proj), proj_w, ((1,), (1,))), proj_grads, sum_rows_apart)
     grad_tokens = grad_mid + unit_norm_back(shaped_one, unit_one, inv_one)
-    grad_tokens = cross(grad_tokens.astype(bf16)).astype(f32)
-
-    output_grad = matmul(grad_attn, attn_rows, ((0,), (0,))).astype(bf16)
-    proj_grad = matmul(acts_one, grad_proj, ((0,), (0,))).astype(bf16)
-    attn_grad = exchange(
-        jnp.concatenate([output_grad, proj_grad], axis=1).reshape(N_GROUPS, CHUNK, VW + PW)
-    )
-    attn_grad = cross(jnp.sum(attn_grad.astype(f32), axis=0).astype(bf16)).astype(f32)
-    mlp_grad = cross(mlp_grad).astype(f32)
-    den_group = cross(den_group)
-
-    output_sum = attn_grad[:, :VW].T
-    unit_value = attn_grad[:, VW : 2 * VW]
-    unit_feature = attn_grad[:, 2 * VW :]
-    unit_gate = mlp_grad[:, :FFL]
-    unit_up = mlp_grad[:, FFP : FFP + FFL]
-    down_sum = mlp_grad[:, 2 * FFP : 2 * FFP + FFL].T
-    gain_one = jnp.sum(unit_value * value_low.astype(f32), axis=1) + jnp.sum(
-        unit_feature * feature_low.astype(f32), axis=1
-    )
-    gain_two = jnp.sum(unit_gate * gate_low.astype(f32), axis=1) + jnp.sum(
-        unit_up * up_low.astype(f32), axis=1
+    grad_tokens = from_group_order(cross(grad_tokens.astype(bf16)), f32)
+    attn_grad = jnp.sum(late[1].astype(f32), axis=0)
+    gain_one = jnp.sum((attn_grad * first_part.astype(f32))[:, VW:], axis=1)
+    gain_two = jnp.sum(
+        (mlp_grad.astype(f32) * gateup_part.astype(f32))[:, : 2 * FFP], axis=1
     )
     small = jnp.concatenate([gain_one[None], gain_two[None], den_group[:6]], axis=0)
     small = jnp.sum(
-        lax.all_to_all(jnp.broadcast_to(small[None], (8, 8, CHUNK)), ("y", "x_hi"), 0, 0), axis=0
-    )
-    gain_total = small[:2]
+        lax.all_to_all(jnp.broadcast_to(small[None], (8, 8, CHUNK)), ("y", "core"), 0, 0), axis=0
+    )
+    small = cross(small)
+    attn_grad = cross(attn_grad.astype(bf16))
+    mlp_grad = cross(mlp_grad)
+
+    gain_total = small[:2] / gain_low
     den_mean = small[2, 0] / (N_GROUPS * ROWS * HEADS)
-    value_sum = unit_value * scale_one
-    feature_sum = (unit_feature * scale_one).reshape(CHUNK, 2, QK // 2)
-    gateup_sum = jnp.stack([unit_gate * scale_two, unit_up * scale_two], axis=1)
-    news = [
-        adam_step(gains, gain_first, gain_second, gain_total, gain_rate),
-        adam_step(feature_weight, feature_first, feature_second, feature_sum, D ** (-0.5)),
-        adam_step(value_weight, value_first, value_second, value_sum, D ** (-0.5)),
-        adam_step(
-            output_weight, output_first, output_second, output_sum, (HEADS * DV // 64) ** (-0.5)
-        ),
-        adam_step(gateup_weight, gateup_first, gateup_second, gateup_sum, D ** (-0.5)),
-        adam_step(down_weight, down_first, down_second, down_sum, FF ** (-0.5)),
-    ]
-    return (mixed, grad_tokens, den_mean) + tuple(a for new in news for a in new)
+    deep = plain(
+        adam_mlp_kernel,
+        same(*flat, down_weight, down_first, down_second),
+        mlp_grad, gain_low, *flat, down_weight, down_first, down_second,
+    )
+    near = (*thin, value_weight, value_first, value_second, output_weight, output_first, output_second)
+    near = plain(adam_attn_kernel, same(*near), attn_grad, gain_low, gain_col, *near)
+    news = list(adam_step(gains, gain_first, gain_second, gain_total, gain_rate))
+    news += [jnp.transpose(a.reshape(2, QK // 2, CHUNK), (2, 0, 1)) for a in near[:3]]
+    news += near[3:]
+    news += [jnp.transpose(a, (2, 0, 1)) for a in deep[:3]]
+    news += deep[3:]
+    return (mixed, grad_tokens, den_mean) + tuple(news)
 
 
 def solution(mesh):

time: 749 us -> 540 us (0.72)
  waiting for transfers between devices: 298 us -> 103 us
  starting transfers between devices: 167 us -> 91.9 us
  blocking collectives: 57.5 us -> 115 us
  Pallas kernels: 28.6 us -> 61.8 us
  other arithmetic: 47.4 us -> 30.9 us
  matrix products: 73.7 us -> 59 us
    all_to_all x0 -> x4, blocking collectives: none -> 90.9 us  [the longest x3 84.1 us: over_y(): return lax.all_to_all(a, 'y', 0, 0)]
    ppermute x24 -> x9, waiting for transfers between devices: 106 us -> 28.1 us  [to_y(): return lax.ppermute(a, 'y', [(i, (i + step) % 4) for i in range(4)])]
    all_gather x2, waiting for transfers between devices: 70 us -> 0.01 us  [the longest x1 0.01 us: shards(): attn_w = lax.all_gather(first_part, GROUPS, axis=0, tiled=True)]
    ppermute x10 -> x9, waiting for transfers between devices: 86.9 us -> 28.3 us  [cross(): return lax.ppermute(a, ('core', 'x_hi'), CROSS)]
    all_to_all x4 -> x3, starting transfers between devices: 60.6 us -> 16.8 us  [exchange(): return lax.all_to_all(a, GROUPS, 0, 0)]
    all_to_all x2, blocking collectives: 57.5 us -> 23.9 us  [exchange(): return lax.all_to_all(a, GROUPS, 0, 0)]
    pallas_call x0 -> x17, Pallas kernels: none -> 33.5 us  [the longest x2 23.3 us: grads(): pl.pallas_call(kernel, grid=(D // TILE,), out_shape=jax.ShapeDtypeStruct(...]
    ppermute x24 -> x9, starting transfers between devices: 39.2 us -> 10.7 us  [to_y(): return lax.ppermute(a, 'y', [(i, (i + step) % 4) for i in range(4)])]
  transfers between devices with their start and end apart: 62 -> 34, of which waited for: 26 -> 15; matrix products, arithmetic and copies ran while one was open for 14% -> 16% of each run, Pallas kernels for 4% -> 11%
where the time goes in v2:
time: 540 us; the launch traced here: 530 us
  blocking collectives  115 us (21%)
  waiting for transfers between devices  103 us (19%)
  starting transfers between devices  91.9 us (17%)
  Pallas kernels  61.8 us (11%)
  matrix products  59 us (11%)
  local copies, waits for them, and re-layouts  50.7 us (9%)
  other arithmetic  30.9 us (6%)
  between operations  17.9 us (3%)
    all_to_all x3, blocking collectives, over_y(): return lax.all_to_all(a, 'y', 0, 0)  84.1 us
    dot_general x16, matrix products, matmul(): return lax.dot_general(a, b, (dims, ((), ())), preferred_element_type=f32)  59 us
    ppermute x9, starting transfers between devices, cross(): return lax.ppermute(a, ('core', 'x_hi'), CROSS)  44.5 us
    unnamed x208, local copies, waits for them, and re-layouts  36.8 us
    ppermute x9, waiting for transfers between devices, cross(): return lax.ppermute(a, ('core', 'x_hi'), CROSS)  28.3 us
    ppermute x9, waiting for transfers between devices, to_y(): return lax.ppermute(a, 'y', [(i, (i + step) % 4) for i in range(4)])  28.1 us
    all_to_all x2, blocking collectives, exchange(): return lax.all_to_all(a, GROUPS, 0, 0)  23.9 us
    pallas_call x2, Pallas kernels, grads(): pl.pallas_call(kernel, grid=(D // TILE,), out_shape=jax.ShapeDtypeStruct(...  23.3 us
  transfers between devices with their start and end apart: 34, of which 15 were waited for; matrix products, arithmetic and copies ran while one was open for 16% of the time, Pallas kernels for 11%

profile of v2, /device:TPU:1, one launch (start us, length us, event | category | flops | bytes accessed | tf_op | source)
XLA Modules:
  0.0 529.6 jit_solution(17461035143093966436)
XLA Ops:
  10.8 6.0 %collective-permute-start.1 = (bf16[128,640]{1,0:T(8,128)(2,1)S(1)}, bf16[128,640]{1,0:T(8,128)(2,1)S(1)}, u32[]{:S(2)}, u32[]{:S(2)}) collective-permute-start(bf16[128,640]{1,0:T(8,128)(2,1)S(1)} %shard_map.401), channel_id=1, source_target_pairs={{0,0},{1,8},{8,1},{9,9},{2,2},{3,10},{10,3},{11,11},{4,4},{5,12},{... | collective-permute-start | bytes 491528 | tf_op jit(solution)/shard_map/ppermute | solution.py:52
  28.0 7.4 %collective-permute-done = bf16[128,2048]{1,0:T(8,128)(2,1)S(1)} collective-permute-done((bf16[128,2048]{1,0:T(8,128)(2,1)}, bf16[128,2048]{1,0:T(8,128)(2,1)S(1)}, u32[]{:S(2)}, u32[]{:S(2)}) %collective-permute-start) | collective-permute-done | bytes 524320 | tf_op jit(solution)/shard_map/ppermute | solution.py:52
  42.7 14.3 %all-to-all-done = bf16[4,128,2048]{2,1,0:T(8,128)(2,1)S(1)} async-done(((bf16[4,128,2048]{2,1,0:T(8,128)(2,1)}), bf16[4,128,2048]{2,1,0:T(8,128)(2,1)S(1)}, u32[]{:S(2)}, u32[]{:S(2)}) %all-to-all-start) | async-done | bytes 2097184 | tf_op jit(solution)/shard_map/all_to_all | solution.py:60
  58.3 7.2 %collective-permute-start.3 = (bf16[128,2304]{1,0:T(8,128)(2,1)}, bf16[128,2304]{1,0:T(8,128)(2,1)S(1)}, u32[]{:S(2)}, u32[]{:S(2)}) collective-permute-start(bf16[128,2304]{1,0:T(8,128)(2,1)} %shard_map.403), channel_id=1, source_target_pairs={{0,0},{1,8},{8,1},{9,9},{2,2},{3,10},{10,3},{11,11},{4,4},{5,12},{... | collective-permute-start | bytes 1769480 | tf_op jit(solution)/shard_map/ppermute | solution.py:52
  65.5 9.9 %collective-permute-done.3.other_ref = bf16[128,2304]{1,0:T(8,128)(2,1)S(1)} collective-permute-done((bf16[128,2304]{1,0:T(8,128)(2,1)}, bf16[128,2304]{1,0:T(8,128)(2,1)S(1)}, u32[]{:S(2)}, u32[]{:S(2)}) %collective-permute-start.3) | collective-permute-done | bytes 589856 | tf_op jit(solution)/shard_map/ppermute | solution.py:52
  80.7 8.0 %collective-permute-done.4 = bf16[128,2048]{1,0:T(8,128)(2,1)S(1)} collective-permute-done((bf16[128,2048]{1,0:T(8,128)(2,1)}, bf16[128,2048]{1,0:T(8,128)(2,1)S(1)}, u32[]{:S(2)}, u32[]{:S(2)}) %collective-permute-start.4) | collective-permute-done | bytes 524320 | tf_op jit(solution)/shard_map/ppermute | solution.py:52
  104.4 5.5 %collective-permute-done.5 = bf16[128,2048]{1,0:T(8,128)(2,1)} collective-permute-done((bf16[128,2048]{1,0:T(8,128)(2,1)}, bf16[128,2048]{1,0:T(8,128)(2,1)}, u32[]{:S(2)}, u32[]{:S(2)}) %collective-permute-start.5) | collective-permute-done | bytes 524320 | tf_op jit(solution)/shard_map/ppermute | solution.py:68
  129.4 6.8 %all-to-all-start.1 = ((f32[16,24,128]{2,1,0:T(8,128)}), f32[16,24,128]{2,1,0:T(8,128)}, u32[]{:S(2)}, u32[]{:S(2)}) async-start(f32[16,24,128]{2,1,0:T(8,128)} %bitcast.65), calls=%async_computation.1 | async-start | bytes 393216 | tf_op jit(solution)/shard_map/all_to_all | solution.py:529
  137.7 7.9 %all-to-all-done.1 = f32[16,24,128]{2,1,0:T(8,128)} async-done(((f32[16,24,128]{2,1,0:T(8,128)}), f32[16,24,128]{2,1,0:T(8,128)}, u32[]{:S(2)}, u32[]{:S(2)}) %all-to-all-start.1) | async-done | bytes 196640 | tf_op jit(solution)/shard_map/all_to_all | solution.py:529
  146.9 11.1 %all_to_all.55 = f32[16,24,128]{2,1,0:T(8,128)S(1)} all-to-all(f32[16,24,128]{2,1,0:T(8,128)S(1)} %multiply_reduce_fusion.1), channel_id=1, replica_groups=mesh['x_lo'=2,'z'=4,'core'=2,'y'=4,'x_hi'=2] {'x_hi','x_lo','z'}, dimensions={0} | all-to-all | bytes 393216 | tf_op jit(solution)/shard_map/all_to_all | solution.py:529
  160.5 6.0 %shard_map.407 = (f32[1024,256]{1,0:T(8,128)S(1)}, f32[1024,2]{1,0:T(8,128)S(1)}, bf16[1024,256]{1,0:T(8,128)(2,1)S(1)}) custom-call(s32[8]{0:T(128)S(1)} %copy-done.55, bf16[1024,320]{1,0:T(8,128)(2,1)S(1)} %copy-done, f32[1024,3]{1,0:T(8,128)S(1)} %copy.85.masks_ref, f32[1,1024]{1,0:T(1,128)S(1)} %bitcast.72, f32[384,128]{1,0:T(8,128)S(1)} %bitcast.63, ...), custom_call_target="tpu_custom_call" | custom-call | tf_op jit(solution)/shard_map/pallas_call | solution.py:615
  179.8 28.6 %all_to_all.56 = bf16[4,128,2048]{2,1,0:T(8,128)(2,1)S(1)} all-to-all(bf16[4,128,2048]{2,1,0:T(8,128)(2,1)S(1)} %bitcast.83), channel_id=1, replica_groups=mesh['x_lo'=2,'z'=4,'core'=2,'y'=4,'x_hi'=2] {'y'}, dimensions={0} | all-to-all | bytes 4194304 | tf_op jit(solution)/shard_map/all_to_all | solution.py:60
  210.7 27.6 %all_to_all.57 = bf16[4,128,2048]{2,1,0:T(8,128)(2,1)S(1)} all-to-all(bf16[4,128,2048]{2,1,0:T(8,128)(2,1)S(1)} %broadcast_in_dim.18), channel_id=1, replica_groups=mesh['x_lo'=2,'z'=4,'core'=2,'y'=4,'x_hi'=2] {'y'}, dimensions={0} | all-to-all | bytes 4194304 | tf_op jit(solution)/shard_map/all_to_all | solution.py:60
  246.1 6.3 %fusion.2 = f32[512,1536]{1,0:T(8,128)S(1)} fusion(bf16[512,2048]{1,0:T(8,128)(2,1)} %collective-permute-done.10.a1, bf16[2048,2304]{1,0:T(8,128)(2,1)} %all-gather.5.cloned.1.call-done), kind=kOutput, calls=%fused_computation.9 | convolution fusion | flops 3221225472 | bytes 11534336 | tf_op jit(solution)/shard_map/dot_general | solution.py:126
  281.9 14.4 %shard_map.417.a_ref = bf16[2048,2304]{1,0:T(8,128)(2,1)} custom-call(bf16[512,2048]{1,0:T(8,128)(2,1)} %add_convert_fusion.2.other_ref, bf16[512,2048]{1,0:T(8,128)(2,1)} %bitcast.80, bf16[512,2048]{1,0:T(8,128)(2,1)} %collective-permute-done.10.a1, bf16[512,2048]{1,0:T(8,128)(2,1)} %constant_dynamic-update-slice_fusion.g0, ...), custom_call_target="tpu_custom_call" | custom-call | tf_op jit(solution)/shard_map/pallas_call | solution.py:495
  296.3 8.6 %all-to-all-done.5 = bf16[4,128,2048]{2,1,0:T(8,128)(2,1)} async-done(((bf16[4,128,2048]{2,1,0:T(8,128)(2,1)}), bf16[4,128,2048]{2,1,0:T(8,128)(2,1)}, u32[]{:S(2)}, u32[]{:S(2)}) %all-to-all-start.5) | async-done | bytes 2097184 | tf_op jit(solution)/shard_map/all_to_all | solution.py:60
  312.4 27.9 %all_to_all.58 = bf16[4,128,2048]{2,1,0:T(8,128)(2,1)S(1)} all-to-all(bf16[4,128,2048]{2,1,0:T(8,128)(2,1)S(1)} %broadcast_in_dim.19), channel_id=1, replica_groups=mesh['x_lo'=2,'z'=4,'core'=2,'y'=4,'x_hi'=2] {'y'}, dimensions={0} | all-to-all | bytes 4194304 | tf_op jit(solution)/shard_map/all_to_all | solution.py:60
  347.4 5.5 %convolution_convert_fusion.2 = bf16[512,2048]{1,0:T(8,128)(2,1)} fusion(bf16[512,768]{1,0:T(8,128)(2,1)} %shard_map.410, bf16[2048,2304]{1,0:T(8,128)(2,1)} %all-gather.5.cloned.1.call-done), kind=kOutput, calls=%fused_computation.20 | convolution fusion | flops 1611661312 | bytes 6029312 | tf_op jit(solution)/shard_map/dot_general | solution.py:126
  375.1 12.8 %all_to_all.59 = f32[16,32,128]{2,1,0:T(8,128)S(1)} all-to-all(f32[16,32,128]{2,1,0:T(8,128)S(1)} %concatenate.24), channel_id=1, replica_groups=mesh['x_lo'=2,'z'=4,'core'=2,'y'=4,'x_hi'=2] {'x_hi','x_lo','z'}, dimensions={0} | all-to-all | bytes 524288 | tf_op jit(solution)/shard_map/all_to_all | solution.py:529
  407.6 15.2 %shard_map.414.proj_ref = bf16[1024,320]{1,0:T(8,128)(2,1)S(1)} custom-call(s32[8]{0:T(128)S(1)} %copy-done.57, bf16[1024,320]{1,0:T(8,128)(2,1)S(1)} %copy-done, f32[1024,256]{1,0:T(8,128)S(1)} %copy-done.29, f32[1024,2]{1,0:T(8,128)S(1)} %copy-done.21, f32[1024,3]{1,0:T(8,128)S(1)} %copy.85.masks_ref, f32[1,1024]{1,0:T(1,128)S(1)} %bitcast.73, ...), custom_call_target="tpu_custom_call" | custom-call | tf_op jit(solution)/shard_map/pallas_call | solution.py:689
  428.7 8.9 %shard_map.416 = bf16[16,128,640]{2,1,0:T(8,128)(2,1)} custom-call(bf16[512,2048]{1,0:T(8,128)(2,1)} %convolution_convert_fusion.1.other_ref, bf16[512,2048]{1,0:T(8,128)(2,1)S(1)} %bitcast.60, bf16[512,2048]{1,0:T(8,128)(2,1)} %collective-permute-done.2.a1, bf16[512,2048]{1,0:T(8,128)(2,1)} %bitcast.78, ...), custom_call_target="tpu_custom_call" | custom-call | tf_op jit(solution)/shard_map/pallas_call | solution.py:495
  450.5 5.7 %collective-permute-start.17 = (bf16[128,2048]{1,0:T(8,128)(2,1)}, bf16[128,2048]{1,0:T(8,128)(2,1)}, u32[]{:S(2)}, u32[]{:S(2)}) collective-permute-start(bf16[128,2048]{1,0:T(8,128)(2,1)} %add_convert_fusion.4.other_ref), channel_id=1, source_target_pairs={{0,0},{1,8},{8,1},{9,9},{2,2},{3,10},{10,3},{11,11},{4,4},{5,12},{... | collective-permute-start | bytes 1572872 | tf_op jit(solution)/shard_map/ppermute | solution.py:52
  456.2 14.8 %collective-permute-done.21 = bf16[128,2048]{1,0:T(8,128)(2,1)S(1)} collective-permute-done((bf16[128,2048]{1,0:T(8,128)(2,1)S(1)}, bf16[128,2048]{1,0:T(8,128)(2,1)S(1)}, u32[]{:S(2)}, u32[]{:S(2)}) %collective-permute-start.21) | collective-permute-done | bytes 524320 | tf_op jit(solution)/shard_map/ppermute | solution.py:68
  493.4 6.8 %all_to_all.60 = f32[8,8,128]{2,1,0:T(8,128)S(1)} all-to-all(f32[8,8,128]{2,1,0:T(8,128)S(1)} %broadcast_in_dim.22), channel_id=1, replica_groups=mesh['x_lo'=2,'z'=4,'core'=2,'y'=4,'x_hi'=2] {'y','core'}, dimensions={0} | all-to-all | bytes 65536 | tf_op jit(solution)/shard_map/all_to_all | solution.py:714
  (361 shorter events, 238.4 us)
Async XLA Ops:
  7.2 83.0 %all-gather.3.cloned.1.call-start = ((), (), s32[]{:S(2)}) async-start(), calls=%async_computation.12 | async-start | bytes 2785280 | tf_op jit(solution)/shard_map/all_gather | solution.py:567
  37.3 19.6 %all-to-all-start = ((bf16[4,128,2048]{2,1,0:T(8,128)(2,1)}), bf16[4,128,2048]{2,1,0:T(8,128)(2,1)S(1)}, u32[]{:S(2)}, u32[]{:S(2)}) async-start(bf16[4,128,2048]{2,1,0:T(8,128)(2,1)} %broadcast_in_dim.17), calls=%async_computation | async-start | bytes 4194304 | tf_op jit(solution)/shard_map/all_to_all | solution.py:60
  41.6 204.5 %all-gather.5.cloned.1.call-start = ((), (), s32[]{:S(2)}) async-start(), calls=%async_computation.13 | async-start | bytes 10027008 | tf_op jit(solution)/shard_map/all_gather | solution.py:571
  58.3 17.2 %collective-permute-start.3 = (bf16[128,2304]{1,0:T(8,128)(2,1)}, bf16[128,2304]{1,0:T(8,128)(2,1)S(1)}, u32[]{:S(2)}, u32[]{:S(2)}) collective-permute-start(bf16[128,2304]{1,0:T(8,128)(2,1)} %shard_map.403), channel_id=1, source_target_pairs={{0,0},{1,8},{8,1},{9,9},{2,2},{3,10},{10,3},{11,11},{4,4},{5,12},{... | collective-permute-start | bytes 1769480 | tf_op jit(solution)/shard_map/ppermute | solution.py:52
  76.3 13.9 %collective-permute-start.2 = (bf16[512,2048]{1,0:T(8,128)(2,1)}, bf16[512,2048]{1,0:T(8,128)(2,1)}, u32[]{:S(2)}, u32[]{:S(2)}) collective-permute-start(bf16[512,2048]{1,0:T(8,128)(2,1)} %bitcast.58), channel_id=1, source_target_pairs={{0,8},{8,0},{1,9},{9,1},{2,10},{10,2},{3,11},{11,3},{4,12},{12,4},... | collective-permute-start | bytes 6291464 | tf_op jit(solution)/shard_map/ppermute | solution.py:56
  97.1 12.8 %collective-permute-start.5 = (bf16[128,2048]{1,0:T(8,128)(2,1)}, bf16[128,2048]{1,0:T(8,128)(2,1)}, u32[]{:S(2)}, u32[]{:S(2)}) collective-permute-start(bf16[128,2048]{1,0:T(8,128)(2,1)} %shard_map.405), channel_id=1, source_target_pairs={{0,2},{2,4},{4,6},{6,0},{1,3},{3,5},{5,7},{7,1},{8,10},{10,12},{12... | collective-permute-start | bytes 1572872 | tf_op jit(solution)/shard_map/ppermute | solution.py:68
  98.3 17.2 %collective-permute-start.6 = (bf16[128,2048]{1,0:T(8,128)(2,1)}, bf16[128,2048]{1,0:T(8,128)(2,1)}, u32[]{:S(2)}, u32[]{:S(2)}) collective-permute-start(bf16[128,2048]{1,0:T(8,128)(2,1)} %shard_map.405), channel_id=1, source_target_pairs={{0,4},{2,6},{4,0},{6,2},{1,5},{3,7},{5,1},{7,3},{8,12},{10,14},{12... | collective-permute-start | bytes 1572872 | tf_op jit(solution)/shard_map/ppermute | solution.py:68
  100.8 16.7 %collective-permute-start.7 = (bf16[128,2048]{1,0:T(8,128)(2,1)}, bf16[128,2048]{1,0:T(8,128)(2,1)S(1)}, u32[]{:S(2)}, u32[]{:S(2)}) collective-permute-start(bf16[128,2048]{1,0:T(8,128)(2,1)} %shard_map.405), channel_id=1, source_target_pairs={{0,6},{2,0},{4,2},{6,4},{1,7},{3,1},{5,3},{7,5},{8,14},{10,8},{12,... | collective-permute-start | bytes 1572872 | tf_op jit(solution)/shard_map/ppermute | solution.py:68
  118.2 51.0 %collective-permute-start.8 = (bf16[512,2048]{1,0:T(8,128)(2,1)}, bf16[512,2048]{1,0:T(8,128)(2,1)}, u32[]{:S(2)}, u32[]{:S(2)}) collective-permute-start(bf16[512,2048]{1,0:T(8,128)(2,1)} %constant_dynamic-update-slice_fusion.g0), channel_id=1, source_target_pairs={{0,8},{8,0},{1,9},{9,1},{2,10},{10,2},{3,11},{11,3},{4,12},{12,4},... | collective-permute-start | bytes 6291464 | tf_op jit(solution)/shard_map/ppermute | solution.py:56
  129.4 16.2 %all-to-all-start.1 = ((f32[16,24,128]{2,1,0:T(8,128)}), f32[16,24,128]{2,1,0:T(8,128)}, u32[]{:S(2)}, u32[]{:S(2)}) async-start(f32[16,24,128]{2,1,0:T(8,128)} %bitcast.65), calls=%async_computation.1 | async-start | bytes 393216 | tf_op jit(solution)/shard_map/all_to_all | solution.py:529
  274.0 30.9 %all-to-all-start.5 = ((bf16[4,128,2048]{2,1,0:T(8,128)(2,1)}), bf16[4,128,2048]{2,1,0:T(8,128)(2,1)}, u32[]{:S(2)}, u32[]{:S(2)}) async-start(bf16[4,128,2048]{2,1,0:T(8,128)(2,1)} %bitcast.82), calls=%async_computation.5 | async-start | bytes 4194304 | tf_op jit(solution)/shard_map/all_to_all | solution.py:60
  278.5 208.6 %reduce-scatter.2.cloned.1.call-start = ((), (), s32[]{:S(2)}) async-start(), calls=%async_computation.14 | async-start | bytes 10027008 | tf_op jit(solution)/shard_map/reduce_scatter | solution.py:656
  366.7 28.4 %collective-permute-start.16 = (bf16[128,2048]{1,0:T(8,128)(2,1)}, bf16[128,2048]{1,0:T(8,128)(2,1)}, u32[]{:S(2)}, u32[]{:S(2)}) collective-permute-start(bf16[128,2048]{1,0:T(8,128)(2,1)} %get-tuple-element.82), channel_id=1, source_target_pairs={{0,6},{2,0},{4,2},{6,4},{1,7},{3,1},{5,3},{7,5},{8,14},{10,8},{12,... | collective-permute-start | bytes 1572872 | tf_op jit(solution)/shard_map/ppermute | solution.py:68
  367.6 27.5 %collective-permute-start.15 = (bf16[128,2048]{1,0:T(8,128)(2,1)}, bf16[128,2048]{1,0:T(8,128)(2,1)}, u32[]{:S(2)}, u32[]{:S(2)}) collective-permute-start(bf16[128,2048]{1,0:T(8,128)(2,1)} %get-tuple-element.83), channel_id=1, source_target_pairs={{0,4},{2,6},{4,0},{6,2},{1,5},{3,7},{5,1},{7,3},{8,12},{10,14},{12... | collective-permute-start | bytes 1572872 | tf_op jit(solution)/shard_map/ppermute | solution.py:68
  368.8 26.3 %collective-permute-start.14 = (bf16[128,2048]{1,0:T(8,128)(2,1)}, bf16[128,2048]{1,0:T(8,128)(2,1)}, u32[]{:S(2)}, u32[]{:S(2)}) collective-permute-start(bf16[128,2048]{1,0:T(8,128)(2,1)} %get-tuple-element.81), channel_id=1, source_target_pairs={{0,2},{2,4},{4,6},{6,0},{1,3},{3,5},{5,7},{7,1},{8,10},{10,12},{12... | collective-permute-start | bytes 1572872 | tf_op jit(solution)/shard_map/ppermute | solution.py:68
  425.5 16.7 %collective-permute-start.18 = (bf16[512,2048]{1,0:T(8,128)(2,1)}, bf16[512,2048]{1,0:T(8,128)(2,1)}, u32[]{:S(2)}, u32[]{:S(2)}) collective-permute-start(bf16[512,2048]{1,0:T(8,128)(2,1)} %convolution_convert_fusion.1.other_ref), channel_id=1, source_target_pairs={{0,8},{8,0},{1,9},{9,1},{2,10},{10,2},{3,11},{11,3},{4,12},{12,4},... | collective-permute-start | bytes 6291464 | tf_op jit(solution)/shard_map/ppermute | solution.py:56
  437.6 44.8 %all-to-all-start.9 = ((bf16[16,128,640]{2,1,0:T(8,128)(2,1)}), bf16[16,128,640]{2,1,0:T(8,128)(2,1)}, u32[]{:S(2)}, u32[]{:S(2)}) async-start(bf16[16,128,640]{2,1,0:T(8,128)(2,1)} %shard_map.416), calls=%async_computation.9 | async-start | bytes 5242880 | tf_op jit(solution)/shard_map/all_to_all | solution.py:529
  445.8 25.2 %collective-permute-start.21 = (bf16[128,2048]{1,0:T(8,128)(2,1)S(1)}, bf16[128,2048]{1,0:T(8,128)(2,1)S(1)}, u32[]{:S(2)}, u32[]{:S(2)}) collective-permute-start(bf16[128,2048]{1,0:T(8,128)(2,1)S(1)} %get-tuple-element.79), channel_id=1, source_target_pairs={{0,6},{2,0},{4,2},{6,4},{1,7},{3,1},{5,3},{7,5},{8,14},{10,8},{12,... | collective-permute-start | bytes 1572872 | tf_op jit(solution)/shard_map/ppermute | solution.py:68
  448.6 22.4 %collective-permute-start.20 = (bf16[128,2048]{1,0:T(8,128)(2,1)S(1)}, bf16[128,2048]{1,0:T(8,128)(2,1)S(1)}, u32[]{:S(2)}, u32[]{:S(2)}) collective-permute-start(bf16[128,2048]{1,0:T(8,128)(2,1)S(1)} %get-tuple-element.80), channel_id=1, source_target_pairs={{0,4},{2,6},{4,0},{6,2},{1,5},{3,7},{5,1},{7,3},{8,12},{10,14},{12... | collective-permute-start | bytes 1572872 | tf_op jit(solution)/shard_map/ppermute | solution.py:68
  449.1 26.2 %collective-permute-start.19 = (bf16[128,2048]{1,0:T(8,128)(2,1)S(1)}, bf16[128,2048]{1,0:T(8,128)(2,1)S(1)}, u32[]{:S(2)}, u32[]{:S(2)}) collective-permute-start(bf16[128,2048]{1,0:T(8,128)(2,1)S(1)} %get-tuple-element.78), channel_id=1, source_target_pairs={{0,2},{2,4},{4,6},{6,0},{1,3},{3,5},{5,7},{7,1},{8,10},{10,12},{12... | collective-permute-start | bytes 1572872 | tf_op jit(solution)/shard_map/ppermute | solution.py:68
  450.5 53.6 %collective-permute-start.17 = (bf16[128,2048]{1,0:T(8,128)(2,1)}, bf16[128,2048]{1,0:T(8,128)(2,1)}, u32[]{:S(2)}, u32[]{:S(2)}) collective-permute-start(bf16[128,2048]{1,0:T(8,128)(2,1)} %add_convert_fusion.4.other_ref), channel_id=1, source_target_pairs={{0,0},{1,8},{8,1},{9,9},{2,2},{3,10},{10,3},{11,11},{4,4},{5,12},{... | collective-permute-start | bytes 1572872 | tf_op jit(solution)/shard_map/ppermute | solution.py:52
  477.4 29.9 %collective-permute-start.22 = (bf16[128,2048]{1,0:T(8,128)(2,1)}, bf16[128,2048]{1,0:T(8,128)(2,1)S(1)}, u32[]{:S(2)}, u32[]{:S(2)}) collective-permute-start(bf16[128,2048]{1,0:T(8,128)(2,1)} %fusion.28), channel_id=1, source_target_pairs={{0,0},{1,8},{8,1},{9,9},{2,2},{3,10},{10,3},{11,11},{4,4},{5,12},{... | collective-permute-start | bytes 1572872 | tf_op jit(solution)/shard_map/ppermute | solution.py:52
  484.7 21.4 %collective-permute-start.24 = (bf16[128,640]{1,0:T(8,128)(2,1)S(1)}, bf16[128,640]{1,0:T(8,128)(2,1)S(1)}, u32[]{:S(2)}, u32[]{:S(2)}) collective-permute-start(bf16[128,640]{1,0:T(8,128)(2,1)S(1)} %convert_element_type.258), channel_id=1, source_target_pairs={{0,0},{1,8},{8,1},{9,9},{2,2},{3,10},{10,3},{11,11},{4,4},{5,12},{... | collective-permute-start | bytes 491528 | tf_op jit(solution)/shard_map/ppermute | solution.py:52
  487.1 25.0 %collective-permute-start.25 = (bf16[128,2304]{1,0:T(8,128)(2,1)}, bf16[128,2304]{1,0:T(8,128)(2,1)S(1)}, u32[]{:S(2)}, u32[]{:S(2)}) collective-permute-start(bf16[128,2304]{1,0:T(8,128)(2,1)} %reduce-scatter.2.cloned.1.call-done), channel_id=1, source_target_pairs={{0,0},{1,8},{8,1},{9,9},{2,2},{3,10},{10,3},{11,11},{4,4},{5,12},{... | collective-permute-start | bytes 1769480 | tf_op jit(solution)/shard_map/ppermute | solution.py:52
  (113 other events, 926.1 us)
Sparse Core Ops, SparseCore 0:
  20.6 49.2 all-gather.2
  76.4 76.8 all-gather.4
  308.1 85.9 reduce-scatter.1

commit v3 on v2

v3 whole, which is shorter than its diff:
```python
import functools

import jax
import jax.numpy as jnp
import numpy as np
from jax import lax
from jax.experimental import pallas as pl
from jax.experimental.pallas import tpu as pltpu
from jax.sharding import PartitionSpec as P

D = 2048
HEADS = 16
FEAT = 16
DV = 128
FF = 5504
STEP = 10
FINE = ("x_lo", "z", "core", "y", "x_hi")
GROUPS = ("x_hi", "x_lo", "z")
N_GROUPS = 16
ROWS = 1024
CHUNK = 128
HALF = ROWS // 2
LOCAL_HEADS = 2
QK = 2 * LOCAL_HEADS * FEAT
VW = LOCAL_HEADS * DV
PW = VW + QK
FFL = 688
FFP = 768
AW = 640
PHI = 256
PHI_ROWS = 160
HEAD_ROWS = 192
STATE_ROWS = LOCAL_HEADS * HEAD_ROWS
TILE = 256

norm_eps = 1e-05
beta_one = 0.5
beta_two = 0.5
adam_eps = 1e-08
weight_decay = 0.01
gain_rate = 0.5

f32 = jnp.float32
bf16 = jnp.bfloat16


FLIP = [(0, 1), (1, 0)]
CROSS = [(0, 0), (1, 2), (2, 1), (3, 3)]


def cross(a):
    return lax.ppermute(a, ("core", "x_hi"), CROSS)


def swap_core(a):
    return lax.ppermute(a, "core", FLIP)


def over_y(a):
    return lax.all_to_all(a, "y", 0, 0)


def spread(mine):
    return jnp.broadcast_to(mine[None], (4,) + mine.shape)


def to_y(a, step):
    return lax.ppermute(a, "y", [(i, (i + step) % 4) for i in range(4)])


def gather_rows(mine):
    own = over_y(spread(mine)).reshape(HALF, -1)
    return own, swap_core(own)


def sum_rows(low):
    return jnp.sum(over_y(low.reshape(4, CHUNK, D)).astype(f32), axis=0)


def sum_rows_apart(low):
    y = lax.axis_index("y")

    def part(step):
        return lax.dynamic_slice(low, ((y + step) % 4 * CHUNK, 0), (CHUNK, D))

    parts = [to_y(part(step), step) for step in (1, 2, 3)]
    out = part(0).astype(f32)
    for a in parts:
        out = out + a.astype(f32)
    return out


def scatter_rows(partial, between=None, total=sum_rows, later=None):
    send = partial(1, None)
    got = swap_core(send)
    if later is not None:
        got = after(got, later)
    low = partial(0, got)
    if between is not None:
        between(send, low)
    return total(low)


def rows_of(halves, weight, dims):
    def partial(half, more):
        total = matmul(halves[half], weight, dims)
        if more is not None:
            total = total + more.astype(f32)
        return total.astype(bf16)

    return partial


def halves_of(a):
    return a[:HALF], a[HALF:]


def matmul(a, b, dims=((1,), (0,))):
    return lax.dot_general(a, b, (dims, ((), ())), preferred_element_type=f32)


def iota(shape, dim):
    return lax.broadcasted_iota(jnp.int32, shape, dim)


def sides_of(kind, head):
    base = (kind * LOCAL_HEADS + head) * FEAT
    row = iota((QK, PHI), 0) - base
    col = iota((QK, PHI), 1)
    a = col % FEAT
    pair = col < 136
    one = (row == a) & (pair | ((col >= 144) & (col < PHI_ROWS)))
    two = (row == (a + col // FEAT) % FEAT) & pair
    return one.astype(f32).astype(bf16), two.astype(f32).astype(bf16)


def feature_rows():
    col = iota((1, PHI), 1)
    only = (col == 136).astype(f32)
    linear = ((col >= 144) & (col < PHI_ROWS)).astype(f32)
    square = (col < FEAT).astype(f32)
    cross_term = ((col >= FEAT) & (col < 136)).astype(f32)
    scale = (
        only
        + linear * FEAT ** (-0.25)
        + (square + cross_term * 2.0**0.5) * (2.0 * FEAT) ** (-0.5)
    )
    return only, only + linear, scale


def mover(kind, head):
    base = (kind * LOCAL_HEADS + head) * FEAT
    other = ((1 - kind) * LOCAL_HEADS + head) * FEAT
    row = iota((QK, QK), 0)
    col = iota((QK, QK), 1)
    hit = (row - base == col - other) & (row >= base) & (row < base + FEAT)
    return (hit.astype(f32) * FEAT ** (-0.5)).astype(bf16)


def doc_at(info_ref, pos):
    return sum((pos >= info_ref[8 + i]).astype(jnp.int32) for i in range(3))


def doc_column(info_ref, lo, hi):
    return doc_at(info_ref, info_ref[11] + lo + iota((hi - lo, 1), 0))


def is_last(info_ref, lo, hi):
    return (doc_column(info_ref, lo, hi) == info_ref[12]).astype(f32)


def continues(info_ref, lo, hi):
    return (doc_column(info_ref, lo, hi) == info_ref[13]).astype(f32)


def allowed_at(info_ref, r, end):
    at = r + iota((TILE, end), 0)
    of = iota((TILE, end), 1)
    doc_row = doc_at(info_ref, info_ref[11] + iota((1, end), 1))
    return (of <= at) & (doc_column(info_ref, r, end) == doc_row)


def split(a):
    hi = a.astype(bf16)
    return hi, (a - hi.astype(f32)).astype(bf16)


def dot_low(a, b, dims):
    hi, lo = split(a)
    return matmul(hi, b, dims) + matmul(lo, b, dims)


def dot_full(a, b, dims):
    ah, al = split(a)
    bh, bl = split(b)
    return matmul(ah, bh, dims) + (matmul(al, bh, dims) + matmul(ah, bl, dims))


def side(u, kind, head):
    left, right = sides_of(kind, head)
    one, two, scale = feature_rows()
    return matmul(u, left) + one, matmul(u, right) + two, scale


def to_order(idx_ref, src_ref, dst):
    for i in range(8):
        dst[pl.ds(i * CHUNK, CHUNK), :] = src_ref[
            pl.ds(pl.multiple_of(idx_ref[i] * CHUNK, CHUNK), CHUNK), :
        ]


def from_order(idx_ref, i, dst_ref, block):
    dst_ref[pl.ds(pl.multiple_of(idx_ref[i] * CHUNK, CHUNK), CHUNK), :] = block


def state_rows(ref, head):
    base = head * HEAD_ROWS
    mat = jnp.concatenate(
        [ref[base : base + PHI_ROWS, :], jnp.zeros((PHI - PHI_ROWS, DV), f32)], axis=0
    )
    vec = jnp.concatenate(
        [ref[base + PHI_ROWS : base + PHI_ROWS + 1, :], ref[base + PHI_ROWS + 1 : base + PHI_ROWS + 2, :]],
        axis=1,
    )
    return mat, vec


def store_state(ref, head, mat, vec):
    base = head * HEAD_ROWS
    ref[base : base + PHI_ROWS, :] = mat[:PHI_ROWS]
    tail = jnp.concatenate(
        [vec[:, :DV], vec[:, DV:], jnp.zeros((HEAD_ROWS - PHI_ROWS - 2, DV), f32)], axis=0
    )
    ref[base + PHI_ROWS : base + HEAD_ROWS, :] = tail


def key_state_kernel(idx_ref, p_ref, out_ref, scr):
    to_order(idx_ref, p_ref, scr)
    for head in range(LOCAL_HEADS):
        mat = jnp.zeros((PHI, DV), f32)
        vec = jnp.zeros((1, PHI), f32)
        for r in range(0, ROWS, TILE):
            u = scr[r : r + TILE, VW:PW]
            v = scr[r : r + TILE, head * DV : (head + 1) * DV]
            one, two, scale = side(u, 1, head)
            phi = one * two * scale * is_last(idx_ref, r, r + TILE)
            mat = mat + dot_low(phi, v, ((0,), (0,)))
            vec = vec + jnp.sum(phi, axis=0, keepdims=True)
        store_state(out_ref, head, mat, vec)


def attend_inside_kernel(
    idx_ref, p_ref, num_ref, den_ref, scr,
):
    to_order(idx_ref, p_ref, scr)
    u_all = scr[:, VW:PW]
    for head in range(LOCAL_HEADS):
        cols = slice(head * DV, (head + 1) * DV)
        v_all = scr[:, cols]
        for r in range(0, ROWS, TILE):
            end = r + TILE
            moved = matmul(scr[r:end, VW:PW], mover(0, head)).astype(bf16)
            s = matmul(moved, u_all[:end], ((1,), (1,)))
            allowed = allowed_at(idx_ref, r, end)
            kern = jnp.where(allowed, 1.0 + s + 0.5 * s * s, 0.0)
            num_ref[r:end, cols] = matmul(kern.astype(bf16), v_all[:end])
            den_ref[r:end, head : head + 1] = jnp.sum(kern, axis=1, keepdims=True)


def attend_kernel(
    idx_ref, p_ref, num_ref, den_in_ref, state_ref,
    att_ref, den_ref, low_ref, scr,
):
    to_order(idx_ref, p_ref, scr)
    for head in range(LOCAL_HEADS):
        cols = slice(head * DV, (head + 1) * DV)
        mat, vec = state_rows(state_ref, head)
        for r in range(0, ROWS, TILE):
            end = r + TILE
            cont = continues(idx_ref, r, end)
            one, two, scale = side(scr[r:end, VW:PW], 0, head)
            phi = one * two * scale
            num = num_ref[r:end, cols] + cont * dot_full(phi, mat, ((1,), (0,)))
            den = den_in_ref[r:end, head : head + 1] + cont * jnp.sum(phi * vec, axis=1, keepdims=True)
            att_ref[r:end, cols] = num / den
            den_ref[r:end, head : head + 1] = den
    for i in range(8):
        from_order(idx_ref, i, low_ref, att_ref[i * CHUNK : (i + 1) * CHUNK, :].astype(bf16))


def query_state_kernel(
    idx_ref, p_ref, ga_ref, att_ref, den_ref,
    out_ref, gn_ref, gd_ref, scr, gscr,
):
    to_order(idx_ref, p_ref, scr)
    to_order(idx_ref, ga_ref, gscr)
    for head in range(LOCAL_HEADS):
        mat = jnp.zeros((PHI, DV), f32)
        vec = jnp.zeros((1, PHI), f32)
        cols = slice(head * DV, (head + 1) * DV)
        for r in range(0, ROWS, TILE):
            end = r + TILE
            den = den_ref[r:end, head : head + 1]
            ga = gscr[r:end, cols].astype(f32)
            gn = ga / den
            gd = -jnp.sum(ga * att_ref[r:end, cols], axis=1, keepdims=True) / den
            gn_ref[r:end, cols] = gn
            gd_ref[r:end, head : head + 1] = gd
            one, two, scale = side(scr[r:end, VW:PW], 0, head)
            phi = one * two * scale * continues(idx_ref, r, end)
            mat = mat + dot_full(phi, gn, ((0,), (0,)))
            vec = vec + jnp.sum(phi * gd, axis=0, keepdims=True)
        store_state(out_ref, head, mat, vec)


def attend_back_inside_kernel(
    idx_ref, p_ref, gn_ref, gd_ref, gqk, gv, scr,
):
    to_order(idx_ref, p_ref, scr)
    u_all = scr[:, VW:PW]
    gqk[...] = jnp.zeros((ROWS, QK), f32)
    gv[...] = jnp.zeros((ROWS, VW), f32)
    for head in range(LOCAL_HEADS):
        cols = slice(head * DV, (head + 1) * DV)
        v_all = scr[:, cols]
        back_all = matmul(u_all, mover(1, head)).astype(bf16)
        for r in range(0, ROWS, TILE):
            end = r + TILE
            low_gn = gn_ref[r:end, cols].astype(bf16)
            gd = gd_ref[r:end, head : head + 1]
            moved = matmul(scr[r:end, VW:PW], mover(0, head)).astype(bf16)
            s = matmul(moved, u_all[:end], ((1,), (1,)))
            allowed = allowed_at(idx_ref, r, end)
            kern = jnp.where(allowed, 1.0 + s + 0.5 * s * s, 0.0).astype(bf16)
            gk = matmul(low_gn, v_all[:end], ((1,), (1,))) + gd
            gs = jnp.where(allowed, gk * (1.0 + s), 0.0).astype(bf16)
            gqk[r:end, :] = gqk[r:end, :] + matmul(gs, back_all[:end])
            gqk[:end, :] = gqk[:end, :] + matmul(gs, moved, ((0,), (0,)))
            gv[:end, cols] = gv[:end, cols] + matmul(kern, low_gn, ((0,), (0,)))


def attend_back_kernel(
    idx_ref, p_ref, gn_ref, gd_ref, gqk_ref, gv_ref, state_ref, grad_state_ref,
    out_ref, scr, gqk, gv,
):
    to_order(idx_ref, p_ref, scr)
    for head in range(LOCAL_HEADS):
        cols = slice(head * DV, (head + 1) * DV)
        mat, vec = state_rows(state_ref, head)
        gmat, gvec = state_rows(grad_state_ref, head)
        for r in range(0, ROWS, TILE):
            end = r + TILE
            u = scr[r:end, VW:PW]
            cont = continues(idx_ref, r, end)
            in_last = is_last(idx_ref, r, end)
            gn = gn_ref[r:end, cols]
            gd = gd_ref[r:end, head : head + 1]
            one, two, scale = side(u, 0, head)
            left, right = sides_of(0, head)
            grad = (dot_low_right(gn.astype(bf16), mat) + gd * vec) * cont * scale
            acc = matmul((grad * two).astype(bf16), left, ((1,), (1,)))
            acc = acc + matmul((grad * one).astype(bf16), right, ((1,), (1,)))
            one, two, scale = side(u, 1, head)
            left, right = sides_of(1, head)
            grad = (dot_low_right(scr[r:end, cols], gmat) + gvec) * in_last * scale
            acc = acc + matmul((grad * two).astype(bf16), left, ((1,), (1,)))
            acc = acc + matmul((grad * one).astype(bf16), right, ((1,), (1,)))
            phi = one * two * scale * in_last
            before = gqk_ref if head == 0 else gqk
            gqk[r:end, :] = before[r:end, :] + acc
            gv[r:end, cols] = gv_ref[r:end, cols] + dot_low(phi, gmat.astype(bf16), ((1,), (0,)))
    for i in range(8):
        chunk = slice(i * CHUNK, (i + 1) * CHUNK)
        from_order(
            idx_ref, i, out_ref,
            jnp.concatenate([gv[chunk, :], gqk[chunk, :]], axis=1).astype(bf16),
        )


def dot_low_right(a, b):
    hi, lo = split(b)
    return matmul(a, hi, ((1,), (1,))) + matmul(a, lo, ((1,), (1,)))


def call(kernel, outs, scratch, n_in):
    return pl.pallas_call(
        kernel,
        out_shape=outs,
        in_specs=[pl.BlockSpec(memory_space=pltpu.SMEM)]
        + [pl.BlockSpec(memory_space=pltpu.VMEM)] * (n_in - 1),
        out_specs=[pl.BlockSpec(memory_space=pltpu.VMEM)] * len(outs),
        scratch_shapes=scratch,
        compiler_params=pltpu.CompilerParams(vmem_limit_bytes=48 * 1024 * 1024),
    )


def adam_step(weight, moment_one, moment_two, reduced, step_rate):
    new_one = beta_one * moment_one + (1.0 - beta_one) * reduced
    new_two = beta_two * moment_two + (1.0 - beta_two) * reduced * reduced
    corrected_one = new_one / (1.0 - beta_one**STEP)
    corrected_two = new_two / (1.0 - beta_two**STEP)
    master = weight - step_rate * (
        corrected_one / (jnp.sqrt(corrected_two) + adam_eps) + weight_decay * weight
    )
    return (new_one, new_two, master)


def nothing_kernel(other_ref, a_ref, out_ref):
    pass


def after(a, other):
    return pl.pallas_call(
        nothing_kernel,
        out_shape=jax.ShapeDtypeStruct(a.shape, a.dtype),
        in_specs=[pl.BlockSpec(memory_space=pl.ANY)] * 2,
        out_specs=pl.BlockSpec(memory_space=pl.ANY),
        input_output_aliases={1: 0},
    )(other, a)


def pack_first_kernel(value_ref, feature_ref, output_ref, gain_row_ref, gain_col_ref, out_ref):
    def low(a):
        return a.astype(bf16).astype(f32)

    out_ref[:, :VW] = low(output_ref[...]).T.astype(bf16)
    out_ref[:, VW : 2 * VW] = (low(value_ref[...]) * gain_col_ref[:, 0:1]).astype(bf16)
    out_ref[:, 2 * VW : VW + PW] = (low(feature_ref[...]) * gain_row_ref[0:1]).T.astype(bf16)
    out_ref[:, VW + PW :] = jnp.zeros((CHUNK, AW - VW - PW), bf16)


def pack_mlp_kernel(gateup_ref, down_ref, gain_row_ref, out_ref):
    def low(a):
        return a.astype(bf16).astype(f32)

    def wide(a):
        return jnp.concatenate([a, jnp.zeros((FFP - FFL, CHUNK), f32)], axis=0).T.astype(bf16)

    out_ref[:, :FFP] = wide(low(gateup_ref[0]) * gain_row_ref[1:2])
    out_ref[:, FFP : 2 * FFP] = wide(low(gateup_ref[1]) * gain_row_ref[1:2])
    out_ref[:, 2 * FFP :] = wide(low(down_ref[...]))


def adam_store(weight, first, second, grad, rate, outs, at=()):
    place = at if at else (slice(None), slice(None))
    for ref, new in zip(outs, adam_step(weight[place], first[place], second[place], grad, rate)):
        ref[place] = new


def adam_mlp_kernel(
    grad_ref, gain_row_ref, gw, gf, gs, dw, df, ds, g1, g2, g3, d1, d2, d3
):
    for part in range(2):
        grad = grad_ref[part * FFP : part * FFP + FFL].astype(f32)
        adam_store(
            gw, gf, gs, grad * gain_row_ref[1:2], D ** (-0.5), (g1, g2, g3),
            (part, slice(None), slice(None)),
        )
    adam_store(dw, df, ds, grad_ref[2 * FFP : 2 * FFP + FFL].astype(f32), FF ** (-0.5), (d1, d2, d3))


def adam_attn_kernel(
    grad_ref, gain_row_ref,
    fw, ff, fs, vw, vf, vs, ow, of, os, f1, f2, f3, v1, v2, v3, o1, o2, o3,
):
    grad = (grad_ref[VW : 2 * VW].astype(f32) * gain_row_ref[0:1]).T
    adam_store(vw, vf, vs, grad, D ** (-0.5), (v1, v2, v3))
    grad = grad_ref[2 * VW :].astype(f32) * gain_row_ref[0:1]
    adam_store(fw, ff, fs, grad, D ** (-0.5), (f1, f2, f3))
    grad = grad_ref[:VW].astype(f32)
    adam_store(ow, of, os, grad, (HEADS * DV // 64) ** (-0.5), (o1, o2, o3))


def turned(a):
    return a.astype(f32).T.astype(bf16)


def store_owners(out_ref, lo, hi, tile):
    for k in range(2):
        out_ref[k, 0, lo:hi, :] = tile[:, k * CHUNK : (k + 1) * CHUNK].astype(bf16)


def mlp_grads_kernel(other_ref, a0, a1, g0, g1, gu0, gu1, h0, h1, out_ref, scr):
    @pl.when(pl.program_id(0) == 0)
    def turn():
        for half, (gu, h) in enumerate(((gu0, h0), (gu1, h1))):
            cols = slice(half * HALF, (half + 1) * HALF)
            scr[:FFP, cols] = turned(gu[:, :FFP])
            scr[FFP : 2 * FFP, cols] = turned(gu[:, FFP:])
            scr[2 * FFP :, cols] = turned(h[...])

    for lo, hi, left, right in ((0, 2 * FFP, a0, a1), (2 * FFP, 3 * FFP, g0, g1)):
        tile = matmul(scr[lo:hi, :HALF], left[...]) + matmul(scr[lo:hi, HALF:], right[...])
        store_owners(out_ref, lo, hi, tile)


def out_grads_kernel(other_ref, g0, g1, rows_ref, out_ref, scr):
    @pl.when(pl.program_id(0) == 0)
    def turn():
        scr[...] = turned(rows_ref[...])

    tile = matmul(scr[:, :HALF], g0[...]) + matmul(scr[:, HALF:], g1[...])
    store_owners(out_ref, 0, VW, tile)


def proj_grads_kernel(other_ref, a0, a1, out_grad_ref, proj_ref, out_ref, scr):
    @pl.when(pl.program_id(0) == 0)
    def turn():
        scr[:VW] = turned(proj_ref[:, :VW])
        scr[VW:] = turned(proj_ref[:, VW:])

    tile = matmul(scr[:, :HALF], a0[...]) + matmul(scr[:, HALF:], a1[...])
    out_ref[:, 0, :VW, :] = out_grad_ref[:, 0]
    store_owners(out_ref, VW, VW + PW, tile)


def grads(kernel, height, other, tiled, whole, turned_rows, blocks=()):
    def by_owner(n):
        return pl.BlockSpec((2, 1, n, CHUNK), lambda i: (0, i, 0, 0))

    def full(a):
        return pl.BlockSpec(a.shape, lambda i: (0,) * a.ndim)

    return pl.pallas_call(
        kernel,
        grid=(D // TILE,),
        out_shape=jax.ShapeDtypeStruct((2, 8, height, CHUNK), bf16),
        in_specs=[pl.BlockSpec(memory_space=pl.ANY)]
        + [pl.BlockSpec((HALF, TILE), lambda i: (0, i))] * len(tiled)
        + [by_owner(a.shape[2]) for a in blocks]
        + [full(a) for a in whole],
        out_specs=by_owner(height),
        scratch_shapes=[pltpu.VMEM((turned_rows, ROWS), bf16)],
        compiler_params=pltpu.CompilerParams(vmem_limit_bytes=48 * 1024 * 1024),
    )(other, *tiled, *blocks, *whole)


def project_kernel(core_ref, a0, a1, w_ref, out_ref, acc):
    step = pl.program_id(0)

    @pl.when(step == 0)
    def start():
        acc[...] = jnp.zeros_like(acc)

    weight = w_ref[0].reshape(TILE, AW)[:, VW : VW + PW]
    acc[:HALF] += matmul(a0[...], weight)
    acc[HALF:] += matmul(a1[...], weight)

    @pl.when(step == D // TILE - 1)
    def end():
        out_ref[...] = acc[...].astype(bf16)


def project(core, acts, every):
    return pl.pallas_call(
        project_kernel,
        grid_spec=pltpu.PrefetchScalarGridSpec(
            num_scalar_prefetch=1,
            grid=(D // TILE,),
            in_specs=[pl.BlockSpec((HALF, TILE), lambda i, core: (0, i))] * 2
            + [pl.BlockSpec((1, 2, CHUNK, AW), lambda i, core: (core[0], i, 0, 0))],
            out_specs=pl.BlockSpec((ROWS, PW), lambda i, core: (0, 0)),
            scratch_shapes=[pltpu.VMEM((ROWS, PW), f32)],
        ),
        out_shape=jax.ShapeDtypeStruct((ROWS, PW), bf16),
        compiler_params=pltpu.CompilerParams(vmem_limit_bytes=48 * 1024 * 1024),
    )(core, *acts, every)


def plain(kernel, outs, *args):
    return pl.pallas_call(
        kernel,
        out_shape=outs,
        compiler_params=pltpu.CompilerParams(vmem_limit_bytes=48 * 1024 * 1024),
    )(*args)


def same(*arrays):
    return [jax.ShapeDtypeStruct(a.shape, f32) for a in arrays]


def unit_norm(rows):
    inv = lax.rsqrt(jnp.mean(rows * rows, axis=-1, keepdims=True) + norm_eps)
    return rows * inv, inv


def unit_norm_back(shaped, unit, inv):
    return inv * (shaped - unit * jnp.mean(shaped * unit, axis=-1, keepdims=True))


def exchange(a):
    return lax.all_to_all(a, GROUPS, 0, 0)


def shards(
    tokens, cotangent, row_lengths, gains, gain_first, gain_second,
    feature_weight, feature_first, feature_second,
    value_weight, value_first, value_second,
    output_weight, output_first, output_second,
    gateup_weight, gateup_first, gateup_second,
    down_weight, down_first, down_second,
):
    core = lax.axis_index("core")
    group = (lax.axis_index("x_lo") * 4 + lax.axis_index("z")) * 2 + lax.axis_index("x_hi")
    gain_low = gains.astype(bf16).astype(f32)
    place = jnp.reshape(core, (1,)).astype(jnp.int32)

    gain_col = gain_low.T
    flat = [jnp.transpose(a, (1, 2, 0)) for a in (gateup_weight, gateup_first, gateup_second)]
    thin = [
        jnp.transpose(a, (1, 2, 0)).reshape(QK, CHUNK)
        for a in (feature_weight, feature_first, feature_second)
    ]
    first_part = plain(
        pack_first_kernel,
        jax.ShapeDtypeStruct((CHUNK, AW), bf16),
        value_weight, thin[0], output_weight, gain_low, gain_col,
    )
    gateup_part = plain(
        pack_mlp_kernel,
        jax.ShapeDtypeStruct((CHUNK, 3 * FFP), bf16),
        flat[0], down_weight, gain_low,
    )

    def gather_weights(part):
        every = lax.all_gather(part, ("x_hi", "x_lo", "z", "core"))
        return every.reshape(2, N_GROUPS, CHUNK, part.shape[1])

    def own_slice(every):
        return lax.dynamic_index_in_dim(every, core, 0, False)

    owner = (lax.axis_index("x_lo") * 4 + lax.axis_index("z")) * 2 + lax.axis_index("x_hi")
    every_attn = gather_weights(first_part)
    both = cross(jnp.stack([tokens, cotangent]))
    tokens = both[0]
    cot = both[1]
    inputs = tokens.astype(f32)
    unit_one, inv_one = unit_norm(inputs)
    acts_one = gather_rows(unit_one.astype(bf16))
    grad_mlp = gather_rows(after(cot, acts_one[0]))
    every_mlp = gather_weights(after(gateup_part, acts_one[0]))
    proj = project(place, acts_one, every_attn)
    attn_w = own_slice(after(every_attn, proj))
    first_own = lax.dynamic_index_in_dim(attn_w, owner, 0, False)[:, VW : VW + PW].astype(f32).T
    attn_w = attn_w.reshape(D, AW)
    out_w = attn_w[:, :VW]
    proj_w = attn_w[:, VW : VW + PW]
    mlp_w = own_slice(every_mlp).reshape(D, 3 * FFP)
    gateup_w = mlp_w[:, : 2 * FFP]
    down_w = mlp_w[:, 2 * FFP :]
    gateup_own = lax.dynamic_slice(
        every_mlp, (core, owner, 0, 0), (1, 1, CHUNK, 2 * FFP)
    ).reshape(CHUNK, 2 * FFP)
    gateup_own = gateup_own.T

    ends = jnp.cumsum(row_lengths)

    def doc_of(pos):
        return jnp.sum((pos[..., None] >= ends).astype(jnp.int32), axis=-1)

    places = jnp.arange(N_GROUPS, dtype=jnp.int32)
    group_ids = (places % 8) * 2 + places // 8
    doc_end = doc_of(group_ids * ROWS + (ROWS - 1))
    doc_before = jnp.where(group_ids > 0, doc_of(group_ids * ROWS - 1), -1)
    last_doc = doc_of(group * ROWS + (ROWS - 1))
    before = jnp.where(group > 0, doc_of(group * ROWS - 1), -1)
    carry = ((group_ids[None, :] < group_ids[:, None]) & (doc_end[None, :] == doc_before[:, None])).astype(f32)
    back = ((group_ids[None, :] > group_ids[:, None]) & (doc_before[None, :] == doc_end[:, None])).astype(f32)
    chunk_ids = jnp.arange(8, dtype=jnp.int32)
    idx = ((chunk_ids % 2) ^ core) * 4 + chunk_ids // 2
    idx = jnp.concatenate([idx, ends, jnp.stack([group * ROWS, last_doc, before])]).astype(jnp.int32)

    own_state = call(
        key_state_kernel,
        [jax.ShapeDtypeStruct((STATE_ROWS, DV), f32)],
        [pltpu.VMEM((ROWS, PW), bf16)],
        2,
    )(idx, proj)[0]
    slices = exchange(after(own_state, grad_mlp[0]).reshape(N_GROUPS, STATE_ROWS // N_GROUPS, DV))
    slices = jnp.sum(carry[:, :, None, None] * slices[None], axis=1)
    state = exchange(slices).reshape(STATE_ROWS, DV)
    num, den = call(
        attend_inside_kernel,
        [jax.ShapeDtypeStruct((ROWS, VW), f32), jax.ShapeDtypeStruct((ROWS, LOCAL_HEADS), f32)],
        [pltpu.VMEM((ROWS, PW), bf16)],
        2,
    )(idx, proj)
    att, den, attn_rows = call(
        attend_kernel,
        [
            jax.ShapeDtypeStruct((ROWS, VW), f32),
            jax.ShapeDtypeStruct((ROWS, LOCAL_HEADS), f32),
            jax.ShapeDtypeStruct((ROWS, VW), bf16),
        ],
        [pltpu.VMEM((ROWS, PW), bf16)],
        5,
    )(idx, proj, num, after(den, attn_w), state)

    middle = after(inputs, mlp_w) + scatter_rows(
        rows_of(halves_of(attn_rows), out_w, ((1,), (1,)))
    )
    unit_two, inv_two = unit_norm(middle)
    acts_two = gather_rows(unit_two.astype(bf16))
    hidden = []
    grad_gate_up = []
    for acts, grad in zip(acts_two, grad_mlp):
        gate_up = matmul(acts, gateup_w)
        grad_hidden = matmul(grad, down_w)
        gate = gate_up[:, :FFP]
        up = gate_up[:, FFP:]
        sigmoid = jax.nn.sigmoid(gate)
        silu = gate * sigmoid
        hidden.append((silu * up).astype(bf16))
        dsilu = sigmoid * (1.0 + gate * (1.0 - sigmoid))
        grad_gate_up.append(
            jnp.concatenate([grad_hidden * up * dsilu, grad_hidden * silu], axis=1).astype(bf16)
        )

    late = []

    def mlp_grads(send, low):
        mlp_grad = grads(
            mlp_grads_kernel, 3 * FFP, low, acts_two + grad_mlp, (*grad_gate_up, *hidden), 3 * FFP
        ).reshape(N_GROUPS * 3 * FFP, CHUNK)
        late.append(mlp_grad)

    shaped_two = scatter_rows(
        rows_of(grad_gate_up, gateup_w, ((1,), (1,))), mlp_grads
    )
    mlp_grad = lax.psum_scatter(after(late[0], shaped_two), GROUPS, scatter_dimension=0, tiled=True)
    grad_out = cot.astype(f32)
    grad_mid = grad_out + unit_norm_back(shaped_two, unit_two, inv_two)
    grad_attn = gather_rows(grad_mid.astype(bf16))

    mixed_own, mixed_other = [
        matmul(after(hidden[half], shaped_two), down_w, ((1,), (1,))).astype(bf16) for half in (0, 1)
    ]
    grad_low = jnp.concatenate([matmul(a, out_w).astype(bf16) for a in grad_attn])
    grad_low = after(after(grad_low, mixed_own), mixed_other)
    mixed_other = swap_core(mixed_other)
    mixed_low = (mixed_own.astype(f32) + mixed_other.astype(f32)).astype(bf16)
    mixed = middle + sum_rows_apart(after(mixed_low, grad_attn[1]))
    own_grad, gn, gd = call(
        query_state_kernel,
        [
            jax.ShapeDtypeStruct((STATE_ROWS, DV), f32),
            jax.ShapeDtypeStruct((ROWS, VW), f32),
            jax.ShapeDtypeStruct((ROWS, LOCAL_HEADS), f32),
        ],
        [pltpu.VMEM((ROWS, PW), bf16), pltpu.VMEM((ROWS, VW), bf16)],
        5,
    )(idx, proj, grad_low, att, den)
    den_part = jnp.sum(jnp.abs(den))
    slices = exchange(
        jnp.concatenate(
            [
                own_grad.reshape(N_GROUPS, STATE_ROWS // N_GROUPS, DV),
                jnp.full((N_GROUPS, 8, DV), den_part, f32),
            ],
            axis=1,
        )
    )
    den_group = jnp.sum(slices[:, STATE_ROWS // N_GROUPS :], axis=0)
    slices = jnp.sum(back[:, :, None, None] * slices[None, :, : STATE_ROWS // N_GROUPS], axis=1)
    output_grad = grads(out_grads_kernel, VW, own_grad, grad_attn, (attn_rows,), VW)
    grad_state = exchange(slices).reshape(STATE_ROWS, DV)
    mlp_grad_own = cross(after(mlp_grad, grad_state))
    gqk, gv = call(
        attend_back_inside_kernel,
        [jax.ShapeDtypeStruct((ROWS, QK), f32), jax.ShapeDtypeStruct((ROWS, VW), f32)],
        [pltpu.VMEM((ROWS, PW), bf16)],
        4,
    )(idx, proj, gn, gd)
    grad_proj = call(
        attend_back_kernel,
        [jax.ShapeDtypeStruct((ROWS, PW), bf16)],
        [pltpu.VMEM((ROWS, PW), bf16), pltpu.VMEM((ROWS, QK), f32), pltpu.VMEM((ROWS, VW), f32)],
        8,
    )(idx, proj, gn, after(after(gd, output_grad), mixed), gqk, gv, state, grad_state)[0]

    def proj_grads(send, low):
        attn_grad = grads(
            proj_grads_kernel, VW + PW, send, acts_one, (grad_proj,), PW, (output_grad,)
        ).reshape(N_GROUPS, VW + PW, CHUNK)
        late.append(exchange(attn_grad))

    mixed = cross(mixed.astype(bf16))
    shaped_one = scatter_rows(rows_of(halves_of(grad_proj), proj_w, ((1,), (1,))), proj_grads, sum_rows_apart)
    grad_tokens = grad_mid + unit_norm_back(shaped_one, unit_one, inv_one)
    grad_tokens = cross(grad_tokens.astype(bf16)).astype(f32)
    deep = plain(
        adam_mlp_kernel,
        same(*flat, down_weight, down_first, down_second),
        mlp_grad_own, gain_low, *flat, down_weight, down_first, down_second,
    )
    attn_grad = jnp.sum(after(late[1], deep[0]).astype(f32), axis=0)
    gain_one = jnp.sum(attn_grad[VW:] * first_own, axis=0)
    gain_two = jnp.sum(mlp_grad[: 2 * FFP].astype(f32) * gateup_own.astype(f32), axis=0)
    small = jnp.concatenate([gain_one[None], gain_two[None], den_group[:6]], axis=0)
    parts = lax.all_to_all(
        jnp.broadcast_to(small[None], (16, 8, CHUNK)), ("core", "y", "x_hi"), 0, 0
    ).reshape(8, 2, 8, CHUNK)
    small = jnp.sum(jnp.where(core == 0, parts[:, 0], parts[:, 1]), axis=0)
    attn_grad = cross(attn_grad.astype(bf16))

    gain_total = small[:2] / gain_low
    den_mean = small[2, 0] / (N_GROUPS * ROWS * HEADS)
    near = (*thin, value_weight, value_first, value_second, output_weight, output_first, output_second)
    near = plain(adam_attn_kernel, same(*near), attn_grad, gain_low, *near)
    news = list(adam_step(gains, gain_first, gain_second, gain_total, gain_rate))
    news += [jnp.transpose(a.reshape(2, QK // 2, CHUNK), (2, 0, 1)) for a in near[:3]]
    news += near[3:]
    news += [jnp.transpose(a, (2, 0, 1)) for a in deep[:3]]
    news += deep[3:]
    return (mixed, grad_tokens, den_mean) + tuple(news)


def solution(mesh):
    fine = jax.sharding.Mesh(mesh.devices.reshape(2, 4, 2, 4, 2), FINE)
    dp = ("x_lo", "z", "core")
    tensor = ("y", "x_hi")
    rows = P(FINE, None)
    gain = P(None, dp)
    deep = P(dp, None, tensor)
    down = P(dp, tensor)
    across = P(tensor, dp)
    return jax.shard_map(
        shards,
        mesh=fine,
        in_specs=(rows, rows, P())
        + (gain,) * 3
        + (deep,) * 3
        + (down,) * 3
        + (across,) * 3
        + (deep,) * 3
        + (across,) * 3,
        out_specs=(rows, rows, P())
        + (gain,) * 3
        + (deep,) * 3
        + (down,) * 3
        + (across,) * 3
        + (deep,) * 3
        + (across,) * 3,
        check_vma=False,
    )
```

time: 540 us -> 500 us (0.926)
  blocking collectives: 115 us -> 56.1 us
  starting transfers between devices: 91.9 us -> 101 us
  local copies, waits for them, and re-layouts: 50.7 us -> 59.1 us
  matrix products: 59 us -> 51 us
  Pallas kernels: 61.8 us -> 67.4 us
    all_to_all x3 -> x0, blocking collectives: 30.8 us -> none  [the longest x2 23.9 us: exchange(): return lax.all_to_all(a, GROUPS, 0, 0)]
    all_to_all x2 -> x4, waiting for transfers between devices: 22.9 us -> 53 us  [over_y(): return lax.all_to_all(a, 'y', 0, 0)]
    all_to_all x3 -> x2, blocking collectives: 84.1 us -> 56.1 us  [over_y(): return lax.all_to_all(a, 'y', 0, 0)]
    ppermute x9 -> x5, starting transfers between devices: 44.5 us -> 24.2 us  [cross(): return lax.ppermute(a, ('core', 'x_hi'), CROSS)]
    all_to_all x3 -> x5, starting transfers between devices: 16.8 us -> 33.3 us  [exchange(): return lax.all_to_all(a, GROUPS, 0, 0)]
    ppermute x9 -> x6, waiting for transfers between devices: 28.1 us -> 12.6 us  [to_y(): return lax.ppermute(a, 'y', [(i, (i + step) % 4) for i in range(4)])]
    dynamic_slice x0 -> x5, local copies, waits for them, and re-layouts: none -> 15.1 us  [the longest x2 12.3 us: own_slice(): return lax.dynamic_index_in_dim(every, core, 0, False)]
    ppermute x9 -> x5, waiting for transfers between devices: 28.3 us -> 15.7 us  [cross(): return lax.ppermute(a, ('core', 'x_hi'), CROSS)]
  transfers between devices with their start and end apart: 34 -> 32, of which waited for: 15 -> 15; matrix products, arithmetic and copies ran while one was open for 16% -> 18% of each run, Pallas kernels for 11% -> 13%
where the time goes in v3:
time: 500 us; the launch traced here: 492 us
  waiting for transfers between devices  104 us (21%)
  starting transfers between devices  101 us (20%)
  Pallas kernels  67.4 us (13%)
  local copies, waits for them, and re-layouts  59.1 us (12%)
  blocking collectives  56.1 us (11%)
  matrix products  51 us (10%)
  other arithmetic  35.7 us (7%)
  between operations  17.6 us (4%)
    all_to_all x2, blocking collectives, over_y(): return lax.all_to_all(a, 'y', 0, 0)  56.1 us
    all_to_all x4, waiting for transfers between devices, over_y(): return lax.all_to_all(a, 'y', 0, 0)  53 us
    dot_general x14, matrix products, matmul(): return lax.dot_general(a, b, (dims, ((), ())), preferred_element_type=f32)  51 us
    all_to_all x5, starting transfers between devices, exchange(): return lax.all_to_all(a, GROUPS, 0, 0)  33.3 us
    unnamed x178, local copies, waits for them, and re-layouts  30 us
    pallas_call x3, Pallas kernels, grads(): pl.pallas_call(kernel, grid=(D // TILE,), out_shape=jax.ShapeDtypeStruct(...  29 us
    ppermute x5, starting transfers between devices, cross(): return lax.ppermute(a, ('core', 'x_hi'), CROSS)  24.2 us
    all_to_all x4, starting transfers between devices, over_y(): return lax.all_to_all(a, 'y', 0, 0)  17.6 us
  transfers between devices with their start and end apart: 32, of which 15 were waited for; matrix products, arithmetic and copies ran while one was open for 18% of the time, Pallas kernels for 13%

profile of v3, /device:TPU:1, one launch (start us, length us, event | category | flops | bytes accessed | tf_op | source)
XLA Modules:
  0.0 492.1 jit_solution(6710024550788188911)
XLA Ops:
  12.8 6.0 %collective-permute-start = (bf16[2,128,2048]{2,1,0:T(8,128)(2,1)S(1)}, bf16[2,128,2048]{2,1,0:T(8,128)(2,1)S(1)}, u32[]{:S(2)}, u32[]{:S(2)}) collective-permute-start(bf16[2,128,2048]{2,1,0:T(8,128)(2,1)S(1)} %pad_maximum_fusion.2), channel_id=1, source_target_pairs={{0,0},{1,8},{8,1},{9,9},{2,2},{3,10},{10,3},{11,11},{4,4},{5,12},{... | collective-permute-start | bytes 3145736 | tf_op jit(solution)/shard_map/ppermute | solution.py:52
  18.8 13.9 %collective-permute-done = bf16[2,128,2048]{2,1,0:T(8,128)(2,1)S(1)} collective-permute-done((bf16[2,128,2048]{2,1,0:T(8,128)(2,1)S(1)}, bf16[2,128,2048]{2,1,0:T(8,128)(2,1)S(1)}, u32[]{:S(2)}, u32[]{:S(2)}) %collective-permute-start) | collective-permute-done | bytes 1048608 | tf_op jit(solution)/shard_map/ppermute | solution.py:52
  39.8 14.3 %all-to-all-done = bf16[4,128,2048]{2,1,0:T(8,128)(2,1)S(1)} async-done(((bf16[4,128,2048]{2,1,0:T(8,128)(2,1)}), bf16[4,128,2048]{2,1,0:T(8,128)(2,1)S(1)}, u32[]{:S(2)}, u32[]{:S(2)}) %all-to-all-start) | async-done | bytes 2097184 | tf_op jit(solution)/shard_map/all_to_all | solution.py:60
  66.5 7.0 %shard_map.368.p_ref.other_ref = bf16[1024,320]{1,0:T(8,128)(2,1)S(1)} custom-call(s32[1]{0:T(128)} %bitcast.13.core_ref, bf16[512,2048]{1,0:T(8,128)(2,1)S(1)} %bitcast.98, bf16[512,2048]{1,0:T(8,128)(2,1)} %collective-permute-done.1.a1, bf16[2,16,128,640]{3,2,1,0:T(8,128)(2,1)} %bitcast.124), custom_call_target="tpu_custom_call" | custom-call | tf_op jit(solution)/shard_map/pallas_call | solution.py:555
  77.6 12.4 %all-to-all-done.1 = bf16[4,128,2048]{2,1,0:T(8,128)(2,1)} async-done(((bf16[4,128,2048]{2,1,0:T(8,128)(2,1)}), bf16[4,128,2048]{2,1,0:T(8,128)(2,1)}, u32[]{:S(2)}, u32[]{:S(2)}) %all-to-all-start.1) | async-done | bytes 2097184 | tf_op jit(solution)/shard_map/all_to_all | solution.py:60
  90.1 10.9 %all-to-all-start.2 = ((f32[16,24,128]{2,1,0:T(8,128)}), f32[16,24,128]{2,1,0:T(8,128)S(1)}, u32[]{:S(2)}, u32[]{:S(2)}) async-start(f32[16,24,128]{2,1,0:T(8,128)} %bitcast.102), calls=%async_computation.2 | async-start | bytes 393216 | tf_op jit(solution)/shard_map/all_to_all | solution.py:592
  101.1 8.8 %all-to-all-done.2 = f32[16,24,128]{2,1,0:T(8,128)S(1)} async-done(((f32[16,24,128]{2,1,0:T(8,128)}), f32[16,24,128]{2,1,0:T(8,128)S(1)}, u32[]{:S(2)}, u32[]{:S(2)}) %all-to-all-start.2) | async-done | bytes 196640 | tf_op jit(solution)/shard_map/all_to_all | solution.py:592
  143.6 28.5 %all_to_all.60 = bf16[4,128,2048]{2,1,0:T(8,128)(2,1)S(1)} all-to-all(bf16[4,128,2048]{2,1,0:T(8,128)(2,1)S(1)} %bitcast.138), channel_id=1, replica_groups=mesh['x_lo'=2,'z'=4,'core'=2,'y'=4,'x_hi'=2] {'y'}, dimensions={0} | all-to-all | bytes 4194304 | tf_op jit(solution)/shard_map/all_to_all | solution.py:60
  173.5 8.1 %constant_dynamic-slice_fusion.9 = bf16[1,16,128,2304]{3,2,1,0:T(8,128)(2,1)} fusion(bf16[2,16,128,2304]{3,2,1,0:T(8,128)(2,1)} %bitcast.139, s32[]{:T(128)S(6)} %select_n.162), kind=kLoop, calls=%fused_computation.89 | loop fusion | bytes 18874372 | tf_op jit(solution)/shard_map/jit(dynamic_index_in_dim)/dynamic_slice | solution.py:630
  184.4 27.5 %all_to_all.61 = bf16[4,128,2048]{2,1,0:T(8,128)(2,1)S(1)} all-to-all(bf16[4,128,2048]{2,1,0:T(8,128)(2,1)S(1)} %broadcast_in_dim.21), channel_id=1, replica_groups=mesh['x_lo'=2,'z'=4,'core'=2,'y'=4,'x_hi'=2] {'y'}, dimensions={0} | all-to-all | bytes 4194304 | tf_op jit(solution)/shard_map/all_to_all | solution.py:60
  251.1 15.6 %shard_map.387 = bf16[2,8,2304,128]{3,2,1,0:T(8,128)(2,1)} custom-call(bf16[512,2048]{1,0:T(8,128)(2,1)} %add_convert_fusion.2.other_ref, bf16[512,2048]{1,0:T(8,128)(2,1)} %bitcast.136, bf16[512,2048]{1,0:T(8,128)(2,1)} %copy-done.70, bf16[512,2048]{1,0:T(8,128)(2,1)} %bitcast.20.other_ref.g0, bf16[512,2048]{1,0:T(8,128)(2,1)} %copy-done.71, ...), custom_call_target="tpu_custom_call" | custom-call | tf_op jit(solution)/shard_map/pallas_call | solution.py:524
  266.7 7.1 %all-to-all-done.6 = bf16[4,128,2048]{2,1,0:T(8,128)(2,1)} async-done(((bf16[4,128,2048]{2,1,0:T(8,128)(2,1)}), bf16[4,128,2048]{2,1,0:T(8,128)(2,1)}, u32[]{:S(2)}, u32[]{:S(2)}) %all-to-all-start.6) | async-done | bytes 2097184 | tf_op jit(solution)/shard_map/all_to_all | solution.py:60
  292.7 19.2 %all-to-all-done.7 = bf16[4,128,2048]{2,1,0:T(8,128)(2,1)} async-done(((bf16[4,128,2048]{2,1,0:T(8,128)(2,1)}), bf16[4,128,2048]{2,1,0:T(8,128)(2,1)}, u32[]{:S(2)}, u32[]{:S(2)}) %all-to-all-start.7) | async-done | bytes 2097184 | tf_op jit(solution)/shard_map/all_to_all | solution.py:60
  317.3 6.5 %add_convert_fusion.1 = (bf16[512,2048]{1,0:T(8,128)(2,1)}, bf16[512,2048]{1,0:T(8,128)(2,1)}) fusion(bf16[512,2048]{1,0:T(8,128)(2,1)} %collective-permute-done.7, bf16[512,768]{1,0:T(8,128)(2,1)S(1)} %copy-done.14, bf16[2048,2304]{1,0:T(8,128)(2,1)} %bitcast.117), kind=kOutput, calls=%fused_computation.2 | convolution fusion | flops 1615855616 | bytes 10223616 | tf_op jit(solution)/shard_map/dot_general | solution.py:119
  342.9 6.8 %all-to-all-start.8 = ((f32[16,32,128]{2,1,0:T(8,128)}), f32[16,32,128]{2,1,0:T(8,128)}, u32[]{:S(2)}, u32[]{:S(2)}) async-start(f32[16,32,128]{2,1,0:T(8,128)} %concatenate.24), calls=%async_computation.8 | async-start | bytes 524288 | tf_op jit(solution)/shard_map/all_to_all | solution.py:592
  350.9 6.9 %shard_map.385 = (f32[1024,64]{1,0:T(8,128)S(1)}, f32[1024,256]{1,0:T(8,128)S(1)}) custom-call(s32[14]{0:T(128)S(1)} %concatenate.20.idx_ref, bf16[1024,320]{1,0:T(8,128)(2,1)S(1)} %copy-done.3, f32[1024,256]{1,0:T(8,128)S(1)} %copy-done.11, f32[1024,2]{1,0:T(8,128)S(1)} %get-tuple-element.53.a_ref.gd_ref), custom_call_target="tpu_custom_call" | custom-call | tf_op jit(solution)/shard_map/pallas_call | solution.py:768
  359.6 6.1 %shard_map.382.other_ref.out_grad_ref = bf16[2,8,256,128]{3,2,1,0:T(8,128)(2,1)S(1)} custom-call(f32[384,128]{1,0:T(8,128)S(1)} %copy-done.40, bf16[512,2048]{1,0:T(8,128)(2,1)} %bitcast.26.g0, bf16[512,2048]{1,0:T(8,128)(2,1)} %collective-permute-done.6.other_ref.g1, bf16[1024,256]{1,0:T(8,128)(2,1)S(1)} %copy-done.25), custom_call_target="tpu_custom_call" | custom-call | tf_op jit(solution)/shard_map/pallas_call | solution.py:524
  368.7 6.8 %all-to-all-start.9 = ((f32[16,24,128]{2,1,0:T(8,128)}), f32[16,24,128]{2,1,0:T(8,128)S(1)}, u32[]{:S(2)}, u32[]{:S(2)}) async-start(f32[16,24,128]{2,1,0:T(8,128)} %multiply_reduce_fusion), calls=%async_computation.9 | async-start | bytes 393216 | tf_op jit(solution)/shard_map/all_to_all | solution.py:592
  387.0 6.1 %shard_map.386.proj_ref = bf16[1024,320]{1,0:T(8,128)(2,1)S(1)} custom-call(s32[14]{0:T(128)S(1)} %concatenate.20.idx_ref, bf16[1024,320]{1,0:T(8,128)(2,1)S(1)} %copy-done.3, f32[1024,256]{1,0:T(8,128)S(1)} %copy-done.12, f32[1024,2]{1,0:T(8,128)S(1)} %copy-done.7, f32[1024,64]{1,0:T(8,128)S(1)} %copy-done.48, f32[1024,256]{1,0:T(8,128)S(1)} %copy-done.38, ...), custom_call_target="tpu_custom_call" | custom-call | tf_op jit(solution)/shard_map/pallas_call | solution.py:774
  398.2 7.3 %shard_map.391 = bf16[2,8,576,128]{3,2,1,0:T(8,128)(2,1)} custom-call(bf16[512,2048]{1,0:T(8,128)(2,1)} %convolution_convert_fusion.1.other_ref, bf16[512,2048]{1,0:T(8,128)(2,1)S(1)} %bitcast.99, bf16[512,2048]{1,0:T(8,128)(2,1)} %collective-permute-done.1.a1, bf16[2,8,256,128]{3,2,1,0:T(8,128)(2,1)S(1)} %copy-done.5, bf16[1024,320]{1,0:T(8,128)(2,1)S(1)} %shard_map.386.proj_ref), custom_call_target="tpu_custom_call" | custom-call | tf_op jit(solution)/shard_map/pallas_call | solution.py:524
  424.5 5.8 %collective-permute-start.11 = (bf16[128,2048]{1,0:T(8,128)(2,1)}, bf16[128,2048]{1,0:T(8,128)(2,1)}, u32[]{:S(2)}, u32[]{:S(2)}) collective-permute-start(bf16[128,2048]{1,0:T(8,128)(2,1)} %get-tuple-element.78), channel_id=1, source_target_pairs={{0,0},{1,8},{8,1},{9,9},{2,2},{3,10},{10,3},{11,11},{4,4},{5,12},{... | collective-permute-start | bytes 1572872 | tf_op jit(solution)/shard_map/ppermute | solution.py:52
  431.3 11.7 %collective-permute-done.14 = bf16[128,2048]{1,0:T(8,128)(2,1)} collective-permute-done((bf16[128,2048]{1,0:T(8,128)(2,1)}, bf16[128,2048]{1,0:T(8,128)(2,1)}, u32[]{:S(2)}, u32[]{:S(2)}) %collective-permute-start.14) | collective-permute-done | bytes 524320 | tf_op jit(solution)/shard_map/ppermute | solution.py:68
  446.9 5.4 %collective-permute-start.17 = (bf16[2304,128]{1,0:T(8,128)(2,1)}, bf16[2304,128]{1,0:T(8,128)(2,1)S(1)}, u32[]{:S(2)}, u32[]{:S(2)}) collective-permute-start(bf16[2304,128]{1,0:T(8,128)(2,1)} %shard_map.389), channel_id=1, source_target_pairs={{0,0},{1,8},{8,1},{9,9},{2,2},{3,10},{10,3},{11,11},{4,4},{5,12},{... | collective-permute-start | bytes 1769480 | tf_op jit(solution)/shard_map/ppermute | solution.py:52
  465.3 6.8 %all-to-all-start.11 = ((f32[16,8,128]{2,1,0:T(8,128)}), f32[16,8,128]{2,1,0:T(8,128)S(1)}, u32[]{:S(2)}, u32[]{:S(2)}) async-start(f32[16,8,128]{2,1,0:T(8,128)} %broadcast_in_dim.25), calls=%async_computation.12 | async-start | bytes 131072 | tf_op jit(solution)/shard_map/all_to_all | solution.py:800
  (325 shorter events, 219.0 us)
Async XLA Ops:
  7.2 59.3 %all-gather.7.cloned.1.call-start = ((), (), s32[]{:S(2)}) async-start(), calls=%async_computation.15 | async-start | bytes 5406720 | tf_op jit(solution)/shard_map/all_gather | solution.py:626
  12.8 19.9 %collective-permute-start = (bf16[2,128,2048]{2,1,0:T(8,128)(2,1)S(1)}, bf16[2,128,2048]{2,1,0:T(8,128)(2,1)S(1)}, u32[]{:S(2)}, u32[]{:S(2)}) collective-permute-start(bf16[2,128,2048]{2,1,0:T(8,128)(2,1)S(1)} %pad_maximum_fusion.2), channel_id=1, source_target_pairs={{0,0},{1,8},{8,1},{9,9},{2,2},{3,10},{10,3},{11,11},{4,4},{5,12},{... | collective-permute-start | bytes 3145736 | tf_op jit(solution)/shard_map/ppermute | solution.py:52
  34.6 19.5 %all-to-all-start = ((bf16[4,128,2048]{2,1,0:T(8,128)(2,1)}), bf16[4,128,2048]{2,1,0:T(8,128)(2,1)S(1)}, u32[]{:S(2)}, u32[]{:S(2)}) async-start(bf16[4,128,2048]{2,1,0:T(8,128)(2,1)} %broadcast_in_dim.19), calls=%async_computation | async-start | bytes 4194304 | tf_op jit(solution)/shard_map/all_to_all | solution.py:60
  38.7 134.8 %all-gather.5.cloned.1.call-start = ((), (), s32[]{:S(2)}) async-start(), calls=%async_computation.14 | async-start | bytes 19464192 | tf_op jit(solution)/shard_map/all_gather | solution.py:626
  59.5 30.6 %all-to-all-start.1 = ((bf16[4,128,2048]{2,1,0:T(8,128)(2,1)}), bf16[4,128,2048]{2,1,0:T(8,128)(2,1)}, u32[]{:S(2)}, u32[]{:S(2)}) async-start(bf16[4,128,2048]{2,1,0:T(8,128)(2,1)} %broadcast_in_dim.20), calls=%async_computation.1 | async-start | bytes 4194304 | tf_op jit(solution)/shard_map/all_to_all | solution.py:60
  90.1 19.8 %all-to-all-start.2 = ((f32[16,24,128]{2,1,0:T(8,128)}), f32[16,24,128]{2,1,0:T(8,128)S(1)}, u32[]{:S(2)}, u32[]{:S(2)}) async-start(f32[16,24,128]{2,1,0:T(8,128)} %bitcast.102), calls=%async_computation.2 | async-start | bytes 393216 | tf_op jit(solution)/shard_map/all_to_all | solution.py:592
  110.9 13.4 %all-to-all-start.3 = ((f32[16,24,128]{2,1,0:T(8,128)}), f32[16,24,128]{2,1,0:T(8,128)S(1)}, u32[]{:S(2)}, u32[]{:S(2)}) async-start(f32[16,24,128]{2,1,0:T(8,128)} %multiply_reduce_fusion.1), calls=%async_computation.3 | async-start | bytes 393216 | tf_op jit(solution)/shard_map/all_to_all | solution.py:592
  243.0 30.8 %all-to-all-start.6 = ((bf16[4,128,2048]{2,1,0:T(8,128)(2,1)}), bf16[4,128,2048]{2,1,0:T(8,128)(2,1)}, u32[]{:S(2)}, u32[]{:S(2)}) async-start(bf16[4,128,2048]{2,1,0:T(8,128)(2,1)} %bitcast.137), calls=%async_computation.6 | async-start | bytes 4194304 | tf_op jit(solution)/shard_map/all_to_all | solution.py:60
  247.4 197.8 %reduce-scatter.2.cloned.1.call-start = ((), (), s32[]{:S(2)}) async-start(), calls=%async_computation.13 | async-start | bytes 10027008 | tf_op jit(solution)/shard_map/reduce_scatter | solution.py:730
  282.0 29.9 %all-to-all-start.7 = ((bf16[4,128,2048]{2,1,0:T(8,128)(2,1)}), bf16[4,128,2048]{2,1,0:T(8,128)(2,1)}, u32[]{:S(2)}, u32[]{:S(2)}) async-start(bf16[4,128,2048]{2,1,0:T(8,128)(2,1)} %broadcast_in_dim.22), calls=%async_computation.7 | async-start | bytes 4194304 | tf_op jit(solution)/shard_map/all_to_all | solution.py:60
  291.8 25.5 %collective-permute-start.7 = (bf16[512,2048]{1,0:T(8,128)(2,1)}, bf16[512,2048]{1,0:T(8,128)(2,1)}, u32[]{:S(2)}, u32[]{:S(2)}) collective-permute-start(bf16[512,2048]{1,0:T(8,128)(2,1)} %convolution_convert_fusion.2.other_ref), channel_id=1, source_target_pairs={{0,8},{8,0},{1,9},{9,1},{2,10},{10,2},{3,11},{11,3},{4,12},{12,4},... | collective-permute-start | bytes 6291464 | tf_op jit(solution)/shard_map/ppermute | solution.py:56
  326.3 49.2 %collective-permute-start.8 = (bf16[128,2048]{1,0:T(8,128)(2,1)}, bf16[128,2048]{1,0:T(8,128)(2,1)}, u32[]{:S(2)}, u32[]{:S(2)}) collective-permute-start(bf16[128,2048]{1,0:T(8,128)(2,1)} %get-tuple-element.91), channel_id=1, source_target_pairs={{0,2},{2,4},{4,6},{6,0},{1,3},{3,5},{5,7},{7,1},{8,10},{10,12},{12... | collective-permute-start | bytes 1572872 | tf_op jit(solution)/shard_map/ppermute | solution.py:68
  326.7 48.8 %collective-permute-start.10 = (bf16[128,2048]{1,0:T(8,128)(2,1)}, bf16[128,2048]{1,0:T(8,128)(2,1)}, u32[]{:S(2)}, u32[]{:S(2)}) collective-permute-start(bf16[128,2048]{1,0:T(8,128)(2,1)} %get-tuple-element.92), channel_id=1, source_target_pairs={{0,6},{2,0},{4,2},{6,4},{1,7},{3,1},{5,3},{7,5},{8,14},{10,8},{12,... | collective-permute-start | bytes 1572872 | tf_op jit(solution)/shard_map/ppermute | solution.py:68
  329.0 46.5 %collective-permute-start.9 = (bf16[128,2048]{1,0:T(8,128)(2,1)}, bf16[128,2048]{1,0:T(8,128)(2,1)}, u32[]{:S(2)}, u32[]{:S(2)}) collective-permute-start(bf16[128,2048]{1,0:T(8,128)(2,1)} %get-tuple-element.93), channel_id=1, source_target_pairs={{0,4},{2,6},{4,0},{6,2},{1,5},{3,7},{5,1},{7,3},{8,12},{10,14},{12... | collective-permute-start | bytes 1572872 | tf_op jit(solution)/shard_map/ppermute | solution.py:68
  342.9 23.9 %all-to-all-start.8 = ((f32[16,32,128]{2,1,0:T(8,128)}), f32[16,32,128]{2,1,0:T(8,128)}, u32[]{:S(2)}, u32[]{:S(2)}) async-start(f32[16,32,128]{2,1,0:T(8,128)} %concatenate.24), calls=%async_computation.8 | async-start | bytes 524288 | tf_op jit(solution)/shard_map/all_to_all | solution.py:592
  368.7 13.7 %all-to-all-start.9 = ((f32[16,24,128]{2,1,0:T(8,128)}), f32[16,24,128]{2,1,0:T(8,128)S(1)}, u32[]{:S(2)}, u32[]{:S(2)}) async-start(f32[16,24,128]{2,1,0:T(8,128)} %multiply_reduce_fusion), calls=%async_computation.9 | async-start | bytes 393216 | tf_op jit(solution)/shard_map/all_to_all | solution.py:592
  395.8 14.3 %collective-permute-start.12 = (bf16[512,2048]{1,0:T(8,128)(2,1)}, bf16[512,2048]{1,0:T(8,128)(2,1)}, u32[]{:S(2)}, u32[]{:S(2)}) collective-permute-start(bf16[512,2048]{1,0:T(8,128)(2,1)} %convolution_convert_fusion.1.other_ref), channel_id=1, source_target_pairs={{0,8},{8,0},{1,9},{9,1},{2,10},{10,2},{3,11},{11,3},{4,12},{12,4},... | collective-permute-start | bytes 6291464 | tf_op jit(solution)/shard_map/ppermute | solution.py:56
  405.5 56.7 %all-to-all-start.10 = ((bf16[16,576,128]{2,1,0:T(8,128)(2,1)}), bf16[16,576,128]{2,1,0:T(8,128)(2,1)}, u32[]{:S(2)}, u32[]{:S(2)}) async-start(bf16[16,576,128]{2,1,0:T(8,128)(2,1)} %bitcast.133), calls=%async_computation.11 | async-start | bytes 4718592 | tf_op jit(solution)/shard_map/all_to_all | solution.py:592
  416.0 15.1 %collective-permute-start.13 = (bf16[128,2048]{1,0:T(8,128)(2,1)}, bf16[128,2048]{1,0:T(8,128)(2,1)S(1)}, u32[]{:S(2)}, u32[]{:S(2)}) collective-permute-start(bf16[128,2048]{1,0:T(8,128)(2,1)} %get-tuple-element.88), channel_id=1, source_target_pairs={{0,2},{2,4},{4,6},{6,0},{1,3},{3,5},{5,7},{7,1},{8,10},{10,12},{12... | collective-permute-start | bytes 1572872 | tf_op jit(solution)/shard_map/ppermute | solution.py:68
  416.7 14.6 %collective-permute-start.15 = (bf16[128,2048]{1,0:T(8,128)(2,1)}, bf16[128,2048]{1,0:T(8,128)(2,1)S(1)}, u32[]{:S(2)}, u32[]{:S(2)}) collective-permute-start(bf16[128,2048]{1,0:T(8,128)(2,1)} %get-tuple-element.89), channel_id=1, source_target_pairs={{0,6},{2,0},{4,2},{6,4},{1,7},{3,1},{5,3},{7,5},{8,14},{10,8},{12,... | collective-permute-start | bytes 1572872 | tf_op jit(solution)/shard_map/ppermute | solution.py:68
  418.7 24.3 %collective-permute-start.14 = (bf16[128,2048]{1,0:T(8,128)(2,1)}, bf16[128,2048]{1,0:T(8,128)(2,1)}, u32[]{:S(2)}, u32[]{:S(2)}) collective-permute-start(bf16[128,2048]{1,0:T(8,128)(2,1)} %get-tuple-element.90), channel_id=1, source_target_pairs={{0,4},{2,6},{4,0},{6,2},{1,5},{3,7},{5,1},{7,3},{8,12},{10,14},{12... | collective-permute-start | bytes 1572872 | tf_op jit(solution)/shard_map/ppermute | solution.py:68
  424.5 47.6 %collective-permute-start.11 = (bf16[128,2048]{1,0:T(8,128)(2,1)}, bf16[128,2048]{1,0:T(8,128)(2,1)}, u32[]{:S(2)}, u32[]{:S(2)}) collective-permute-start(bf16[128,2048]{1,0:T(8,128)(2,1)} %get-tuple-element.78), channel_id=1, source_target_pairs={{0,0},{1,8},{8,1},{9,9},{2,2},{3,10},{10,3},{11,11},{4,4},{5,12},{... | collective-permute-start | bytes 1572872 | tf_op jit(solution)/shard_map/ppermute | solution.py:52
  456.3 15.8 %collective-permute-start.16 = (bf16[128,2048]{1,0:T(8,128)(2,1)}, bf16[128,2048]{1,0:T(8,128)(2,1)S(1)}, u32[]{:S(2)}, u32[]{:S(2)}) collective-permute-start(bf16[128,2048]{1,0:T(8,128)(2,1)} %add_convert_fusion.4), channel_id=1, source_target_pairs={{0,0},{1,8},{8,1},{9,9},{2,2},{3,10},{10,3},{11,11},{4,4},{5,12},{... | collective-permute-start | bytes 1572872 | tf_op jit(solution)/shard_map/ppermute | solution.py:52
  465.3 13.9 %all-to-all-start.11 = ((f32[16,8,128]{2,1,0:T(8,128)}), f32[16,8,128]{2,1,0:T(8,128)S(1)}, u32[]{:S(2)}, u32[]{:S(2)}) async-start(f32[16,8,128]{2,1,0:T(8,128)} %broadcast_in_dim.25), calls=%async_computation.12 | async-start | bytes 131072 | tf_op jit(solution)/shard_map/all_to_all | solution.py:800
  (96 other events, 934.3 us)
Sparse Core Ops, SparseCore 0:
  11.6 51.9 all-gather.6
  66.4 81.7 all-gather.4
  277.0 88.9 reduce-scatter.1

commit v4 on v3

--- a/solution.py
+++ b/solution.py
@@ -68,13 +68,51 @@
     return lax.ppermute(a, "y", [(i, (i + step) % 4) for i in range(4)])
 
 
-def gather_rows(mine):
-    own = over_y(spread(mine)).reshape(HALF, -1)
+def gather_rows(spread_rows):
+    own = over_y(spread_rows).reshape(HALF, -1)
     return own, swap_core(own)
 
 
-def sum_rows(low):
-    return jnp.sum(over_y(low.reshape(4, CHUNK, D)).astype(f32), axis=0)
+def parts_of_rows(low):
+    return over_y(low.reshape(4, CHUNK, D))
+
+
+def norm_kernel(parts_ref, inputs_ref, middle_ref, out_ref):
+    middle = inputs_ref[...].astype(f32)
+    for k in range(4):
+        middle = middle + parts_ref[k].astype(f32)
+    middle_ref[...] = middle
+    inv = lax.rsqrt(jnp.mean(middle * middle, axis=-1, keepdims=True) + norm_eps)
+    low = (middle * inv).astype(bf16)
+    for k in range(4):
+        out_ref[k] = low
+
+
+def norm_back_kernel(parts_ref, middle_ref, cot_ref, grad_ref, out_ref):
+    middle = middle_ref[...]
+    inv = lax.rsqrt(jnp.mean(middle * middle, axis=-1, keepdims=True) + norm_eps)
+    unit = middle * inv
+    shaped = parts_ref[0].astype(f32)
+    for k in range(1, 4):
+        shaped = shaped + parts_ref[k].astype(f32)
+    grad = cot_ref[...].astype(f32) + inv * (
+        shaped - unit * jnp.mean(shaped * unit, axis=-1, keepdims=True)
+    )
+    grad_ref[...] = grad
+    low = grad.astype(bf16)
+    for k in range(4):
+        out_ref[k] = low
+
+
+def on_rows(kernel, *args):
+    return pl.pallas_call(
+        kernel,
+        out_shape=[
+            jax.ShapeDtypeStruct((CHUNK, D), f32),
+            jax.ShapeDtypeStruct((4, CHUNK, D), bf16),
+        ],
+        compiler_params=pltpu.CompilerParams(vmem_limit_bytes=32 * 1024 * 1024),
+    )(*args)
 
 
 def sum_rows_apart(low):
@@ -90,7 +128,7 @@
     return out
 
 
-def scatter_rows(partial, between=None, total=sum_rows, later=None):
+def scatter_rows(partial, between=None, total=parts_of_rows, later=None):
     send = partial(1, None)
     got = swap_core(send)
     if later is not None:
@@ -480,21 +518,24 @@
         out_ref[k, 0, lo:hi, :] = tile[:, k * CHUNK : (k + 1) * CHUNK].astype(bf16)
 
 
-def mlp_grads_kernel(other_ref, a0, a1, g0, g1, gu0, gu1, h0, h1, out_ref, scr):
+def mlp_grads_kernel(core_ref, other_ref, a0, a1, g0, g1, gu0, gu1, h0, h1, out_ref, scr):
     @pl.when(pl.program_id(0) == 0)
     def turn():
         for half, (gu, h) in enumerate(((gu0, h0), (gu1, h1))):
             cols = slice(half * HALF, (half + 1) * HALF)
-            scr[:FFP, cols] = turned(gu[:, :FFP])
-            scr[FFP : 2 * FFP, cols] = turned(gu[:, FFP:])
+            for j in range(FFP // TILE):
+                rows = slice(j * TILE, (j + 1) * TILE)
+                later = slice(FFP + j * TILE, FFP + (j + 1) * TILE)
+                scr[rows, cols] = turned(gu[:, 2 * j * TILE : (2 * j + 1) * TILE])
+                scr[later, cols] = turned(gu[:, (2 * j + 1) * TILE : (2 * j + 2) * TILE])
             scr[2 * FFP :, cols] = turned(h[...])
 
-    for lo, hi, left, right in ((0, 2 * FFP, a0, a1), (2 * FFP, 3 * FFP, g0, g1)):
+    for lo, hi, left, right in ((0, 2 * FFP, a0, a1), (2 * FFP, 3 * FFP, g0.at[0], g1.at[0])):
         tile = matmul(scr[lo:hi, :HALF], left[...]) + matmul(scr[lo:hi, HALF:], right[...])
         store_owners(out_ref, lo, hi, tile)
 
 
-def out_grads_kernel(other_ref, g0, g1, rows_ref, out_ref, scr):
+def out_grads_kernel(core_ref, other_ref, g0, g1, rows_ref, out_ref, scr):
     @pl.when(pl.program_id(0) == 0)
     def turn():
         scr[...] = turned(rows_ref[...])
@@ -503,7 +544,7 @@
     store_owners(out_ref, 0, VW, tile)
 
 
-def proj_grads_kernel(other_ref, a0, a1, out_grad_ref, proj_ref, out_ref, scr):
+def proj_grads_kernel(core_ref, other_ref, a0, a1, out_grad_ref, proj_ref, out_ref, scr):
     @pl.when(pl.program_id(0) == 0)
     def turn():
         scr[:VW] = turned(proj_ref[:, :VW])
@@ -514,25 +555,87 @@
     store_owners(out_ref, VW, VW + PW, tile)
 
 
-def grads(kernel, height, other, tiled, whole, turned_rows, blocks=()):
+def grads(kernel, height, place, other, tiled, whole, turned_rows, blocks=(), split=()):
     def by_owner(n):
-        return pl.BlockSpec((2, 1, n, CHUNK), lambda i: (0, i, 0, 0))
+        return pl.BlockSpec((2, 1, n, CHUNK), lambda i, core: (0, i, 0, 0))
 
     def full(a):
-        return pl.BlockSpec(a.shape, lambda i: (0,) * a.ndim)
-
+        return pl.BlockSpec(a.shape, lambda i, core: (0,) * a.ndim)
+
+    in_specs = [pl.BlockSpec(memory_space=pl.ANY)]
+    in_specs += [pl.BlockSpec((HALF, TILE), lambda i, core: (0, i))] * len(tiled)
+    operands = list(tiled)
+    for a in split:
+        in_specs += [
+            pl.BlockSpec((1, HALF, TILE), lambda i, core: (core[0], 0, i)),
+            pl.BlockSpec((1, HALF, TILE), lambda i, core: (1 - core[0], 0, i)),
+        ]
+        operands += [a, a]
+    in_specs += [by_owner(a.shape[2]) for a in blocks] + [full(a) for a in whole]
     return pl.pallas_call(
         kernel,
-        grid=(D // TILE,),
+        grid_spec=pltpu.PrefetchScalarGridSpec(
+            num_scalar_prefetch=1,
+            grid=(D // TILE,),
+            in_specs=in_specs,
+            out_specs=by_owner(height),
+            scratch_shapes=[pltpu.VMEM((turned_rows, ROWS), bf16)],
+        ),
         out_shape=jax.ShapeDtypeStruct((2, 8, height, CHUNK), bf16),
-        in_specs=[pl.BlockSpec(memory_space=pl.ANY)]
-        + [pl.BlockSpec((HALF, TILE), lambda i: (0, i))] * len(tiled)
-        + [by_owner(a.shape[2]) for a in blocks]
-        + [full(a) for a in whole],
-        out_specs=by_owner(height),
-        scratch_shapes=[pltpu.VMEM((turned_rows, ROWS), bf16)],
         compiler_params=pltpu.CompilerParams(vmem_limit_bytes=48 * 1024 * 1024),
-    )(other, *tiled, *blocks, *whole)
+    )(place, other, *operands, *blocks, *whole)
+
+
+def mlp_kernel(
+    core_ref, a0, a1, g0, g1, gate_ref, up_ref, down_ref,
+    h0, h1, gu0, gu1, gateup_out, down_out,
+):
+    weights = [ref[0].reshape(D, TILE) for ref in (gate_ref, up_ref, down_ref)]
+    gateup_out[:, :TILE] = weights[0]
+    gateup_out[:, TILE:] = weights[1]
+    down_out[...] = weights[2]
+    for a, g, h, gu in ((a0, g0, h0, gu0), (a1, g1, h1, gu1)):
+        gate = matmul(a[...], weights[0])
+        up = matmul(a[...], weights[1])
+        grad = matmul(g[0], weights[2])
+        sigmoid = jax.nn.sigmoid(gate)
+        silu = gate * sigmoid
+        h[...] = (silu * up).astype(bf16)
+        gu[:, :TILE] = (grad * up * (sigmoid * (1.0 + gate * (1.0 - sigmoid)))).astype(bf16)
+        gu[:, TILE:] = (grad * silu).astype(bf16)
+
+
+def mlp(place, acts, grad, every):
+    steps = FFP // TILE
+
+    def cols(part):
+        return pl.BlockSpec(
+            (1, N_GROUPS, CHUNK, TILE), lambda j, core: (core[0], 0, 0, part * steps + j)
+        )
+
+    hidden = pl.BlockSpec((HALF, TILE), lambda j, core: (0, j))
+
+    def wide(n, width):
+        return pl.BlockSpec((n, width), lambda j, core: (0, j))
+
+    return pl.pallas_call(
+        mlp_kernel,
+        grid_spec=pltpu.PrefetchScalarGridSpec(
+            num_scalar_prefetch=1,
+            grid=(steps,),
+            in_specs=[pl.BlockSpec((HALF, D), lambda j, core: (0, 0))] * 2
+            + [
+                pl.BlockSpec((1, HALF, D), lambda j, core: (core[0], 0, 0)),
+                pl.BlockSpec((1, HALF, D), lambda j, core: (1 - core[0], 0, 0)),
+                cols(0), cols(1), cols(2),
+            ],
+            out_specs=[hidden] * 2 + [wide(HALF, 2 * TILE)] * 2 + [wide(D, 2 * TILE), wide(D, TILE)],
+        ),
+        out_shape=[jax.ShapeDtypeStruct((HALF, FFP), bf16)] * 2
+        + [jax.ShapeDtypeStruct((HALF, 2 * FFP), bf16)] * 2
+        + [jax.ShapeDtypeStruct((D, 2 * FFP), bf16), jax.ShapeDtypeStruct((D, FFP), bf16)],
+        compiler_params=pltpu.CompilerParams(vmem_limit_bytes=56 * 1024 * 1024),
+    )(place, *acts, grad, grad, every, every, every)
 
 
 def project_kernel(core_ref, a0, a1, w_ref, out_ref, acc):
@@ -636,22 +739,14 @@
     cot = both[1]
     inputs = tokens.astype(f32)
     unit_one, inv_one = unit_norm(inputs)
-    acts_one = gather_rows(unit_one.astype(bf16))
-    grad_mlp = gather_rows(after(cot, acts_one[0]))
-    every_mlp = gather_weights(after(gateup_part, acts_one[0]))
+    acts_one = gather_rows(spread(unit_one.astype(bf16)))
+    grad_mlp = lax.all_gather(after(after(cot, acts_one[0]), every_attn), ("core", "y")).reshape(2, HALF, D)
     proj = project(place, acts_one, every_attn)
     attn_w = own_slice(after(every_attn, proj))
     first_own = lax.dynamic_index_in_dim(attn_w, owner, 0, False)[:, VW : VW + PW].astype(f32).T
     attn_w = attn_w.reshape(D, AW)
     out_w = attn_w[:, :VW]
     proj_w = attn_w[:, VW : VW + PW]
-    mlp_w = own_slice(every_mlp).reshape(D, 3 * FFP)
-    gateup_w = mlp_w[:, : 2 * FFP]
-    down_w = mlp_w[:, 2 * FFP :]
-    gateup_own = lax.dynamic_slice(
-        every_mlp, (core, owner, 0, 0), (1, 1, CHUNK, 2 * FFP)
-    ).reshape(CHUNK, 2 * FFP)
-    gateup_own = gateup_own.T
 
     ends = jnp.cumsum(row_lengths)
 
@@ -676,7 +771,12 @@
         [pltpu.VMEM((ROWS, PW), bf16)],
         2,
     )(idx, proj)[0]
-    slices = exchange(after(own_state, grad_mlp[0]).reshape(N_GROUPS, STATE_ROWS // N_GROUPS, DV))
+    every_mlp = gather_weights(after(gateup_part, own_state))
+    gateup_own = lax.dynamic_slice(
+        every_mlp, (core, owner, 0, 0), (1, 1, CHUNK, 2 * FFP)
+    ).reshape(CHUNK, 2 * FFP)
+    gateup_own = gateup_own.T
+    slices = exchange(own_state.reshape(N_GROUPS, STATE_ROWS // N_GROUPS, DV))
     slices = jnp.sum(carry[:, :, None, None] * slices[None], axis=1)
     state = exchange(slices).reshape(STATE_ROWS, DV)
     num, den = call(
@@ -696,50 +796,29 @@
         5,
     )(idx, proj, num, after(den, attn_w), state)
 
-    middle = after(inputs, mlp_w) + scatter_rows(
-        rows_of(halves_of(attn_rows), out_w, ((1,), (1,)))
-    )
-    unit_two, inv_two = unit_norm(middle)
-    acts_two = gather_rows(unit_two.astype(bf16))
-    hidden = []
-    grad_gate_up = []
-    for acts, grad in zip(acts_two, grad_mlp):
-        gate_up = matmul(acts, gateup_w)
-        grad_hidden = matmul(grad, down_w)
-        gate = gate_up[:, :FFP]
-        up = gate_up[:, FFP:]
-        sigmoid = jax.nn.sigmoid(gate)
-        silu = gate * sigmoid
-        hidden.append((silu * up).astype(bf16))
-        dsilu = sigmoid * (1.0 + gate * (1.0 - sigmoid))
-        grad_gate_up.append(
-            jnp.concatenate([grad_hidden * up * dsilu, grad_hidden * silu], axis=1).astype(bf16)
-        )
+    middle, spread_two = on_rows(
+        norm_kernel, scatter_rows(rows_of(halves_of(attn_rows), out_w, ((1,), (1,)))), inputs
+    )
+    acts_two = gather_rows(spread_two)
+    hid0, hid1, gu0, gu1, gateup_w, down_w = mlp(place, acts_two, grad_mlp, every_mlp)
+    hidden = [hid0, hid1]
+    grad_gate_up = [gu0, gu1]
 
     late = []
 
     def mlp_grads(send, low):
         mlp_grad = grads(
-            mlp_grads_kernel, 3 * FFP, low, acts_two + grad_mlp, (*grad_gate_up, *hidden), 3 * FFP
+            mlp_grads_kernel, 3 * FFP, place, low, acts_two, (*grad_gate_up, *hidden), 3 * FFP,
+            split=(grad_mlp,),
         ).reshape(N_GROUPS * 3 * FFP, CHUNK)
         late.append(mlp_grad)
 
-    shaped_two = scatter_rows(
-        rows_of(grad_gate_up, gateup_w, ((1,), (1,))), mlp_grads
-    )
-    mlp_grad = lax.psum_scatter(after(late[0], shaped_two), GROUPS, scatter_dimension=0, tiled=True)
-    grad_out = cot.astype(f32)
-    grad_mid = grad_out + unit_norm_back(shaped_two, unit_two, inv_two)
-    grad_attn = gather_rows(grad_mid.astype(bf16))
-
-    mixed_own, mixed_other = [
-        matmul(after(hidden[half], shaped_two), down_w, ((1,), (1,))).astype(bf16) for half in (0, 1)
-    ]
+    grad_mid, spread_grad = on_rows(
+        norm_back_kernel, scatter_rows(rows_of(grad_gate_up, gateup_w, ((1,), (1,))), mlp_grads), middle, cot
+    )
+    mlp_grad = lax.psum_scatter(after(late[0], grad_mid), GROUPS, scatter_dimension=0, tiled=True)
+    grad_attn = gather_rows(spread_grad)
     grad_low = jnp.concatenate([matmul(a, out_w).astype(bf16) for a in grad_attn])
-    grad_low = after(after(grad_low, mixed_own), mixed_other)
-    mixed_other = swap_core(mixed_other)
-    mixed_low = (mixed_own.astype(f32) + mixed_other.astype(f32)).astype(bf16)
-    mixed = middle + sum_rows_apart(after(mixed_low, grad_attn[1]))
     own_grad, gn, gd = call(
         query_state_kernel,
         [
@@ -762,30 +841,37 @@
     )
     den_group = jnp.sum(slices[:, STATE_ROWS // N_GROUPS :], axis=0)
     slices = jnp.sum(back[:, :, None, None] * slices[None, :, : STATE_ROWS // N_GROUPS], axis=1)
-    output_grad = grads(out_grads_kernel, VW, own_grad, grad_attn, (attn_rows,), VW)
+    output_grad = grads(out_grads_kernel, VW, place, slices, grad_attn, (attn_rows,), VW)
     grad_state = exchange(slices).reshape(STATE_ROWS, DV)
-    mlp_grad_own = cross(after(mlp_grad, grad_state))
     gqk, gv = call(
         attend_back_inside_kernel,
         [jax.ShapeDtypeStruct((ROWS, QK), f32), jax.ShapeDtypeStruct((ROWS, VW), f32)],
         [pltpu.VMEM((ROWS, PW), bf16)],
         4,
     )(idx, proj, gn, gd)
+    mlp_grad_own = cross(after(mlp_grad, grad_state))
     grad_proj = call(
         attend_back_kernel,
         [jax.ShapeDtypeStruct((ROWS, PW), bf16)],
         [pltpu.VMEM((ROWS, PW), bf16), pltpu.VMEM((ROWS, QK), f32), pltpu.VMEM((ROWS, VW), f32)],
         8,
-    )(idx, proj, gn, after(after(gd, output_grad), mixed), gqk, gv, state, grad_state)[0]
+    )(idx, proj, gn, after(gd, output_grad), gqk, gv, state, grad_state)[0]
 
     def proj_grads(send, low):
         attn_grad = grads(
-            proj_grads_kernel, VW + PW, send, acts_one, (grad_proj,), PW, (output_grad,)
+            proj_grads_kernel, VW + PW, place, place, acts_one, (grad_proj,), PW, (output_grad,)
         ).reshape(N_GROUPS, VW + PW, CHUNK)
         late.append(exchange(attn_grad))
-
+        mixed_parts = [
+            matmul(after(a, low), down_w, ((1,), (1,))).astype(bf16) for a in hidden
+        ]
+        other = swap_core(mixed_parts[1])
+        late.append((mixed_parts[0].astype(f32) + other.astype(f32)).astype(bf16))
+
+
+    shaped_one = scatter_rows(rows_of(halves_of(grad_proj), proj_w, ((1,), (1,))), proj_grads, sum_rows_apart)
+    mixed = middle + sum_rows_apart(after(late[2], shaped_one))
     mixed = cross(mixed.astype(bf16))
-    shaped_one = scatter_rows(rows_of(halves_of(grad_proj), proj_w, ((1,), (1,))), proj_grads, sum_rows_apart)
     grad_tokens = grad_mid + unit_norm_back(shaped_one, unit_one, inv_one)
     grad_tokens = cross(grad_tokens.astype(bf16)).astype(f32)
     deep = plain(

time: 500 us -> 482 us (0.964)
  blocking collectives: 56.1 us -> 103 us
  waiting for transfers between devices: 104 us -> 78.3 us
  starting transfers between devices: 101 us -> 76 us
  matrix products: 51 us -> 30.9 us
  Pallas kernels: 67.4 us -> 86.4 us
  other arithmetic: 35.7 us -> 26.1 us
    all_to_all x4 -> x2, waiting for transfers between devices: 53 us -> 17.7 us  [over_y(): return lax.all_to_all(a, 'y', 0, 0)]
    all_to_all x2 -> x3, blocking collectives: 56.1 us -> 86.3 us  [over_y(): return lax.all_to_all(a, 'y', 0, 0)]
    dot_general x14 -> x10, matrix products: 51 us -> 30.9 us  [matmul(): return lax.dot_general(a, b, (dims, ((), ())), preferred_element_type=f32)]
    pallas_call x3 -> x6, Pallas kernels: 29 us -> 46.8 us  [the longest x3 26.4 us: grads(): pl.pallas_call(kernel, grid_spec=pltpu.PrefetchScalarGridSpec(num_scalar_...]
    all_to_all x0 -> x1, blocking collectives: none -> 16.5 us  [exchange(): return lax.all_to_all(a, GROUPS, 0, 0)]
    all_to_all x5 -> x4, starting transfers between devices: 33.3 us -> 20.9 us  [exchange(): return lax.all_to_all(a, GROUPS, 0, 0)]
    unnamed x178 -> x163, local copies, waits for them, and re-layouts: 30 us -> 39.7 us
    all_to_all x4 -> x2, starting transfers between devices: 17.6 us -> 8.45 us  [over_y(): return lax.all_to_all(a, 'y', 0, 0)]
  transfers between devices with their start and end apart: 32 -> 29, of which waited for: 15 -> 14; matrix products, arithmetic and copies ran while one was open for 18% -> 13% of each run, Pallas kernels for 13% -> 14%
where the time goes in v4:
time: 482 us; the launch traced here: 474 us
  blocking collectives  103 us (21%)
  Pallas kernels  86.4 us (18%)
  waiting for transfers between devices  78.3 us (16%)
  starting transfers between devices  76 us (16%)
  local copies, waits for them, and re-layouts  56.1 us (12%)
  matrix products  30.9 us (6%)
  other arithmetic  26.1 us (5%)
  between operations  17.6 us (4%)
    all_to_all x3, blocking collectives, over_y(): return lax.all_to_all(a, 'y', 0, 0)  86.3 us
    unnamed x163, local copies, waits for them, and re-layouts  39.7 us
    dot_general x10, matrix products, matmul(): return lax.dot_general(a, b, (dims, ((), ())), preferred_element_type=f32)  30.9 us
    pallas_call x3, Pallas kernels, grads(): pl.pallas_call(kernel, grid_spec=pltpu.PrefetchScalarGridSpec(num_scalar_...  26.4 us
    ppermute x5, starting transfers between devices, cross(): return lax.ppermute(a, ('core', 'x_hi'), CROSS)  26.1 us
    all_to_all x4, starting transfers between devices, exchange(): return lax.all_to_all(a, GROUPS, 0, 0)  20.9 us
    ppermute x7, waiting for transfers between devices, swap_core(): return lax.ppermute(a, 'core', FLIP)  17.8 us
    all_to_all x2, waiting for transfers between devices, over_y(): return lax.all_to_all(a, 'y', 0, 0)  17.7 us
  transfers between devices with their start and end apart: 29, of which 14 were waited for; matrix products, arithmetic and copies ran while one was open for 13% of the time, Pallas kernels for 14%

profile of v4, /device:TPU:1, one launch (start us, length us, event | category | flops | bytes accessed | tf_op | source)
XLA Modules:
  0.0 474.2 jit_solution(5670334077670025786)
XLA Ops:
  12.8 6.0 %collective-permute-start = (bf16[2,128,2048]{2,1,0:T(8,128)(2,1)S(1)}, bf16[2,128,2048]{2,1,0:T(8,128)(2,1)S(1)}, u32[]{:S(2)}, u32[]{:S(2)}) collective-permute-start(bf16[2,128,2048]{2,1,0:T(8,128)(2,1)S(1)} %pad_maximum_fusion), channel_id=1, source_target_pairs={{0,0},{1,8},{8,1},{9,9},{2,2},{3,10},{10,3},{11,11},{4,4},{5,12},{... | collective-permute-start | bytes 3145736 | tf_op jit(solution)/shard_map/ppermute | solution.py:52
  18.8 13.9 %collective-permute-done = bf16[2,128,2048]{2,1,0:T(8,128)(2,1)S(1)} collective-permute-done((bf16[2,128,2048]{2,1,0:T(8,128)(2,1)S(1)}, bf16[2,128,2048]{2,1,0:T(8,128)(2,1)S(1)}, u32[]{:S(2)}, u32[]{:S(2)}) %collective-permute-start) | collective-permute-done | bytes 1048608 | tf_op jit(solution)/shard_map/ppermute | solution.py:52
  41.7 12.3 %all-to-all-done = bf16[4,128,2048]{2,1,0:T(8,128)(2,1)S(1)} async-done(((bf16[4,128,2048]{2,1,0:T(8,128)(2,1)}), bf16[4,128,2048]{2,1,0:T(8,128)(2,1)S(1)}, u32[]{:S(2)}, u32[]{:S(2)}) %all-to-all-start) | async-done | bytes 2097184 | tf_op jit(solution)/shard_map/all_to_all | solution.py:60
  55.3 8.3 %all-gather.7.cloned.1.call-done = bf16[4096,640]{1,0:T(8,128)(2,1)} async-done(((bf16[128,640]{1,0:T(8,128)(2,1)}), bf16[4096,640]{1,0:T(8,128)(2,1)}) %all-gather.7.cloned.1.call-update) | async-done | bytes 5242896 | tf_op jit(solution)/shard_map/all_gather | solution.py:729
  69.7 7.2 %shard_map.365.p_ref.other_ref = bf16[1024,320]{1,0:T(8,128)(2,1)S(1)} custom-call(s32[1]{0:T(128)} %bitcast.5.core_ref.other_ref, bf16[512,2048]{1,0:T(8,128)(2,1)S(1)} %bitcast.92, bf16[512,2048]{1,0:T(8,128)(2,1)} %collective-permute-done.1.a1, bf16[2,16,128,640]{3,2,1,0:T(8,128)(2,1)} %bitcast.117), custom_call_target="tpu_custom_call" | custom-call | tf_op jit(solution)/shard_map/pallas_call | solution.py:658
  85.8 7.0 %all-to-all-done.1 = f32[16,24,128]{2,1,0:T(8,128)} async-done(((f32[16,24,128]{2,1,0:T(8,128)}), f32[16,24,128]{2,1,0:T(8,128)}, u32[]{:S(2)}, u32[]{:S(2)}) %all-to-all-start.1) | async-done | bytes 196640 | tf_op jit(solution)/shard_map/all_to_all | solution.py:695
  125.6 29.5 %all_to_all.55.parts_ref = bf16[4,128,2048]{2,1,0:T(8,128)(2,1)S(1)} all-to-all(bf16[4,128,2048]{2,1,0:T(8,128)(2,1)S(1)} %bitcast.127), channel_id=1, replica_groups=mesh['x_lo'=2,'z'=4,'core'=2,'y'=4,'x_hi'=2] {'y'}, dimensions={0} | all-to-all | bytes 4194304 | tf_op jit(solution)/shard_map/all_to_all | solution.py:60
  156.6 27.8 %all_to_all.56 = bf16[4,128,2048]{2,1,0:T(8,128)(2,1)} all-to-all(bf16[4,128,2048]{2,1,0:T(8,128)(2,1)S(1)} %get-tuple-element.60), channel_id=1, replica_groups=mesh['x_lo'=2,'z'=4,'core'=2,'y'=4,'x_hi'=2] {'y'}, dimensions={0} | all-to-all | bytes 4194304 | tf_op jit(solution)/shard_map/all_to_all | solution.py:60
  191.7 17.4 %shard_map.376 = (bf16[512,768]{1,0:T(8,128)(2,1)}, bf16[512,768]{1,0:T(8,128)(2,1)}, bf16[512,1536]{1,0:T(8,128)(2,1)}, bf16[512,1536]{1,0:T(8,128)(2,1)}, bf16...) custom-call(s32[1]{0:T(128)} %bitcast.5.core_ref.other_ref, bf16[512,2048]{1,0:T(8,128)(2,1)} %bitcast.19.a0, ...), custom_call_target="tpu_custom_call" | custom-call | tf_op jit(solution)/shard_map/pallas_call | solution.py:621
  209.0 6.8 %convolution_convert_fusion.4 = bf16[512,2048]{1,0:T(8,128)(2,1)S(1)} fusion(bf16[512,1536]{1,0:T(8,128)(2,1)} %get-tuple-element.63.gu1, bf16[2048,1536]{1,0:T(8,128)(2,1)} %get-tuple-element.62), kind=kOutput, calls=%fused_computation.11 | convolution fusion | flops 3222274048 | bytes 9961472 | tf_op jit(solution)/shard_map/dot_general | solution.py:157
  234.5 15.6 %shard_map.386 = bf16[2,8,2304,128]{3,2,1,0:T(8,128)(2,1)} custom-call(s32[1]{0:T(128)} %bitcast.5.core_ref.other_ref, bf16[512,2048]{1,0:T(8,128)(2,1)} %add_convert_fusion.2.other_ref, bf16[512,2048]{1,0:T(8,128)(2,1)} %bitcast.19.a0, bf16[512,2048]{1,0:T(8,128)(2,1)} %collective-permute-done.3.a1, bf16[2,512,2048]{2,1,0:T(8,128)(2,1)} %bitcast.114, ...), custom_call_target="tpu_custom_call" | custom-call | tf_op jit(solution)/shard_map/pallas_call | solution.py:575
  250.1 5.4 %all-to-all-done.5.parts_ref = bf16[4,128,2048]{2,1,0:T(8,128)(2,1)} async-done(((bf16[4,128,2048]{2,1,0:T(8,128)(2,1)}), bf16[4,128,2048]{2,1,0:T(8,128)(2,1)}, u32[]{:S(2)}, u32[]{:S(2)}) %all-to-all-start.5) | async-done | bytes 2097184 | tf_op jit(solution)/shard_map/all_to_all | solution.py:60
  261.5 29.0 %all_to_all.57 = bf16[4,128,2048]{2,1,0:T(8,128)(2,1)S(1)} all-to-all(bf16[4,128,2048]{2,1,0:T(8,128)(2,1)} %copy-done.29), channel_id=1, replica_groups=mesh['x_lo'=2,'z'=4,'core'=2,'y'=4,'x_hi'=2] {'y'}, dimensions={0} | all-to-all | bytes 4194304 | tf_op jit(solution)/shard_map/all_to_all | solution.py:60
  303.5 16.5 %all_to_all.58 = f32[16,32,128]{2,1,0:T(8,128)S(1)} all-to-all(f32[16,32,128]{2,1,0:T(8,128)S(1)} %concatenate.14), channel_id=1, replica_groups=mesh['x_lo'=2,'z'=4,'core'=2,'y'=4,'x_hi'=2] {'x_hi','x_lo','z'}, dimensions={0} | all-to-all | bytes 524288 | tf_op jit(solution)/shard_map/all_to_all | solution.py:695
  321.8 4.8 %all-to-all-start.8 = ((f32[16,24,128]{2,1,0:T(8,128)}), f32[16,24,128]{2,1,0:T(8,128)}, u32[]{:S(2)}, u32[]{:S(2)}) async-start(f32[16,24,128]{2,1,0:T(8,128)} %multiply_reduce_fusion.other_ref), calls=%async_computation.8 | async-start | bytes 393216 | tf_op jit(solution)/shard_map/all_to_all | solution.py:695
  328.0 6.8 %shard_map.381 = (f32[1024,64]{1,0:T(8,128)S(1)}, f32[1024,256]{1,0:T(8,128)S(1)}) custom-call(s32[14]{0:T(128)S(1)} %concatenate.12.idx_ref, bf16[1024,320]{1,0:T(8,128)(2,1)S(1)} %copy-done.2, f32[1024,256]{1,0:T(8,128)S(1)} %copy-done.19, f32[1024,2]{1,0:T(8,128)S(1)} %get-tuple-element.69.a_ref.gd_ref), custom_call_target="tpu_custom_call" | custom-call | tf_op jit(solution)/shard_map/pallas_call | solution.py:846
  348.5 6.7 %shard_map.382.proj_ref = bf16[1024,320]{1,0:T(8,128)(2,1)S(1)} custom-call(s32[14]{0:T(128)S(1)} %concatenate.12.idx_ref, bf16[1024,320]{1,0:T(8,128)(2,1)S(1)} %copy-done.2, f32[1024,256]{1,0:T(8,128)S(1)} %copy-done.20, f32[1024,2]{1,0:T(8,128)S(1)} %copy-done.11, f32[1024,64]{1,0:T(8,128)S(1)} %copy-done.56, f32[1024,256]{1,0:T(8,128)S(1)} %copy-done.48, ...), custom_call_target="tpu_custom_call" | custom-call | tf_op jit(solution)/shard_map/pallas_call | solution.py:853
  364.4 5.3 %convolution_convert_fusion.1 = bf16[512,2048]{1,0:T(8,128)(2,1)} fusion(bf16[512,768]{1,0:T(8,128)(2,1)} %shard_map.384, bf16[2048,768]{1,0:T(8,128)(2,1)} %get-tuple-element.73), kind=kOutput, calls=%fused_computation.8 | convolution fusion | flops 1611661312 | bytes 6029312 | tf_op jit(solution)/shard_map/dot_general | solution.py:157
  381.1 7.2 %shard_map.390 = bf16[2,8,576,128]{3,2,1,0:T(8,128)(2,1)} custom-call(s32[1]{0:T(128)} %bitcast.5.core_ref.other_ref, s32[1]{0:T(128)} %bitcast.5.core_ref.other_ref, bf16[512,2048]{1,0:T(8,128)(2,1)S(1)} %bitcast.93, bf16[512,2048]{1,0:T(8,128)(2,1)} %collective-permute-done.1.a1, bf16[2,8,256,128]{3,2,1,0:T(8,128)(2,1)S(1)} %copy-done.6, ...), custom_call_target="tpu_custom_call" | custom-call | tf_op jit(solution)/shard_map/pallas_call | solution.py:575
  388.3 7.1 %all-to-all-start.9 = ((bf16[16,576,128]{2,1,0:T(8,128)(2,1)}), bf16[16,576,128]{2,1,0:T(8,128)(2,1)}, u32[]{:S(2)}, u32[]{:S(2)}) async-start(bf16[16,576,128]{2,1,0:T(8,128)(2,1)} %bitcast.126), calls=%async_computation.10 | async-start | bytes 4718592 | tf_op jit(solution)/shard_map/all_to_all | solution.py:695
  416.5 6.7 %collective-permute-start.16 = (bf16[2304,128]{1,0:T(8,128)(2,1)}, bf16[2304,128]{1,0:T(8,128)(2,1)S(1)}, u32[]{:S(2)}, u32[]{:S(2)}) collective-permute-start(bf16[2304,128]{1,0:T(8,128)(2,1)} %shard_map.388), channel_id=1, source_target_pairs={{0,0},{1,8},{8,1},{9,9},{2,2},{3,10},{10,3},{11,11},{4,4},{5,12},{... | collective-permute-start | bytes 1769480 | tf_op jit(solution)/shard_map/ppermute | solution.py:52
  427.7 9.8 %collective-permute-done.12 = bf16[128,2048]{1,0:T(8,128)(2,1)} collective-permute-done((bf16[128,2048]{1,0:T(8,128)(2,1)}, bf16[128,2048]{1,0:T(8,128)(2,1)}, u32[]{:S(2)}, u32[]{:S(2)}) %collective-permute-start.12) | collective-permute-done | bytes 524320 | tf_op jit(solution)/shard_map/ppermute | solution.py:68
  439.4 6.1 %collective-permute-start.14 = (bf16[128,2048]{1,0:T(8,128)(2,1)S(1)}, bf16[128,2048]{1,0:T(8,128)(2,1)S(1)}, u32[]{:S(2)}, u32[]{:S(2)}) collective-permute-start(bf16[128,2048]{1,0:T(8,128)(2,1)S(1)} %add_convert_fusion.5), channel_id=1, source_target_pairs={{0,0},{1,8},{8,1},{9,9},{2,2},{3,10},{10,3},{11,11},{4,4},{5,12},{... | collective-permute-start | bytes 1572872 | tf_op jit(solution)/shard_map/ppermute | solution.py:52
  456.2 5.0 %collective-permute-start.17 = (bf16[576,128]{1,0:T(8,128)(2,1)S(1)}, bf16[576,128]{1,0:T(8,128)(2,1)S(1)}, u32[]{:S(2)}, u32[]{:S(2)}) collective-permute-start(bf16[576,128]{1,0:T(8,128)(2,1)S(1)} %convert_element_type.187), channel_id=1, source_target_pairs={{0,0},{1,8},{8,1},{9,9},{2,2},{3,10},{10,3},{11,11},{4,4},{5,12},{... | collective-permute-start | bytes 442376 | tf_op jit(solution)/shard_map/ppermute | solution.py:52
  (289 shorter events, 188.2 us)
Async XLA Ops:
  7.2 56.4 %all-gather.7.cloned.1.call-start = ((), (), s32[]{:S(2)}) async-start(), calls=%async_computation.13 | async-start | bytes 5406720 | tf_op jit(solution)/shard_map/all_gather | solution.py:729
  12.8 19.9 %collective-permute-start = (bf16[2,128,2048]{2,1,0:T(8,128)(2,1)S(1)}, bf16[2,128,2048]{2,1,0:T(8,128)(2,1)S(1)}, u32[]{:S(2)}, u32[]{:S(2)}) collective-permute-start(bf16[2,128,2048]{2,1,0:T(8,128)(2,1)S(1)} %pad_maximum_fusion), channel_id=1, source_target_pairs={{0,0},{1,8},{8,1},{9,9},{2,2},{3,10},{10,3},{11,11},{4,4},{5,12},{... | collective-permute-start | bytes 3145736 | tf_op jit(solution)/shard_map/ppermute | solution.py:52
  34.6 19.4 %all-to-all-start = ((bf16[4,128,2048]{2,1,0:T(8,128)(2,1)}), bf16[4,128,2048]{2,1,0:T(8,128)(2,1)S(1)}, u32[]{:S(2)}, u32[]{:S(2)}) async-start(bf16[4,128,2048]{2,1,0:T(8,128)(2,1)} %broadcast_in_dim.13), calls=%async_computation | async-start | bytes 4194304 | tf_op jit(solution)/shard_map/all_to_all | solution.py:60
  38.6 148.9 %all-gather.9.cloned.1.call-start = ((), (), s32[]{:S(2)}) async-start(), calls=%async_computation.14 | async-start | bytes 4718592 | tf_op jit(solution)/shard_map/all_gather | solution.py:743
  63.6 128.1 %all-gather.11.cloned.1.call-start = ((), (), s32[]{:S(2)}) async-start(), calls=%async_computation.15 | async-start | bytes 19464192 | tf_op jit(solution)/shard_map/all_gather | solution.py:729
  81.2 11.6 %all-to-all-start.1 = ((f32[16,24,128]{2,1,0:T(8,128)}), f32[16,24,128]{2,1,0:T(8,128)}, u32[]{:S(2)}, u32[]{:S(2)}) async-start(f32[16,24,128]{2,1,0:T(8,128)} %bitcast.99), calls=%async_computation.1 | async-start | bytes 393216 | tf_op jit(solution)/shard_map/all_to_all | solution.py:695
  94.8 13.6 %all-to-all-start.2 = ((f32[16,24,128]{2,1,0:T(8,128)}), f32[16,24,128]{2,1,0:T(8,128)}, u32[]{:S(2)}, u32[]{:S(2)}) async-start(f32[16,24,128]{2,1,0:T(8,128)} %multiply_reduce_fusion.1), calls=%async_computation.2 | async-start | bytes 393216 | tf_op jit(solution)/shard_map/all_to_all | solution.py:695
  184.4 7.2 %collective-permute-start.3 = (bf16[512,2048]{1,0:T(8,128)(2,1)}, bf16[512,2048]{1,0:T(8,128)(2,1)}, u32[]{:S(2)}, u32[]{:S(2)}) collective-permute-start(bf16[512,2048]{1,0:T(8,128)(2,1)} %bitcast.19.a0), channel_id=1, source_target_pairs={{0,8},{8,0},{1,9},{9,1},{2,10},{10,2},{3,11},{11,3},{4,12},{12,4},... | collective-permute-start | bytes 6291464 | tf_op jit(solution)/shard_map/ppermute | solution.py:56
  224.9 30.6 %all-to-all-start.5 = ((bf16[4,128,2048]{2,1,0:T(8,128)(2,1)}), bf16[4,128,2048]{2,1,0:T(8,128)(2,1)}, u32[]{:S(2)}, u32[]{:S(2)}) async-start(bf16[4,128,2048]{2,1,0:T(8,128)(2,1)} %bitcast.128), calls=%async_computation.5 | async-start | bytes 4194304 | tf_op jit(solution)/shard_map/all_to_all | solution.py:60
  229.3 186.0 %reduce-scatter.2.cloned.1.call-start = ((), (), s32[]{:S(2)}) async-start(), calls=%async_computation.12 | async-start | bytes 10027008 | tf_op jit(solution)/shard_map/reduce_scatter | solution.py:819
  321.8 22.1 %all-to-all-start.8 = ((f32[16,24,128]{2,1,0:T(8,128)}), f32[16,24,128]{2,1,0:T(8,128)}, u32[]{:S(2)}, u32[]{:S(2)}) async-start(f32[16,24,128]{2,1,0:T(8,128)} %multiply_reduce_fusion.other_ref), calls=%async_computation.8 | async-start | bytes 393216 | tf_op jit(solution)/shard_map/all_to_all | solution.py:695
  369.7 35.3 %collective-permute-start.10 = (bf16[512,2048]{1,0:T(8,128)(2,1)}, bf16[512,2048]{1,0:T(8,128)(2,1)}, u32[]{:S(2)}, u32[]{:S(2)}) collective-permute-start(bf16[512,2048]{1,0:T(8,128)(2,1)} %convolution_convert_fusion.1), channel_id=1, source_target_pairs={{0,8},{8,0},{1,9},{9,1},{2,10},{10,2},{3,11},{11,3},{4,12},{12,4},... | collective-permute-start | bytes 6291464 | tf_op jit(solution)/shard_map/ppermute | solution.py:56
  376.3 23.2 %collective-permute-start.7 = (bf16[128,2048]{1,0:T(8,128)(2,1)}, bf16[128,2048]{1,0:T(8,128)(2,1)}, u32[]{:S(2)}, u32[]{:S(2)}) collective-permute-start(bf16[128,2048]{1,0:T(8,128)(2,1)} %get-tuple-element.103), channel_id=1, source_target_pairs={{0,2},{2,4},{4,6},{6,0},{1,3},{3,5},{5,7},{7,1},{8,10},{10,12},{12... | collective-permute-start | bytes 1572872 | tf_op jit(solution)/shard_map/ppermute | solution.py:68
  376.8 22.8 %collective-permute-start.9 = (bf16[128,2048]{1,0:T(8,128)(2,1)}, bf16[128,2048]{1,0:T(8,128)(2,1)}, u32[]{:S(2)}, u32[]{:S(2)}) collective-permute-start(bf16[128,2048]{1,0:T(8,128)(2,1)} %get-tuple-element.104), channel_id=1, source_target_pairs={{0,6},{2,0},{4,2},{6,4},{1,7},{3,1},{5,3},{7,5},{8,14},{10,8},{12,... | collective-permute-start | bytes 1572872 | tf_op jit(solution)/shard_map/ppermute | solution.py:68
  379.0 23.2 %collective-permute-start.8 = (bf16[128,2048]{1,0:T(8,128)(2,1)S(1)}, bf16[128,2048]{1,0:T(8,128)(2,1)}, u32[]{:S(2)}, u32[]{:S(2)}) collective-permute-start(bf16[128,2048]{1,0:T(8,128)(2,1)S(1)} %get-tuple-element.105), channel_id=1, source_target_pairs={{0,4},{2,6},{4,0},{6,2},{1,5},{3,7},{5,1},{7,3},{8,12},{10,14},{12... | collective-permute-start | bytes 1572872 | tf_op jit(solution)/shard_map/ppermute | solution.py:68
  388.3 59.5 %all-to-all-start.9 = ((bf16[16,576,128]{2,1,0:T(8,128)(2,1)}), bf16[16,576,128]{2,1,0:T(8,128)(2,1)}, u32[]{:S(2)}, u32[]{:S(2)}) async-start(bf16[16,576,128]{2,1,0:T(8,128)(2,1)} %bitcast.126), calls=%async_computation.10 | async-start | bytes 4718592 | tf_op jit(solution)/shard_map/all_to_all | solution.py:695
  411.4 16.2 %collective-permute-start.11 = (bf16[128,2048]{1,0:T(8,128)(2,1)}, bf16[128,2048]{1,0:T(8,128)(2,1)}, u32[]{:S(2)}, u32[]{:S(2)}) collective-permute-start(bf16[128,2048]{1,0:T(8,128)(2,1)} %get-tuple-element.100), channel_id=1, source_target_pairs={{0,2},{2,4},{4,6},{6,0},{1,3},{3,5},{5,7},{7,1},{8,10},{10,12},{12... | collective-permute-start | bytes 1572872 | tf_op jit(solution)/shard_map/ppermute | solution.py:68
  412.0 15.6 %collective-permute-start.13 = (bf16[128,2048]{1,0:T(8,128)(2,1)}, bf16[128,2048]{1,0:T(8,128)(2,1)}, u32[]{:S(2)}, u32[]{:S(2)}) collective-permute-start(bf16[128,2048]{1,0:T(8,128)(2,1)} %get-tuple-element.101), channel_id=1, source_target_pairs={{0,6},{2,0},{4,2},{6,4},{1,7},{3,1},{5,3},{7,5},{8,14},{10,8},{12,... | collective-permute-start | bytes 1572872 | tf_op jit(solution)/shard_map/ppermute | solution.py:68
  414.1 23.4 %collective-permute-start.12 = (bf16[128,2048]{1,0:T(8,128)(2,1)}, bf16[128,2048]{1,0:T(8,128)(2,1)}, u32[]{:S(2)}, u32[]{:S(2)}) collective-permute-start(bf16[128,2048]{1,0:T(8,128)(2,1)} %get-tuple-element.102), channel_id=1, source_target_pairs={{0,4},{2,6},{4,0},{6,2},{1,5},{3,7},{5,1},{7,3},{8,12},{10,14},{12... | collective-permute-start | bytes 1572872 | tf_op jit(solution)/shard_map/ppermute | solution.py:68
  416.5 29.0 %collective-permute-start.16 = (bf16[2304,128]{1,0:T(8,128)(2,1)}, bf16[2304,128]{1,0:T(8,128)(2,1)S(1)}, u32[]{:S(2)}, u32[]{:S(2)}) collective-permute-start(bf16[2304,128]{1,0:T(8,128)(2,1)} %shard_map.388), channel_id=1, source_target_pairs={{0,0},{1,8},{8,1},{9,9},{2,2},{3,10},{10,3},{11,11},{4,4},{5,12},{... | collective-permute-start | bytes 1769480 | tf_op jit(solution)/shard_map/ppermute | solution.py:52
  425.5 29.7 %collective-permute-start.15 = (bf16[128,2048]{1,0:T(8,128)(2,1)}, bf16[128,2048]{1,0:T(8,128)(2,1)S(1)}, u32[]{:S(2)}, u32[]{:S(2)}) collective-permute-start(bf16[128,2048]{1,0:T(8,128)(2,1)} %add_convert_fusion.4), channel_id=1, source_target_pairs={{0,0},{1,8},{8,1},{9,9},{2,2},{3,10},{10,3},{11,11},{4,4},{5,12},{... | collective-permute-start | bytes 1572872 | tf_op jit(solution)/shard_map/ppermute | solution.py:52
  439.4 16.8 %collective-permute-start.14 = (bf16[128,2048]{1,0:T(8,128)(2,1)S(1)}, bf16[128,2048]{1,0:T(8,128)(2,1)S(1)}, u32[]{:S(2)}, u32[]{:S(2)}) collective-permute-start(bf16[128,2048]{1,0:T(8,128)(2,1)S(1)} %add_convert_fusion.5), channel_id=1, source_target_pairs={{0,0},{1,8},{8,1},{9,9},{2,2},{3,10},{10,3},{11,11},{4,4},{5,12},{... | collective-permute-start | bytes 1572872 | tf_op jit(solution)/shard_map/ppermute | solution.py:52
  450.9 11.3 %all-to-all-start.10 = ((f32[16,8,128]{2,1,0:T(8,128)}), f32[16,8,128]{2,1,0:T(8,128)S(1)}, u32[]{:S(2)}, u32[]{:S(2)}) async-start(f32[16,8,128]{2,1,0:T(8,128)} %broadcast_in_dim.16), calls=%async_computation.11 | async-start | bytes 131072 | tf_op jit(solution)/shard_map/all_to_all | solution.py:886
  456.2 8.0 %collective-permute-start.17 = (bf16[576,128]{1,0:T(8,128)(2,1)S(1)}, bf16[576,128]{1,0:T(8,128)(2,1)S(1)}, u32[]{:S(2)}, u32[]{:S(2)}) collective-permute-start(bf16[576,128]{1,0:T(8,128)(2,1)S(1)} %convert_element_type.187), channel_id=1, source_target_pairs={{0,0},{1,8},{8,1},{9,9},{2,2},{3,10},{10,3},{11,11},{4,4},{5,12},{... | collective-permute-start | bytes 442376 | tf_op jit(solution)/shard_map/ppermute | solution.py:52
  (85 other events, 714.0 us)
Sparse Core Ops, SparseCore 0:
  11.6 51.9 all-gather.6
  65.9 31.4 all-gather.8
  100.1 77.4 all-gather.10
  261.6 88.4 reduce-scatter.1

commit v5 on v4

--- a/solution.py
+++ b/solution.py
@@ -342,7 +342,7 @@
             ga = gscr[r:end, cols].astype(f32)
             gn = ga / den
             gd = -jnp.sum(ga * att_ref[r:end, cols], axis=1, keepdims=True) / den
-            gn_ref[r:end, cols] = gn
+            gn_ref[r:end, cols] = gn.astype(bf16)
             gd_ref[r:end, head : head + 1] = gd
             one, two, scale = side(scr[r:end, VW:PW], 0, head)
             phi = one * two * scale * continues(idx_ref, r, end)
@@ -364,7 +364,7 @@
         back_all = matmul(u_all, mover(1, head)).astype(bf16)
         for r in range(0, ROWS, TILE):
             end = r + TILE
-            low_gn = gn_ref[r:end, cols].astype(bf16)
+            low_gn = gn_ref[r:end, cols]
             gd = gd_ref[r:end, head : head + 1]
             moved = matmul(scr[r:end, VW:PW], mover(0, head)).astype(bf16)
             s = matmul(moved, u_all[:end], ((1,), (1,)))
@@ -395,7 +395,7 @@
             gd = gd_ref[r:end, head : head + 1]
             one, two, scale = side(u, 0, head)
             left, right = sides_of(0, head)
-            grad = (dot_low_right(gn.astype(bf16), mat) + gd * vec) * cont * scale
+            grad = (dot_low_right(gn, mat) + gd * vec) * cont * scale
             acc = matmul((grad * two).astype(bf16), left, ((1,), (1,)))
             acc = acc + matmul((grad * one).astype(bf16), right, ((1,), (1,)))
             one, two, scale = side(u, 1, head)
@@ -535,24 +535,16 @@
         store_owners(out_ref, lo, hi, tile)
 
 
-def out_grads_kernel(core_ref, other_ref, g0, g1, rows_ref, out_ref, scr):
+def attn_grads_kernel(core_ref, other_ref, a0, a1, g0, g1, rows_ref, proj_ref, out_ref, scr):
     @pl.when(pl.program_id(0) == 0)
     def turn():
-        scr[...] = turned(rows_ref[...])
-
-    tile = matmul(scr[:, :HALF], g0[...]) + matmul(scr[:, HALF:], g1[...])
-    store_owners(out_ref, 0, VW, tile)
-
-
-def proj_grads_kernel(core_ref, other_ref, a0, a1, out_grad_ref, proj_ref, out_ref, scr):
-    @pl.when(pl.program_id(0) == 0)
-    def turn():
-        scr[:VW] = turned(proj_ref[:, :VW])
-        scr[VW:] = turned(proj_ref[:, VW:])
-
-    tile = matmul(scr[:, :HALF], a0[...]) + matmul(scr[:, HALF:], a1[...])
-    out_ref[:, 0, :VW, :] = out_grad_ref[:, 0]
-    store_owners(out_ref, VW, VW + PW, tile)
+        scr[:VW] = turned(rows_ref[...])
+        scr[VW : 2 * VW] = turned(proj_ref[:, :VW])
+        scr[2 * VW :] = turned(proj_ref[:, VW:])
+
+    for lo, hi, left, right in ((0, VW, g0, g1), (VW, VW + PW, a0, a1)):
+        tile = matmul(scr[lo:hi, :HALF], left[...]) + matmul(scr[lo:hi, HALF:], right[...])
+        store_owners(out_ref, lo, hi, tile)
 
 
 def grads(kernel, height, place, other, tiled, whole, turned_rows, blocks=(), split=()):
@@ -823,7 +815,7 @@
         query_state_kernel,
         [
             jax.ShapeDtypeStruct((STATE_ROWS, DV), f32),
-            jax.ShapeDtypeStruct((ROWS, VW), f32),
+            jax.ShapeDtypeStruct((ROWS, VW), bf16),
             jax.ShapeDtypeStruct((ROWS, LOCAL_HEADS), f32),
         ],
         [pltpu.VMEM((ROWS, PW), bf16), pltpu.VMEM((ROWS, VW), bf16)],
@@ -841,7 +833,6 @@
     )
     den_group = jnp.sum(slices[:, STATE_ROWS // N_GROUPS :], axis=0)
     slices = jnp.sum(back[:, :, None, None] * slices[None, :, : STATE_ROWS // N_GROUPS], axis=1)
-    output_grad = grads(out_grads_kernel, VW, place, slices, grad_attn, (attn_rows,), VW)
     grad_state = exchange(slices).reshape(STATE_ROWS, DV)
     gqk, gv = call(
         attend_back_inside_kernel,
@@ -855,11 +846,12 @@
         [jax.ShapeDtypeStruct((ROWS, PW), bf16)],
         [pltpu.VMEM((ROWS, PW), bf16), pltpu.VMEM((ROWS, QK), f32), pltpu.VMEM((ROWS, VW), f32)],
         8,
-    )(idx, proj, gn, after(gd, output_grad), gqk, gv, state, grad_state)[0]
+    )(idx, proj, gn, gd, gqk, gv, state, grad_state)[0]
 
     def proj_grads(send, low):
         attn_grad = grads(
-            proj_grads_kernel, VW + PW, place, place, acts_one, (grad_proj,), PW, (output_grad,)
+            attn_grads_kernel, VW + PW, place, place, acts_one + grad_attn,
+            (attn_rows, grad_proj), VW + PW,
         ).reshape(N_GROUPS, VW + PW, CHUNK)
         late.append(exchange(attn_grad))
         mixed_parts = [

time: 482 us -> 476 us (0.988)
    unnamed x163 -> x155, local copies, waits for them, and re-layouts: 39.7 us -> 37.4 us
    pallas_call x3 -> x2, Pallas kernels: 26.4 us -> 24.3 us  [grads(): pl.pallas_call(kernel, grid_spec=pltpu.PrefetchScalarGridSpec(num_scalar_...]
  transfers between devices with their start and end apart: 29 -> 29, of which waited for: 14 -> 14; matrix products, arithmetic and copies ran while one was open for 13% -> 14% of each run, Pallas kernels for 14% -> 13%
where the time goes in v5:
time: 476 us; the launch traced here: 468 us
  blocking collectives  103 us (22%)
  Pallas kernels  84.5 us (18%)
  waiting for transfers between devices  76.5 us (16%)
  starting transfers between devices  75.8 us (16%)
  local copies, waits for them, and re-layouts  54.7 us (11%)
  matrix products  30.1 us (6%)
  other arithmetic  26.2 us (6%)
  between operations  17.3 us (4%)
    all_to_all x3, blocking collectives, over_y(): return lax.all_to_all(a, 'y', 0, 0)  86.3 us
    unnamed x155, local copies, waits for them, and re-layouts  37.4 us
    dot_general x10, matrix products, matmul(): return lax.dot_general(a, b, (dims, ((), ())), preferred_element_type=f32)  30.1 us
    ppermute x5, starting transfers between devices, cross(): return lax.ppermute(a, ('core', 'x_hi'), CROSS)  26.2 us
    pallas_call x2, Pallas kernels, grads(): pl.pallas_call(kernel, grid_spec=pltpu.PrefetchScalarGridSpec(num_scalar_...  24.3 us
    all_to_all x4, starting transfers between devices, exchange(): return lax.all_to_all(a, GROUPS, 0, 0)  20.7 us
    ppermute x7, waiting for transfers between devices, swap_core(): return lax.ppermute(a, 'core', FLIP)  17.8 us
    all_to_all x2, waiting for transfers between devices, over_y(): return lax.all_to_all(a, 'y', 0, 0)  17.7 us
  transfers between devices with their start and end apart: 29, of which 14 were waited for; matrix products, arithmetic and copies ran while one was open for 14% of the time, Pallas kernels for 13%

profile of v5, /device:TPU:1, one launch (start us, length us, event | category | flops | bytes accessed | tf_op | source)
XLA Modules:
  0.0 468.3 jit_solution(1715479323093913762)
XLA Ops:
  12.8 6.0 %collective-permute-start = (bf16[2,128,2048]{2,1,0:T(8,128)(2,1)S(1)}, bf16[2,128,2048]{2,1,0:T(8,128)(2,1)S(1)}, u32[]{:S(2)}, u32[]{:S(2)}) collective-permute-start(bf16[2,128,2048]{2,1,0:T(8,128)(2,1)S(1)} %pad_maximum_fusion), channel_id=1, source_target_pairs={{0,0},{1,8},{8,1},{9,9},{2,2},{3,10},{10,3},{11,11},{4,4},{5,12},{... | collective-permute-start | bytes 3145736 | tf_op jit(solution)/shard_map/ppermute | solution.py:52
  18.8 13.6 %collective-permute-done = bf16[2,128,2048]{2,1,0:T(8,128)(2,1)S(1)} collective-permute-done((bf16[2,128,2048]{2,1,0:T(8,128)(2,1)S(1)}, bf16[2,128,2048]{2,1,0:T(8,128)(2,1)S(1)}, u32[]{:S(2)}, u32[]{:S(2)}) %collective-permute-start) | collective-permute-done | bytes 1048608 | tf_op jit(solution)/shard_map/ppermute | solution.py:52
  42.5 12.3 %all-to-all-done = bf16[4,128,2048]{2,1,0:T(8,128)(2,1)S(1)} async-done(((bf16[4,128,2048]{2,1,0:T(8,128)(2,1)}), bf16[4,128,2048]{2,1,0:T(8,128)(2,1)S(1)}, u32[]{:S(2)}, u32[]{:S(2)}) %all-to-all-start) | async-done | bytes 2097184 | tf_op jit(solution)/shard_map/all_to_all | solution.py:60
  56.0 7.5 %all-gather.7.cloned.1.call-done = bf16[4096,640]{1,0:T(8,128)(2,1)} async-done(((bf16[128,640]{1,0:T(8,128)(2,1)}), bf16[4096,640]{1,0:T(8,128)(2,1)}) %all-gather.7.cloned.1.call-update) | async-done | bytes 5242896 | tf_op jit(solution)/shard_map/all_gather | solution.py:721
  69.7 7.2 %shard_map.365.p_ref.other_ref = bf16[1024,320]{1,0:T(8,128)(2,1)S(1)} custom-call(s32[1]{0:T(128)} %bitcast.5.core_ref.other_ref, bf16[512,2048]{1,0:T(8,128)(2,1)S(1)} %bitcast.92, bf16[512,2048]{1,0:T(8,128)(2,1)} %collective-permute-done.1.a1, bf16[2,16,128,640]{3,2,1,0:T(8,128)(2,1)} %bitcast.114), custom_call_target="tpu_custom_call" | custom-call | tf_op jit(solution)/shard_map/pallas_call | solution.py:650
  85.8 7.0 %all-to-all-done.1 = f32[16,24,128]{2,1,0:T(8,128)} async-done(((f32[16,24,128]{2,1,0:T(8,128)}), f32[16,24,128]{2,1,0:T(8,128)}, u32[]{:S(2)}, u32[]{:S(2)}) %all-to-all-start.1) | async-done | bytes 196640 | tf_op jit(solution)/shard_map/all_to_all | solution.py:687
  125.9 29.4 %all_to_all.55.parts_ref = bf16[4,128,2048]{2,1,0:T(8,128)(2,1)S(1)} all-to-all(bf16[4,128,2048]{2,1,0:T(8,128)(2,1)S(1)} %bitcast.124), channel_id=1, replica_groups=mesh['x_lo'=2,'z'=4,'core'=2,'y'=4,'x_hi'=2] {'y'}, dimensions={0} | all-to-all | bytes 4194304 | tf_op jit(solution)/shard_map/all_to_all | solution.py:60
  156.9 27.8 %all_to_all.56 = bf16[4,128,2048]{2,1,0:T(8,128)(2,1)} all-to-all(bf16[4,128,2048]{2,1,0:T(8,128)(2,1)S(1)} %get-tuple-element.60), channel_id=1, replica_groups=mesh['x_lo'=2,'z'=4,'core'=2,'y'=4,'x_hi'=2] {'y'}, dimensions={0} | all-to-all | bytes 4194304 | tf_op jit(solution)/shard_map/all_to_all | solution.py:60
  191.7 17.3 %shard_map.376 = (bf16[512,768]{1,0:T(8,128)(2,1)}, bf16[512,768]{1,0:T(8,128)(2,1)}, bf16[512,1536]{1,0:T(8,128)(2,1)}, bf16[512,1536]{1,0:T(8,128)(2,1)}, bf16...) custom-call(s32[1]{0:T(128)} %bitcast.5.core_ref.other_ref, bf16[512,2048]{1,0:T(8,128)(2,1)} %bitcast.19.a0, ...), custom_call_target="tpu_custom_call" | custom-call | tf_op jit(solution)/shard_map/pallas_call | solution.py:613
  209.0 6.8 %convolution_convert_fusion.4 = bf16[512,2048]{1,0:T(8,128)(2,1)S(1)} fusion(bf16[512,1536]{1,0:T(8,128)(2,1)} %get-tuple-element.63.gu1, bf16[2048,1536]{1,0:T(8,128)(2,1)} %get-tuple-element.62), kind=kOutput, calls=%fused_computation.11 | convolution fusion | flops 3222274048 | bytes 9961472 | tf_op jit(solution)/shard_map/dot_general | solution.py:157
  220.1 4.7 %add_convert_fusion.2.other_ref = bf16[512,2048]{1,0:T(8,128)(2,1)} fusion(bf16[512,2048]{1,0:T(8,128)(2,1)S(1)} %collective-permute-done.4, bf16[512,1536]{1,0:T(8,128)(2,1)S(1)} %copy-done.31, bf16[2048,1536]{1,0:T(8,128)(2,1)S(1)} %copy-done.73), kind=kOutput, calls=%fused_computation.3 | convolution fusion | flops 3224371200 | bytes 12058624 | tf_op jit(solution)/shard_map/dot_general | solution.py:157
  234.4 15.6 %shard_map.384 = bf16[2,8,2304,128]{3,2,1,0:T(8,128)(2,1)} custom-call(s32[1]{0:T(128)} %bitcast.5.core_ref.other_ref, bf16[512,2048]{1,0:T(8,128)(2,1)} %add_convert_fusion.2.other_ref, bf16[512,2048]{1,0:T(8,128)(2,1)} %bitcast.19.a0, bf16[512,2048]{1,0:T(8,128)(2,1)} %collective-permute-done.3.a1, bf16[2,512,2048]{2,1,0:T(8,128)(2,1)} %bitcast.111, ...), custom_call_target="tpu_custom_call" | custom-call | tf_op jit(solution)/shard_map/pallas_call | solution.py:567
  250.0 5.4 %all-to-all-done.5.parts_ref = bf16[4,128,2048]{2,1,0:T(8,128)(2,1)} async-done(((bf16[4,128,2048]{2,1,0:T(8,128)(2,1)}), bf16[4,128,2048]{2,1,0:T(8,128)(2,1)}, u32[]{:S(2)}, u32[]{:S(2)}) %all-to-all-start.5) | async-done | bytes 2097184 | tf_op jit(solution)/shard_map/all_to_all | solution.py:60
  261.5 29.0 %all_to_all.57 = bf16[4,128,2048]{2,1,0:T(8,128)(2,1)S(1)} all-to-all(bf16[4,128,2048]{2,1,0:T(8,128)(2,1)} %copy-done.18), channel_id=1, replica_groups=mesh['x_lo'=2,'z'=4,'core'=2,'y'=4,'x_hi'=2] {'y'}, dimensions={0} | all-to-all | bytes 4194304 | tf_op jit(solution)/shard_map/all_to_all | solution.py:60
  304.0 16.9 %all_to_all.58 = f32[16,32,128]{2,1,0:T(8,128)S(1)} all-to-all(f32[16,32,128]{2,1,0:T(8,128)S(1)} %concatenate.14), channel_id=1, replica_groups=mesh['x_lo'=2,'z'=4,'core'=2,'y'=4,'x_hi'=2] {'x_hi','x_lo','z'}, dimensions={0} | all-to-all | bytes 524288 | tf_op jit(solution)/shard_map/all_to_all | solution.py:687
  328.4 6.9 %shard_map.379 = (f32[1024,64]{1,0:T(8,128)S(1)}, f32[1024,256]{1,0:T(8,128)S(1)}) custom-call(s32[14]{0:T(128)S(1)} %concatenate.12.idx_ref, bf16[1024,320]{1,0:T(8,128)(2,1)S(1)} %copy-done.2, bf16[1024,256]{1,0:T(8,128)(2,1)S(1)} %copy-done.20, f32[1024,2]{1,0:T(8,128)S(1)} %copy-done.22), custom_call_target="tpu_custom_call" | custom-call | tf_op jit(solution)/shard_map/pallas_call | solution.py:837
  340.4 6.7 %shard_map.380.proj_ref = bf16[1024,320]{1,0:T(8,128)(2,1)S(1)} custom-call(s32[14]{0:T(128)S(1)} %concatenate.12.idx_ref, bf16[1024,320]{1,0:T(8,128)(2,1)S(1)} %copy-done.2, bf16[1024,256]{1,0:T(8,128)(2,1)S(1)} %copy-done.20, f32[1024,2]{1,0:T(8,128)S(1)} %copy-done.23, f32[1024,64]{1,0:T(8,128)S(1)} %copy-done.45, f32[1024,256]{1,0:T(8,128)S(1)} %copy-done.39, ...), custom_call_target="tpu_custom_call" | custom-call | tf_op jit(solution)/shard_map/pallas_call | solution.py:844
  356.5 5.3 %convolution_convert_fusion.1 = bf16[512,2048]{1,0:T(8,128)(2,1)} fusion(bf16[512,768]{1,0:T(8,128)(2,1)} %shard_map.382, bf16[2048,768]{1,0:T(8,128)(2,1)} %get-tuple-element.73), kind=kOutput, calls=%fused_computation.8 | convolution fusion | flops 1611661312 | bytes 6029312 | tf_op jit(solution)/shard_map/dot_general | solution.py:157
  373.9 8.7 %shard_map.388 = bf16[2,8,576,128]{3,2,1,0:T(8,128)(2,1)} custom-call(s32[1]{0:T(128)} %bitcast.5.core_ref.other_ref, s32[1]{0:T(128)} %bitcast.5.core_ref.other_ref, bf16[512,2048]{1,0:T(8,128)(2,1)S(1)} %bitcast.93, bf16[512,2048]{1,0:T(8,128)(2,1)} %collective-permute-done.1.a1, bf16[512,2048]{1,0:T(8,128)(2,1)} %bitcast.127, ...), custom_call_target="tpu_custom_call" | custom-call | tf_op jit(solution)/shard_map/pallas_call | solution.py:567
  382.6 6.9 %all-to-all-start.9 = ((bf16[16,576,128]{2,1,0:T(8,128)(2,1)}), bf16[16,576,128]{2,1,0:T(8,128)(2,1)}, u32[]{:S(2)}, u32[]{:S(2)}) async-start(bf16[16,576,128]{2,1,0:T(8,128)(2,1)} %bitcast.123), calls=%async_computation.10 | async-start | bytes 4718592 | tf_op jit(solution)/shard_map/all_to_all | solution.py:687
  410.5 6.7 %collective-permute-start.16 = (bf16[2304,128]{1,0:T(8,128)(2,1)}, bf16[2304,128]{1,0:T(8,128)(2,1)S(1)}, u32[]{:S(2)}, u32[]{:S(2)}) collective-permute-start(bf16[2304,128]{1,0:T(8,128)(2,1)} %shard_map.386), channel_id=1, source_target_pairs={{0,0},{1,8},{8,1},{9,9},{2,2},{3,10},{10,3},{11,11},{4,4},{5,12},{... | collective-permute-start | bytes 1769480 | tf_op jit(solution)/shard_map/ppermute | solution.py:52
  421.7 9.8 %collective-permute-done.12 = bf16[128,2048]{1,0:T(8,128)(2,1)} collective-permute-done((bf16[128,2048]{1,0:T(8,128)(2,1)}, bf16[128,2048]{1,0:T(8,128)(2,1)}, u32[]{:S(2)}, u32[]{:S(2)}) %collective-permute-start.12) | collective-permute-done | bytes 524320 | tf_op jit(solution)/shard_map/ppermute | solution.py:68
  433.4 6.2 %collective-permute-start.14 = (bf16[128,2048]{1,0:T(8,128)(2,1)S(1)}, bf16[128,2048]{1,0:T(8,128)(2,1)S(1)}, u32[]{:S(2)}, u32[]{:S(2)}) collective-permute-start(bf16[128,2048]{1,0:T(8,128)(2,1)S(1)} %add_convert_fusion.5), channel_id=1, source_target_pairs={{0,0},{1,8},{8,1},{9,9},{2,2},{3,10},{10,3},{11,11},{4,4},{5,12},{... | collective-permute-start | bytes 1572872 | tf_op jit(solution)/shard_map/ppermute | solution.py:52
  450.6 5.0 %collective-permute-start.17 = (bf16[576,128]{1,0:T(8,128)(2,1)S(1)}, bf16[576,128]{1,0:T(8,128)(2,1)S(1)}, u32[]{:S(2)}, u32[]{:S(2)}) collective-permute-start(bf16[576,128]{1,0:T(8,128)(2,1)S(1)} %convert_element_type.187), channel_id=1, source_target_pairs={{0,0},{1,8},{8,1},{9,9},{2,2},{3,10},{10,3},{11,11},{4,4},{5,12},{... | collective-permute-start | bytes 442376 | tf_op jit(solution)/shard_map/ppermute | solution.py:52
  (279 shorter events, 181.8 us)
Async XLA Ops:
  7.2 56.4 %all-gather.7.cloned.1.call-start = ((), (), s32[]{:S(2)}) async-start(), calls=%async_computation.13 | async-start | bytes 5406720 | tf_op jit(solution)/shard_map/all_gather | solution.py:721
  12.8 19.7 %collective-permute-start = (bf16[2,128,2048]{2,1,0:T(8,128)(2,1)S(1)}, bf16[2,128,2048]{2,1,0:T(8,128)(2,1)S(1)}, u32[]{:S(2)}, u32[]{:S(2)}) collective-permute-start(bf16[2,128,2048]{2,1,0:T(8,128)(2,1)S(1)} %pad_maximum_fusion), channel_id=1, source_target_pairs={{0,0},{1,8},{8,1},{9,9},{2,2},{3,10},{10,3},{11,11},{4,4},{5,12},{... | collective-permute-start | bytes 3145736 | tf_op jit(solution)/shard_map/ppermute | solution.py:52
  35.1 19.6 %all-to-all-start = ((bf16[4,128,2048]{2,1,0:T(8,128)(2,1)}), bf16[4,128,2048]{2,1,0:T(8,128)(2,1)S(1)}, u32[]{:S(2)}, u32[]{:S(2)}) async-start(bf16[4,128,2048]{2,1,0:T(8,128)(2,1)} %broadcast_in_dim.13), calls=%async_computation | async-start | bytes 4194304 | tf_op jit(solution)/shard_map/all_to_all | solution.py:60
  39.4 148.2 %all-gather.9.cloned.1.call-start = ((), (), s32[]{:S(2)}) async-start(), calls=%async_computation.14 | async-start | bytes 4718592 | tf_op jit(solution)/shard_map/all_gather | solution.py:735
  63.6 128.1 %all-gather.11.cloned.1.call-start = ((), (), s32[]{:S(2)}) async-start(), calls=%async_computation.15 | async-start | bytes 19464192 | tf_op jit(solution)/shard_map/all_gather | solution.py:721
  81.2 11.6 %all-to-all-start.1 = ((f32[16,24,128]{2,1,0:T(8,128)}), f32[16,24,128]{2,1,0:T(8,128)}, u32[]{:S(2)}, u32[]{:S(2)}) async-start(f32[16,24,128]{2,1,0:T(8,128)} %bitcast.96), calls=%async_computation.1 | async-start | bytes 393216 | tf_op jit(solution)/shard_map/all_to_all | solution.py:687
  94.8 13.8 %all-to-all-start.2 = ((f32[16,24,128]{2,1,0:T(8,128)}), f32[16,24,128]{2,1,0:T(8,128)}, u32[]{:S(2)}, u32[]{:S(2)}) async-start(f32[16,24,128]{2,1,0:T(8,128)} %multiply_reduce_fusion.1), calls=%async_computation.2 | async-start | bytes 393216 | tf_op jit(solution)/shard_map/all_to_all | solution.py:687
  184.7 7.0 %collective-permute-start.3 = (bf16[512,2048]{1,0:T(8,128)(2,1)}, bf16[512,2048]{1,0:T(8,128)(2,1)}, u32[]{:S(2)}, u32[]{:S(2)}) collective-permute-start(bf16[512,2048]{1,0:T(8,128)(2,1)} %bitcast.19.a0), channel_id=1, source_target_pairs={{0,8},{8,0},{1,9},{9,1},{2,10},{10,2},{3,11},{11,3},{4,12},{12,4},... | collective-permute-start | bytes 6291464 | tf_op jit(solution)/shard_map/ppermute | solution.py:56
  224.9 30.6 %all-to-all-start.5 = ((bf16[4,128,2048]{2,1,0:T(8,128)(2,1)}), bf16[4,128,2048]{2,1,0:T(8,128)(2,1)}, u32[]{:S(2)}, u32[]{:S(2)}) async-start(bf16[4,128,2048]{2,1,0:T(8,128)(2,1)} %bitcast.128), calls=%async_computation.5 | async-start | bytes 4194304 | tf_op jit(solution)/shard_map/all_to_all | solution.py:60
  229.3 180.0 %reduce-scatter.2.cloned.1.call-start = ((), (), s32[]{:S(2)}) async-start(), calls=%async_computation.12 | async-start | bytes 10027008 | tf_op jit(solution)/shard_map/reduce_scatter | solution.py:811
  322.7 14.3 %all-to-all-start.8 = ((f32[16,24,128]{2,1,0:T(8,128)}), f32[16,24,128]{2,1,0:T(8,128)}, u32[]{:S(2)}, u32[]{:S(2)}) async-start(f32[16,24,128]{2,1,0:T(8,128)} %multiply_reduce_fusion), calls=%async_computation.8 | async-start | bytes 393216 | tf_op jit(solution)/shard_map/all_to_all | solution.py:687
  361.9 37.5 %collective-permute-start.10 = (bf16[512,2048]{1,0:T(8,128)(2,1)}, bf16[512,2048]{1,0:T(8,128)(2,1)}, u32[]{:S(2)}, u32[]{:S(2)}) collective-permute-start(bf16[512,2048]{1,0:T(8,128)(2,1)} %convolution_convert_fusion.1), channel_id=1, source_target_pairs={{0,8},{8,0},{1,9},{9,1},{2,10},{10,2},{3,11},{11,3},{4,12},{12,4},... | collective-permute-start | bytes 6291464 | tf_op jit(solution)/shard_map/ppermute | solution.py:56
  370.3 24.2 %collective-permute-start.7 = (bf16[128,2048]{1,0:T(8,128)(2,1)}, bf16[128,2048]{1,0:T(8,128)(2,1)}, u32[]{:S(2)}, u32[]{:S(2)}) collective-permute-start(bf16[128,2048]{1,0:T(8,128)(2,1)} %get-tuple-element.103), channel_id=1, source_target_pairs={{0,2},{2,4},{4,6},{6,0},{1,3},{3,5},{5,7},{7,1},{8,10},{10,12},{12... | collective-permute-start | bytes 1572872 | tf_op jit(solution)/shard_map/ppermute | solution.py:68
  370.8 23.7 %collective-permute-start.9 = (bf16[128,2048]{1,0:T(8,128)(2,1)}, bf16[128,2048]{1,0:T(8,128)(2,1)}, u32[]{:S(2)}, u32[]{:S(2)}) collective-permute-start(bf16[128,2048]{1,0:T(8,128)(2,1)} %get-tuple-element.104), channel_id=1, source_target_pairs={{0,6},{2,0},{4,2},{6,4},{1,7},{3,1},{5,3},{7,5},{8,14},{10,8},{12,... | collective-permute-start | bytes 1572872 | tf_op jit(solution)/shard_map/ppermute | solution.py:68
  373.0 23.5 %collective-permute-start.8 = (bf16[128,2048]{1,0:T(8,128)(2,1)}, bf16[128,2048]{1,0:T(8,128)(2,1)}, u32[]{:S(2)}, u32[]{:S(2)}) collective-permute-start(bf16[128,2048]{1,0:T(8,128)(2,1)} %get-tuple-element.105), channel_id=1, source_target_pairs={{0,4},{2,6},{4,0},{6,2},{1,5},{3,7},{5,1},{7,3},{8,12},{10,14},{12... | collective-permute-start | bytes 1572872 | tf_op jit(solution)/shard_map/ppermute | solution.py:68
  382.6 59.5 %all-to-all-start.9 = ((bf16[16,576,128]{2,1,0:T(8,128)(2,1)}), bf16[16,576,128]{2,1,0:T(8,128)(2,1)}, u32[]{:S(2)}, u32[]{:S(2)}) async-start(bf16[16,576,128]{2,1,0:T(8,128)(2,1)} %bitcast.123), calls=%async_computation.10 | async-start | bytes 4718592 | tf_op jit(solution)/shard_map/all_to_all | solution.py:687
  405.7 16.0 %collective-permute-start.11 = (bf16[128,2048]{1,0:T(8,128)(2,1)}, bf16[128,2048]{1,0:T(8,128)(2,1)}, u32[]{:S(2)}, u32[]{:S(2)}) collective-permute-start(bf16[128,2048]{1,0:T(8,128)(2,1)} %get-tuple-element.100), channel_id=1, source_target_pairs={{0,2},{2,4},{4,6},{6,0},{1,3},{3,5},{5,7},{7,1},{8,10},{10,12},{12... | collective-permute-start | bytes 1572872 | tf_op jit(solution)/shard_map/ppermute | solution.py:68
  406.3 15.4 %collective-permute-start.13 = (bf16[128,2048]{1,0:T(8,128)(2,1)}, bf16[128,2048]{1,0:T(8,128)(2,1)}, u32[]{:S(2)}, u32[]{:S(2)}) collective-permute-start(bf16[128,2048]{1,0:T(8,128)(2,1)} %get-tuple-element.101), channel_id=1, source_target_pairs={{0,6},{2,0},{4,2},{6,4},{1,7},{3,1},{5,3},{7,5},{8,14},{10,8},{12,... | collective-permute-start | bytes 1572872 | tf_op jit(solution)/shard_map/ppermute | solution.py:68
  408.4 23.1 %collective-permute-start.12 = (bf16[128,2048]{1,0:T(8,128)(2,1)}, bf16[128,2048]{1,0:T(8,128)(2,1)}, u32[]{:S(2)}, u32[]{:S(2)}) collective-permute-start(bf16[128,2048]{1,0:T(8,128)(2,1)} %get-tuple-element.102), channel_id=1, source_target_pairs={{0,4},{2,6},{4,0},{6,2},{1,5},{3,7},{5,1},{7,3},{8,12},{10,14},{12... | collective-permute-start | bytes 1572872 | tf_op jit(solution)/shard_map/ppermute | solution.py:68
  410.5 29.2 %collective-permute-start.16 = (bf16[2304,128]{1,0:T(8,128)(2,1)}, bf16[2304,128]{1,0:T(8,128)(2,1)S(1)}, u32[]{:S(2)}, u32[]{:S(2)}) collective-permute-start(bf16[2304,128]{1,0:T(8,128)(2,1)} %shard_map.386), channel_id=1, source_target_pairs={{0,0},{1,8},{8,1},{9,9},{2,2},{3,10},{10,3},{11,11},{4,4},{5,12},{... | collective-permute-start | bytes 1769480 | tf_op jit(solution)/shard_map/ppermute | solution.py:52
  419.5 30.0 %collective-permute-start.15 = (bf16[128,2048]{1,0:T(8,128)(2,1)}, bf16[128,2048]{1,0:T(8,128)(2,1)S(1)}, u32[]{:S(2)}, u32[]{:S(2)}) collective-permute-start(bf16[128,2048]{1,0:T(8,128)(2,1)} %add_convert_fusion.4), channel_id=1, source_target_pairs={{0,0},{1,8},{8,1},{9,9},{2,2},{3,10},{10,3},{11,11},{4,4},{5,12},{... | collective-permute-start | bytes 1572872 | tf_op jit(solution)/shard_map/ppermute | solution.py:52
  433.4 17.1 %collective-permute-start.14 = (bf16[128,2048]{1,0:T(8,128)(2,1)S(1)}, bf16[128,2048]{1,0:T(8,128)(2,1)S(1)}, u32[]{:S(2)}, u32[]{:S(2)}) collective-permute-start(bf16[128,2048]{1,0:T(8,128)(2,1)S(1)} %add_convert_fusion.5), channel_id=1, source_target_pairs={{0,0},{1,8},{8,1},{9,9},{2,2},{3,10},{10,3},{11,11},{4,4},{5,12},{... | collective-permute-start | bytes 1572872 | tf_op jit(solution)/shard_map/ppermute | solution.py:52
  445.1 11.4 %all-to-all-start.10 = ((f32[16,8,128]{2,1,0:T(8,128)}), f32[16,8,128]{2,1,0:T(8,128)S(1)}, u32[]{:S(2)}, u32[]{:S(2)}) async-start(f32[16,8,128]{2,1,0:T(8,128)} %broadcast_in_dim.16), calls=%async_computation.11 | async-start | bytes 131072 | tf_op jit(solution)/shard_map/all_to_all | solution.py:878
  450.6 8.0 %collective-permute-start.17 = (bf16[576,128]{1,0:T(8,128)(2,1)S(1)}, bf16[576,128]{1,0:T(8,128)(2,1)S(1)}, u32[]{:S(2)}, u32[]{:S(2)}) collective-permute-start(bf16[576,128]{1,0:T(8,128)(2,1)S(1)} %convert_element_type.187), channel_id=1, source_target_pairs={{0,0},{1,8},{8,1},{9,9},{2,2},{3,10},{10,3},{11,11},{4,4},{5,12},{... | collective-permute-start | bytes 442376 | tf_op jit(solution)/shard_map/ppermute | solution.py:52
  (81 other events, 686.5 us)
Sparse Core Ops, SparseCore 0:
  11.6 51.9 all-gather.6
  65.9 31.4 all-gather.8
  100.1 77.6 all-gather.10
  261.6 88.3 reduce-scatter.1

commit v6 on v5

--- a/solution.py
+++ b/solution.py
@@ -32,6 +32,7 @@
 HEAD_ROWS = 192
 STATE_ROWS = LOCAL_HEADS * HEAD_ROWS
 TILE = 256
+WIDE = 512
 
 norm_eps = 1e-05
 beta_one = 0.5
@@ -637,11 +638,11 @@
     def start():
         acc[...] = jnp.zeros_like(acc)
 
-    weight = w_ref[0].reshape(TILE, AW)[:, VW : VW + PW]
+    weight = w_ref[0].reshape(WIDE, AW)[:, VW : VW + PW]
     acc[:HALF] += matmul(a0[...], weight)
     acc[HALF:] += matmul(a1[...], weight)
 
-    @pl.when(step == D // TILE - 1)
+    @pl.when(step == D // WIDE - 1)
     def end():
         out_ref[...] = acc[...].astype(bf16)
 
@@ -651,9 +652,9 @@
         project_kernel,
         grid_spec=pltpu.PrefetchScalarGridSpec(
             num_scalar_prefetch=1,
-            grid=(D // TILE,),
-            in_specs=[pl.BlockSpec((HALF, TILE), lambda i, core: (0, i))] * 2
-            + [pl.BlockSpec((1, 2, CHUNK, AW), lambda i, core: (core[0], i, 0, 0))],
+            grid=(D // WIDE,),
+            in_specs=[pl.BlockSpec((HALF, WIDE), lambda i, core: (0, i))] * 2
+            + [pl.BlockSpec((1, WIDE // CHUNK, CHUNK, AW), lambda i, core: (core[0], i, 0, 0))],
             out_specs=pl.BlockSpec((ROWS, PW), lambda i, core: (0, 0)),
             scratch_shapes=[pltpu.VMEM((ROWS, PW), f32)],
         ),

time: 476 us -> 474 us (level)
  no operation moved by 1% of the time
where the time goes in v6:
time: 474 us; the launch traced here: 467 us
  blocking collectives  103 us (22%)
  Pallas kernels  82.5 us (17%)
  starting transfers between devices  77.8 us (16%)
  waiting for transfers between devices  74.8 us (16%)
  local copies, waits for them, and re-layouts  54.6 us (12%)
  matrix products  30.2 us (6%)
  other arithmetic  26.2 us (6%)
  between operations  17.3 us (4%)
    all_to_all x3, blocking collectives, over_y(): return lax.all_to_all(a, 'y', 0, 0)  86.2 us
    unnamed x155, local copies, waits for them, and re-layouts  37.3 us
    dot_general x10, matrix products, matmul(): return lax.dot_general(a, b, (dims, ((), ())), preferred_element_type=f32)  30.2 us
    ppermute x5, starting transfers between devices, cross(): return lax.ppermute(a, ('core', 'x_hi'), CROSS)  28.8 us
    pallas_call x2, Pallas kernels, grads(): pl.pallas_call(kernel, grid_spec=pltpu.PrefetchScalarGridSpec(num_scalar_...  24.3 us
    all_to_all x4, starting transfers between devices, exchange(): return lax.all_to_all(a, GROUPS, 0, 0)  20.8 us
    ppermute x7, waiting for transfers between devices, swap_core(): return lax.ppermute(a, 'core', FLIP)  17.8 us
    all_to_all x2, waiting for transfers between devices, over_y(): return lax.all_to_all(a, 'y', 0, 0)  17.7 us
  transfers between devices with their start and end apart: 29, of which 14 were waited for; matrix products, arithmetic and copies ran while one was open for 14% of the time, Pallas kernels for 13%

profile of v6, /device:TPU:1, one launch (start us, length us, event | category | flops | bytes accessed | tf_op | source)
XLA Modules:
  0.0 466.6 jit_solution(11464623688759290149)
XLA Ops:
  12.8 6.0 %collective-permute-start = (bf16[2,128,2048]{2,1,0:T(8,128)(2,1)S(1)}, bf16[2,128,2048]{2,1,0:T(8,128)(2,1)S(1)}, u32[]{:S(2)}, u32[]{:S(2)}) collective-permute-start(bf16[2,128,2048]{2,1,0:T(8,128)(2,1)S(1)} %pad_maximum_fusion), channel_id=1, source_target_pairs={{0,0},{1,8},{8,1},{9,9},{2,2},{3,10},{10,3},{11,11},{4,4},{5,12},{... | collective-permute-start | bytes 3145736 | tf_op jit(solution)/shard_map/ppermute | solution.py:53
  18.8 13.6 %collective-permute-done = bf16[2,128,2048]{2,1,0:T(8,128)(2,1)S(1)} collective-permute-done((bf16[2,128,2048]{2,1,0:T(8,128)(2,1)S(1)}, bf16[2,128,2048]{2,1,0:T(8,128)(2,1)S(1)}, u32[]{:S(2)}, u32[]{:S(2)}) %collective-permute-start) | collective-permute-done | bytes 1048608 | tf_op jit(solution)/shard_map/ppermute | solution.py:53
  42.5 12.3 %all-to-all-done = bf16[4,128,2048]{2,1,0:T(8,128)(2,1)S(1)} async-done(((bf16[4,128,2048]{2,1,0:T(8,128)(2,1)}), bf16[4,128,2048]{2,1,0:T(8,128)(2,1)S(1)}, u32[]{:S(2)}, u32[]{:S(2)}) %all-to-all-start) | async-done | bytes 2097184 | tf_op jit(solution)/shard_map/all_to_all | solution.py:61
  56.0 7.5 %all-gather.7.cloned.1.call-done = bf16[4096,640]{1,0:T(8,128)(2,1)} async-done(((bf16[128,640]{1,0:T(8,128)(2,1)}), bf16[4096,640]{1,0:T(8,128)(2,1)}) %all-gather.7.cloned.1.call-update) | async-done | bytes 5242896 | tf_op jit(solution)/shard_map/all_gather | solution.py:722
  69.7 5.2 %shard_map.365.p_ref.other_ref = bf16[1024,320]{1,0:T(8,128)(2,1)S(1)} custom-call(s32[1]{0:T(128)} %bitcast.5.core_ref.other_ref, bf16[512,2048]{1,0:T(8,128)(2,1)S(1)} %bitcast.92, bf16[512,2048]{1,0:T(8,128)(2,1)} %collective-permute-done.1.a1, bf16[2,16,128,640]{3,2,1,0:T(8,128)(2,1)} %bitcast.114), custom_call_target="tpu_custom_call" | custom-call | tf_op jit(solution)/shard_map/pallas_call | solution.py:651
  83.9 7.0 %all-to-all-done.1 = f32[16,24,128]{2,1,0:T(8,128)} async-done(((f32[16,24,128]{2,1,0:T(8,128)}), f32[16,24,128]{2,1,0:T(8,128)}, u32[]{:S(2)}, u32[]{:S(2)}) %all-to-all-start.1) | async-done | bytes 196640 | tf_op jit(solution)/shard_map/all_to_all | solution.py:688
  124.0 29.4 %all_to_all.55.parts_ref = bf16[4,128,2048]{2,1,0:T(8,128)(2,1)S(1)} all-to-all(bf16[4,128,2048]{2,1,0:T(8,128)(2,1)S(1)} %bitcast.124), channel_id=1, replica_groups=mesh['x_lo'=2,'z'=4,'core'=2,'y'=4,'x_hi'=2] {'y'}, dimensions={0} | all-to-all | bytes 4194304 | tf_op jit(solution)/shard_map/all_to_all | solution.py:61
  155.0 27.8 %all_to_all.56 = bf16[4,128,2048]{2,1,0:T(8,128)(2,1)} all-to-all(bf16[4,128,2048]{2,1,0:T(8,128)(2,1)S(1)} %get-tuple-element.60), channel_id=1, replica_groups=mesh['x_lo'=2,'z'=4,'core'=2,'y'=4,'x_hi'=2] {'y'}, dimensions={0} | all-to-all | bytes 4194304 | tf_op jit(solution)/shard_map/all_to_all | solution.py:61
  189.8 17.3 %shard_map.376 = (bf16[512,768]{1,0:T(8,128)(2,1)}, bf16[512,768]{1,0:T(8,128)(2,1)}, bf16[512,1536]{1,0:T(8,128)(2,1)}, bf16[512,1536]{1,0:T(8,128)(2,1)}, bf16...) custom-call(s32[1]{0:T(128)} %bitcast.5.core_ref.other_ref, bf16[512,2048]{1,0:T(8,128)(2,1)} %bitcast.19.a0, ...), custom_call_target="tpu_custom_call" | custom-call | tf_op jit(solution)/shard_map/pallas_call | solution.py:614
  207.2 6.8 %convolution_convert_fusion.4 = bf16[512,2048]{1,0:T(8,128)(2,1)S(1)} fusion(bf16[512,1536]{1,0:T(8,128)(2,1)} %get-tuple-element.63.gu1, bf16[2048,1536]{1,0:T(8,128)(2,1)} %get-tuple-element.62), kind=kOutput, calls=%fused_computation.11 | convolution fusion | flops 3222274048 | bytes 9961472 | tf_op jit(solution)/shard_map/dot_general | solution.py:158
  218.3 4.7 %add_convert_fusion.2.other_ref = bf16[512,2048]{1,0:T(8,128)(2,1)} fusion(bf16[512,2048]{1,0:T(8,128)(2,1)S(1)} %collective-permute-done.4, bf16[512,1536]{1,0:T(8,128)(2,1)S(1)} %copy-done.31, bf16[2048,1536]{1,0:T(8,128)(2,1)S(1)} %copy-done.73), kind=kOutput, calls=%fused_computation.3 | convolution fusion | flops 3224371200 | bytes 12058624 | tf_op jit(solution)/shard_map/dot_general | solution.py:158
  232.6 15.6 %shard_map.384 = bf16[2,8,2304,128]{3,2,1,0:T(8,128)(2,1)} custom-call(s32[1]{0:T(128)} %bitcast.5.core_ref.other_ref, bf16[512,2048]{1,0:T(8,128)(2,1)} %add_convert_fusion.2.other_ref, bf16[512,2048]{1,0:T(8,128)(2,1)} %bitcast.19.a0, bf16[512,2048]{1,0:T(8,128)(2,1)} %collective-permute-done.3.a1, bf16[2,512,2048]{2,1,0:T(8,128)(2,1)} %bitcast.111, ...), custom_call_target="tpu_custom_call" | custom-call | tf_op jit(solution)/shard_map/pallas_call | solution.py:568
  248.2 5.4 %all-to-all-done.5.parts_ref = bf16[4,128,2048]{2,1,0:T(8,128)(2,1)} async-done(((bf16[4,128,2048]{2,1,0:T(8,128)(2,1)}), bf16[4,128,2048]{2,1,0:T(8,128)(2,1)}, u32[]{:S(2)}, u32[]{:S(2)}) %all-to-all-start.5) | async-done | bytes 2097184 | tf_op jit(solution)/shard_map/all_to_all | solution.py:61
  259.7 29.0 %all_to_all.57 = bf16[4,128,2048]{2,1,0:T(8,128)(2,1)S(1)} all-to-all(bf16[4,128,2048]{2,1,0:T(8,128)(2,1)} %copy-done.18), channel_id=1, replica_groups=mesh['x_lo'=2,'z'=4,'core'=2,'y'=4,'x_hi'=2] {'y'}, dimensions={0} | all-to-all | bytes 4194304 | tf_op jit(solution)/shard_map/all_to_all | solution.py:61
  302.2 17.0 %all_to_all.58 = f32[16,32,128]{2,1,0:T(8,128)S(1)} all-to-all(f32[16,32,128]{2,1,0:T(8,128)S(1)} %concatenate.14), channel_id=1, replica_groups=mesh['x_lo'=2,'z'=4,'core'=2,'y'=4,'x_hi'=2] {'x_hi','x_lo','z'}, dimensions={0} | all-to-all | bytes 524288 | tf_op jit(solution)/shard_map/all_to_all | solution.py:688
  326.6 6.9 %shard_map.379 = (f32[1024,64]{1,0:T(8,128)S(1)}, f32[1024,256]{1,0:T(8,128)S(1)}) custom-call(s32[14]{0:T(128)S(1)} %concatenate.12.idx_ref, bf16[1024,320]{1,0:T(8,128)(2,1)S(1)} %copy-done.2, bf16[1024,256]{1,0:T(8,128)(2,1)S(1)} %copy-done.20, f32[1024,2]{1,0:T(8,128)S(1)} %copy-done.22), custom_call_target="tpu_custom_call" | custom-call | tf_op jit(solution)/shard_map/pallas_call | solution.py:838
  338.6 6.7 %shard_map.380.proj_ref = bf16[1024,320]{1,0:T(8,128)(2,1)S(1)} custom-call(s32[14]{0:T(128)S(1)} %concatenate.12.idx_ref, bf16[1024,320]{1,0:T(8,128)(2,1)S(1)} %copy-done.2, bf16[1024,256]{1,0:T(8,128)(2,1)S(1)} %copy-done.20, f32[1024,2]{1,0:T(8,128)S(1)} %copy-done.23, f32[1024,64]{1,0:T(8,128)S(1)} %copy-done.45, f32[1024,256]{1,0:T(8,128)S(1)} %copy-done.39, ...), custom_call_target="tpu_custom_call" | custom-call | tf_op jit(solution)/shard_map/pallas_call | solution.py:845
  354.8 5.3 %convolution_convert_fusion.1 = bf16[512,2048]{1,0:T(8,128)(2,1)} fusion(bf16[512,768]{1,0:T(8,128)(2,1)} %shard_map.382, bf16[2048,768]{1,0:T(8,128)(2,1)} %get-tuple-element.73), kind=kOutput, calls=%fused_computation.8 | convolution fusion | flops 1611661312 | bytes 6029312 | tf_op jit(solution)/shard_map/dot_general | solution.py:158
  372.2 8.7 %shard_map.388 = bf16[2,8,576,128]{3,2,1,0:T(8,128)(2,1)} custom-call(s32[1]{0:T(128)} %bitcast.5.core_ref.other_ref, s32[1]{0:T(128)} %bitcast.5.core_ref.other_ref, bf16[512,2048]{1,0:T(8,128)(2,1)S(1)} %bitcast.93, bf16[512,2048]{1,0:T(8,128)(2,1)} %collective-permute-done.1.a1, bf16[512,2048]{1,0:T(8,128)(2,1)} %bitcast.127, ...), custom_call_target="tpu_custom_call" | custom-call | tf_op jit(solution)/shard_map/pallas_call | solution.py:568
  380.9 6.9 %all-to-all-start.9 = ((bf16[16,576,128]{2,1,0:T(8,128)(2,1)}), bf16[16,576,128]{2,1,0:T(8,128)(2,1)}, u32[]{:S(2)}, u32[]{:S(2)}) async-start(bf16[16,576,128]{2,1,0:T(8,128)(2,1)} %bitcast.123), calls=%async_computation.10 | async-start | bytes 4718592 | tf_op jit(solution)/shard_map/all_to_all | solution.py:688
  408.0 7.6 %collective-permute-start.16 = (bf16[2304,128]{1,0:T(8,128)(2,1)}, bf16[2304,128]{1,0:T(8,128)(2,1)S(1)}, u32[]{:S(2)}, u32[]{:S(2)}) collective-permute-start(bf16[2304,128]{1,0:T(8,128)(2,1)} %shard_map.386), channel_id=1, source_target_pairs={{0,0},{1,8},{8,1},{9,9},{2,2},{3,10},{10,3},{11,11},{4,4},{5,12},{... | collective-permute-start | bytes 1769480 | tf_op jit(solution)/shard_map/ppermute | solution.py:53
  420.0 8.1 %collective-permute-done.12 = bf16[128,2048]{1,0:T(8,128)(2,1)} collective-permute-done((bf16[128,2048]{1,0:T(8,128)(2,1)}, bf16[128,2048]{1,0:T(8,128)(2,1)}, u32[]{:S(2)}, u32[]{:S(2)}) %collective-permute-start.12) | collective-permute-done | bytes 524320 | tf_op jit(solution)/shard_map/ppermute | solution.py:69
  430.1 7.9 %collective-permute-start.14 = (bf16[128,2048]{1,0:T(8,128)(2,1)S(1)}, bf16[128,2048]{1,0:T(8,128)(2,1)S(1)}, u32[]{:S(2)}, u32[]{:S(2)}) collective-permute-start(bf16[128,2048]{1,0:T(8,128)(2,1)S(1)} %add_convert_fusion.5), channel_id=1, source_target_pairs={{0,0},{1,8},{8,1},{9,9},{2,2},{3,10},{10,3},{11,11},{4,4},{5,12},{... | collective-permute-start | bytes 1572872 | tf_op jit(solution)/shard_map/ppermute | solution.py:53
  448.9 5.0 %collective-permute-start.17 = (bf16[576,128]{1,0:T(8,128)(2,1)S(1)}, bf16[576,128]{1,0:T(8,128)(2,1)S(1)}, u32[]{:S(2)}, u32[]{:S(2)}) collective-permute-start(bf16[576,128]{1,0:T(8,128)(2,1)S(1)} %convert_element_type.187), channel_id=1, source_target_pairs={{0,0},{1,8},{8,1},{9,9},{2,2},{3,10},{10,3},{11,11},{4,4},{5,12},{... | collective-permute-start | bytes 442376 | tf_op jit(solution)/shard_map/ppermute | solution.py:53
  (279 shorter events, 181.3 us)
Async XLA Ops:
  7.2 56.4 %all-gather.7.cloned.1.call-start = ((), (), s32[]{:S(2)}) async-start(), calls=%async_computation.13 | async-start | bytes 5406720 | tf_op jit(solution)/shard_map/all_gather | solution.py:722
  12.8 19.7 %collective-permute-start = (bf16[2,128,2048]{2,1,0:T(8,128)(2,1)S(1)}, bf16[2,128,2048]{2,1,0:T(8,128)(2,1)S(1)}, u32[]{:S(2)}, u32[]{:S(2)}) collective-permute-start(bf16[2,128,2048]{2,1,0:T(8,128)(2,1)S(1)} %pad_maximum_fusion), channel_id=1, source_target_pairs={{0,0},{1,8},{8,1},{9,9},{2,2},{3,10},{10,3},{11,11},{4,4},{5,12},{... | collective-permute-start | bytes 3145736 | tf_op jit(solution)/shard_map/ppermute | solution.py:53
  35.1 19.6 %all-to-all-start = ((bf16[4,128,2048]{2,1,0:T(8,128)(2,1)}), bf16[4,128,2048]{2,1,0:T(8,128)(2,1)S(1)}, u32[]{:S(2)}, u32[]{:S(2)}) async-start(bf16[4,128,2048]{2,1,0:T(8,128)(2,1)} %broadcast_in_dim.13), calls=%async_computation | async-start | bytes 4194304 | tf_op jit(solution)/shard_map/all_to_all | solution.py:61
  39.4 146.3 %all-gather.9.cloned.1.call-start = ((), (), s32[]{:S(2)}) async-start(), calls=%async_computation.14 | async-start | bytes 4718592 | tf_op jit(solution)/shard_map/all_gather | solution.py:736
  63.6 126.2 %all-gather.11.cloned.1.call-start = ((), (), s32[]{:S(2)}) async-start(), calls=%async_computation.15 | async-start | bytes 19464192 | tf_op jit(solution)/shard_map/all_gather | solution.py:722
  79.1 11.7 %all-to-all-start.1 = ((f32[16,24,128]{2,1,0:T(8,128)}), f32[16,24,128]{2,1,0:T(8,128)}, u32[]{:S(2)}, u32[]{:S(2)}) async-start(f32[16,24,128]{2,1,0:T(8,128)} %bitcast.96), calls=%async_computation.1 | async-start | bytes 393216 | tf_op jit(solution)/shard_map/all_to_all | solution.py:688
  92.8 13.8 %all-to-all-start.2 = ((f32[16,24,128]{2,1,0:T(8,128)}), f32[16,24,128]{2,1,0:T(8,128)}, u32[]{:S(2)}, u32[]{:S(2)}) async-start(f32[16,24,128]{2,1,0:T(8,128)} %multiply_reduce_fusion.1), calls=%async_computation.2 | async-start | bytes 393216 | tf_op jit(solution)/shard_map/all_to_all | solution.py:688
  182.8 7.0 %collective-permute-start.3 = (bf16[512,2048]{1,0:T(8,128)(2,1)}, bf16[512,2048]{1,0:T(8,128)(2,1)}, u32[]{:S(2)}, u32[]{:S(2)}) collective-permute-start(bf16[512,2048]{1,0:T(8,128)(2,1)} %bitcast.19.a0), channel_id=1, source_target_pairs={{0,8},{8,0},{1,9},{9,1},{2,10},{10,2},{3,11},{11,3},{4,12},{12,4},... | collective-permute-start | bytes 6291464 | tf_op jit(solution)/shard_map/ppermute | solution.py:57
  223.0 30.6 %all-to-all-start.5 = ((bf16[4,128,2048]{2,1,0:T(8,128)(2,1)}), bf16[4,128,2048]{2,1,0:T(8,128)(2,1)}, u32[]{:S(2)}, u32[]{:S(2)}) async-start(bf16[4,128,2048]{2,1,0:T(8,128)(2,1)} %bitcast.128), calls=%async_computation.5 | async-start | bytes 4194304 | tf_op jit(solution)/shard_map/all_to_all | solution.py:61
  227.5 179.3 %reduce-scatter.2.cloned.1.call-start = ((), (), s32[]{:S(2)}) async-start(), calls=%async_computation.12 | async-start | bytes 10027008 | tf_op jit(solution)/shard_map/reduce_scatter | solution.py:812
  320.9 14.3 %all-to-all-start.8 = ((f32[16,24,128]{2,1,0:T(8,128)}), f32[16,24,128]{2,1,0:T(8,128)}, u32[]{:S(2)}, u32[]{:S(2)}) async-start(f32[16,24,128]{2,1,0:T(8,128)} %multiply_reduce_fusion), calls=%async_computation.8 | async-start | bytes 393216 | tf_op jit(solution)/shard_map/all_to_all | solution.py:688
  360.2 37.4 %collective-permute-start.10 = (bf16[512,2048]{1,0:T(8,128)(2,1)}, bf16[512,2048]{1,0:T(8,128)(2,1)}, u32[]{:S(2)}, u32[]{:S(2)}) collective-permute-start(bf16[512,2048]{1,0:T(8,128)(2,1)} %convolution_convert_fusion.1), channel_id=1, source_target_pairs={{0,8},{8,0},{1,9},{9,1},{2,10},{10,2},{3,11},{11,3},{4,12},{12,4},... | collective-permute-start | bytes 6291464 | tf_op jit(solution)/shard_map/ppermute | solution.py:57
  368.6 24.2 %collective-permute-start.7 = (bf16[128,2048]{1,0:T(8,128)(2,1)}, bf16[128,2048]{1,0:T(8,128)(2,1)}, u32[]{:S(2)}, u32[]{:S(2)}) collective-permute-start(bf16[128,2048]{1,0:T(8,128)(2,1)} %get-tuple-element.103), channel_id=1, source_target_pairs={{0,2},{2,4},{4,6},{6,0},{1,3},{3,5},{5,7},{7,1},{8,10},{10,12},{12... | collective-permute-start | bytes 1572872 | tf_op jit(solution)/shard_map/ppermute | solution.py:69
  369.2 23.6 %collective-permute-start.9 = (bf16[128,2048]{1,0:T(8,128)(2,1)}, bf16[128,2048]{1,0:T(8,128)(2,1)}, u32[]{:S(2)}, u32[]{:S(2)}) collective-permute-start(bf16[128,2048]{1,0:T(8,128)(2,1)} %get-tuple-element.104), channel_id=1, source_target_pairs={{0,6},{2,0},{4,2},{6,4},{1,7},{3,1},{5,3},{7,5},{8,14},{10,8},{12,... | collective-permute-start | bytes 1572872 | tf_op jit(solution)/shard_map/ppermute | solution.py:69
  371.3 23.4 %collective-permute-start.8 = (bf16[128,2048]{1,0:T(8,128)(2,1)}, bf16[128,2048]{1,0:T(8,128)(2,1)}, u32[]{:S(2)}, u32[]{:S(2)}) collective-permute-start(bf16[128,2048]{1,0:T(8,128)(2,1)} %get-tuple-element.105), channel_id=1, source_target_pairs={{0,4},{2,6},{4,0},{6,2},{1,5},{3,7},{5,1},{7,3},{8,12},{10,14},{12... | collective-permute-start | bytes 1572872 | tf_op jit(solution)/shard_map/ppermute | solution.py:69
  380.9 59.5 %all-to-all-start.9 = ((bf16[16,576,128]{2,1,0:T(8,128)(2,1)}), bf16[16,576,128]{2,1,0:T(8,128)(2,1)}, u32[]{:S(2)}, u32[]{:S(2)}) async-start(bf16[16,576,128]{2,1,0:T(8,128)(2,1)} %bitcast.123), calls=%async_computation.10 | async-start | bytes 4718592 | tf_op jit(solution)/shard_map/all_to_all | solution.py:688
  404.0 16.0 %collective-permute-start.11 = (bf16[128,2048]{1,0:T(8,128)(2,1)}, bf16[128,2048]{1,0:T(8,128)(2,1)}, u32[]{:S(2)}, u32[]{:S(2)}) collective-permute-start(bf16[128,2048]{1,0:T(8,128)(2,1)} %get-tuple-element.100), channel_id=1, source_target_pairs={{0,2},{2,4},{4,6},{6,0},{1,3},{3,5},{5,7},{7,1},{8,10},{10,12},{12... | collective-permute-start | bytes 1572872 | tf_op jit(solution)/shard_map/ppermute | solution.py:69
  404.6 15.5 %collective-permute-start.13 = (bf16[128,2048]{1,0:T(8,128)(2,1)}, bf16[128,2048]{1,0:T(8,128)(2,1)}, u32[]{:S(2)}, u32[]{:S(2)}) collective-permute-start(bf16[128,2048]{1,0:T(8,128)(2,1)} %get-tuple-element.101), channel_id=1, source_target_pairs={{0,6},{2,0},{4,2},{6,4},{1,7},{3,1},{5,3},{7,5},{8,14},{10,8},{12,... | collective-permute-start | bytes 1572872 | tf_op jit(solution)/shard_map/ppermute | solution.py:69
  406.7 21.4 %collective-permute-start.12 = (bf16[128,2048]{1,0:T(8,128)(2,1)}, bf16[128,2048]{1,0:T(8,128)(2,1)}, u32[]{:S(2)}, u32[]{:S(2)}) collective-permute-start(bf16[128,2048]{1,0:T(8,128)(2,1)} %get-tuple-element.102), channel_id=1, source_target_pairs={{0,4},{2,6},{4,0},{6,2},{1,5},{3,7},{5,1},{7,3},{8,12},{10,14},{12... | collective-permute-start | bytes 1572872 | tf_op jit(solution)/shard_map/ppermute | solution.py:69
  408.0 30.0 %collective-permute-start.16 = (bf16[2304,128]{1,0:T(8,128)(2,1)}, bf16[2304,128]{1,0:T(8,128)(2,1)S(1)}, u32[]{:S(2)}, u32[]{:S(2)}) collective-permute-start(bf16[2304,128]{1,0:T(8,128)(2,1)} %shard_map.386), channel_id=1, source_target_pairs={{0,0},{1,8},{8,1},{9,9},{2,2},{3,10},{10,3},{11,11},{4,4},{5,12},{... | collective-permute-start | bytes 1769480 | tf_op jit(solution)/shard_map/ppermute | solution.py:53
  417.8 29.9 %collective-permute-start.15 = (bf16[128,2048]{1,0:T(8,128)(2,1)}, bf16[128,2048]{1,0:T(8,128)(2,1)S(1)}, u32[]{:S(2)}, u32[]{:S(2)}) collective-permute-start(bf16[128,2048]{1,0:T(8,128)(2,1)} %add_convert_fusion.4), channel_id=1, source_target_pairs={{0,0},{1,8},{8,1},{9,9},{2,2},{3,10},{10,3},{11,11},{4,4},{5,12},{... | collective-permute-start | bytes 1572872 | tf_op jit(solution)/shard_map/ppermute | solution.py:53
  430.1 18.8 %collective-permute-start.14 = (bf16[128,2048]{1,0:T(8,128)(2,1)S(1)}, bf16[128,2048]{1,0:T(8,128)(2,1)S(1)}, u32[]{:S(2)}, u32[]{:S(2)}) collective-permute-start(bf16[128,2048]{1,0:T(8,128)(2,1)S(1)} %add_convert_fusion.5), channel_id=1, source_target_pairs={{0,0},{1,8},{8,1},{9,9},{2,2},{3,10},{10,3},{11,11},{4,4},{5,12},{... | collective-permute-start | bytes 1572872 | tf_op jit(solution)/shard_map/ppermute | solution.py:53
  443.5 11.4 %all-to-all-start.10 = ((f32[16,8,128]{2,1,0:T(8,128)}), f32[16,8,128]{2,1,0:T(8,128)S(1)}, u32[]{:S(2)}, u32[]{:S(2)}) async-start(f32[16,8,128]{2,1,0:T(8,128)} %broadcast_in_dim.16), calls=%async_computation.11 | async-start | bytes 131072 | tf_op jit(solution)/shard_map/all_to_all | solution.py:879
  448.9 8.0 %collective-permute-start.17 = (bf16[576,128]{1,0:T(8,128)(2,1)S(1)}, bf16[576,128]{1,0:T(8,128)(2,1)S(1)}, u32[]{:S(2)}, u32[]{:S(2)}) collective-permute-start(bf16[576,128]{1,0:T(8,128)(2,1)S(1)} %convert_element_type.187), channel_id=1, source_target_pairs={{0,0},{1,8},{8,1},{9,9},{2,2},{3,10},{10,3},{11,11},{4,4},{5,12},{... | collective-permute-start | bytes 442376 | tf_op jit(solution)/shard_map/ppermute | solution.py:53
  (81 other events, 685.5 us)
Sparse Core Ops, SparseCore 0:
  11.6 51.9 all-gather.6
  65.9 31.4 all-gather.8
  100.2 77.6 all-gather.10
  259.8 88.4 reduce-scatter.1
